TPU v7x, 32 devices: a whole 2x2x4 slice. The times are simulated.
32 devices in a mesh: seq: 4 (over y, x), fsdp: 8 (over z, core).
Axes of the slice: x: 2, y: 2, z: 4, core: 2. Of those that a mesh axis runs over, the one named last changes fastest.
Arguments:
- tokens: bfloat16 [2, 8, 2048, 640], P(None, 'fsdp', 'seq'), may hold values from -6 to 6
- document_lengths: int32 [2, 8, 2], P(None, 'fsdp'), may hold values from 0 to 2048, as said below
- cotangent: bfloat16 [2, 8, 2048, 640], P(None, 'fsdp', 'seq'), may hold values from -6 to 6
- attention_gain: bfloat16 [640], P('fsdp'), may hold values from 0.5 to 1.5
- query_projection: bfloat16 [640, 1024], P('fsdp'), may hold values from -0.25 to 0.25
- narrowing_factor: bfloat16 [640, 256], P('fsdp'), may hold values from -0.25 to 0.25
- widening_factor: bfloat16 [256, 1024], P('fsdp'), may hold values from -0.1875 to 0.1875
- key_value_projection: bfloat16 [640, 512], P('fsdp'), may hold values from -0.25 to 0.25
- output_projection: bfloat16 [1024, 640], P('fsdp'), may hold values from -3 to 3
- feedforward_gain: bfloat16 [640], P('fsdp'), may hold values from 0.5 to 1.5
- gate_projection: bfloat16 [640, 2048], P('fsdp'), may hold values from -0.25 to 0.25
- up_projection: bfloat16 [640, 2048], P('fsdp'), may hold values from -0.25 to 0.25
- down_projection: bfloat16 [2048, 640], P('fsdp'), may hold values from -0.125 to 0.125
Outputs:
- output: bfloat16 [2, 8, 2048, 640], P(None, 'fsdp', 'seq')
- input_grad: float32 [2, 8, 2048, 640], P(None, 'fsdp', 'seq')
- attn_gain_grad: float32 [640], P('fsdp')
- query_weight_grad: float32 [640, 1024], P('fsdp')
- lora_down_grad: float32 [640, 256], P('fsdp')
- lora_up_grad: float32 [256, 1024], P('fsdp')
- key_value_weight_grad: float32 [640, 512], P('fsdp')
- out_weight_grad: float32 [1024, 640], P('fsdp')
- ffn_gain_grad: float32 [640], P('fsdp')
- gate_weight_grad: float32 [640, 2048], P('fsdp')
- up_weight_grad: float32 [640, 2048], P('fsdp')
- down_weight_grad: float32 [2048, 640], P('fsdp')
Inputs may be any that keep to these rules, and one draw needn't show every extreme that they name: document_lengths[m, g] lists the lengths of the documents packed one after another from the first token of group g in micro-batch m; unused slots hold 0 and come after the used ones; tokens past the last document are padding. In micro-batches of even index one document covers all but at most 256 tokens of its group, and in at least one group the whole group; in micro-batches of odd index the documents fill the group, none longer than 2048.
All inputs are finite; a program needn't handle non-finite values.
Results may differ from a plain program's by a relative error of at most 0.023.
Values may be sent and summed in bfloat16 or wider, within the bound.
No kernel may reach another device: no remote copies, remote signals or barrier semaphores. Data moves between devices by JAX's collectives and lax.ppermute only.
A program may use at most 128 MiB of HBM per device.

v0:
```python
import math

import jax
import jax.numpy as jnp
from jax import lax
from jax.sharding import PartitionSpec as P

EPSILON = 1e-06
MASKED = -1e30
THETA = 10000.0


def from_behind(block, axis, distance):
    devices = range(lax.axis_size(axis))
    route = [(i - distance, i) for i in devices if i - distance in devices]
    return lax.ppermute(block, axis, route)


def from_behind_2(x, axis, by):
    peers = lax.axis_size(axis)
    return lax.ppermute(x, axis, [(i, (i + by) % peers) for i in range(peers)])


def norm_rows(value_rows, gain):
    return (
        value_rows
        * lax.rsqrt(jnp.mean(value_rows * value_rows, axis=-1, keepdims=True) + EPSILON)
        * gain
    )


def doc_layout(lengths, loop_index):
    ends = jnp.cumsum(lengths, dtype=jnp.int32)
    starts = ends - lengths
    number = jnp.sum(
        (loop_index[:, None] >= ends[None, :]).astype(jnp.int32), axis=1, dtype=jnp.int32
    )
    live = loop_index < ends[-1]
    match = number[:, None] == jnp.arange(lengths.shape[0], dtype=jnp.int32)[None, :]
    begin = jnp.sum(jnp.where(match, starts[None, :], 0), axis=1, dtype=jnp.int32)
    token_position = jnp.where(live, loop_index - begin, 0)
    token_label = jnp.where(live, number, lengths.shape[0] + loop_index)
    return (token_label, token_position)


def rotate(value_rows, token_position):
    half = value_rows.shape[-1] // 2
    freqs = THETA ** (-(jnp.arange(half, dtype=jnp.float32) * 2.0 / value_rows.shape[-1]))
    angles = token_position.astype(jnp.float32)[:, None] * freqs[None, :]
    if value_rows.ndim == 3:
        angles = angles[:, None, :]
    cosine = jnp.cos(angles)
    sine = jnp.sin(angles)
    first = value_rows[..., :half]
    second = value_rows[..., half:]
    return jnp.concatenate(
        [first * cosine - second * sine, second * cosine + first * sine], axis=-1
    )


def allowed(query_label, query_index, key_label, key_index):
    return (query_label[:, None] == key_label[None, :]) & (
        key_index[None, :] <= query_index[:, None]
    )


def local(
    tokens,
    document_lengths,
    cotangent,
    attention_gain,
    query_projection,
    narrowing_factor,
    widening_factor,
    key_value_projection,
    output_projection,
    feedforward_gain,
    gate_projection,
    up_projection,
    down_projection,
):
    batches = tokens.shape[0]
    rows = tokens.shape[2]
    head_dim = key_value_projection.shape[1] // 2
    heads = query_projection.shape[1] // head_dim
    scale = head_dim ** (-0.5)
    span = lax.axis_size("seq")
    place = lax.axis_index("seq")
    width = math.gcd(rows, 512)
    single_float_type = jnp.float32
    bfloat_type = jnp.bfloat16
    query_index = place * rows + jnp.arange(rows, dtype=jnp.int32)

    def fetch():
        return (
            lax.all_gather(attention_gain, "fsdp", axis=0, tiled=True),
            lax.all_gather(query_projection, "fsdp", axis=0, tiled=True),
            lax.all_gather(narrowing_factor, "fsdp", axis=0, tiled=True),
            lax.all_gather(widening_factor, "fsdp", axis=0, tiled=True),
            lax.all_gather(key_value_projection, "fsdp", axis=0, tiled=True),
            lax.all_gather(output_projection, "fsdp", axis=0, tiled=True),
            lax.all_gather(feedforward_gain, "fsdp", axis=0, tiled=True),
            lax.all_gather(gate_projection, "fsdp", axis=0, tiled=True),
            lax.all_gather(up_projection, "fsdp", axis=0, tiled=True),
            lax.all_gather(down_projection, "fsdp", axis=0, tiled=True),
        )

    totals = None
    outputs = []
    input_grads = []
    for batch in range(batches):
        forward_set = fetch()
        (
            gain_one,
            query_matrix,
            adapter_first,
            adapter_second,
            pair_matrix,
            out_matrix,
            gain_two,
            gate_matrix,
            lift_matrix,
            down_matrix,
        ) = forward_set
        gain_one = gain_one.astype(single_float_type)
        gain_two = gain_two.astype(single_float_type)
        x_rows = tokens[batch, 0].astype(single_float_type)
        lengths = document_lengths[batch, 0]
        query_label, query_pos = doc_layout(lengths, query_index)
        normalized_rows = norm_rows(x_rows, gain_one)
        normalized_low = normalized_rows.astype(bfloat_type)
        adapter_low = jnp.dot(
            normalized_low, adapter_first, preferred_element_type=single_float_type
        ).astype(bfloat_type)
        query_lin = jnp.dot(
            normalized_low, query_matrix, preferred_element_type=single_float_type
        ) + jnp.dot(adapter_low, adapter_second, preferred_element_type=single_float_type)
        query_heads = query_lin.reshape(rows, heads, head_dim)
        query_low = rotate(query_heads, query_pos).astype(bfloat_type)
        pair_lin = jnp.dot(normalized_low, pair_matrix, preferred_element_type=single_float_type)
        key_value = jnp.concatenate(
            [rotate(pair_lin[:, :head_dim], query_pos), pair_lin[:, head_dim:]], axis=1
        ).astype(bfloat_type)
        start_state = (
            jnp.full((heads, rows), MASKED, single_float_type),
            jnp.zeros((heads, rows), single_float_type),
            jnp.zeros((heads, rows, head_dim), single_float_type),
        )
        carry = start_state
        piece = lax.all_gather(key_value, "seq", axis=0, tiled=True)
        count = piece.shape[0]
        step = math.gcd(count, 512)
        blocks = piece.reshape(count // step, step, 2 * head_dim)
        offsets = jnp.arange(count // step, dtype=jnp.int32) * step

        def attend_visit(state, item):
            block, offset = item
            key_index = offset + jnp.arange(step, dtype=jnp.int32)
            key_label, unused_pos = doc_layout(lengths, key_index)
            mask = allowed(query_label, query_index, key_label, key_index)
            peak, total, gathered = state
            scores = (
                jnp.einsum(
                    "qhd,kd->hqk",
                    query_low,
                    block[:, :head_dim],
                    preferred_element_type=single_float_type,
                )
                * scale
            )
            scores = jnp.where(mask[None], scores, MASKED)
            new_peak = jnp.maximum(peak, jnp.max(scores, axis=-1))
            factor = jnp.exp(peak - new_peak)
            probs = jnp.where(mask[None], jnp.exp(scores - new_peak[..., None]), 0.0)
            total = total * factor + jnp.sum(probs, axis=-1)
            gathered = gathered * factor[..., None] + jnp.einsum(
                "hqk,kd->hqd",
                probs.astype(bfloat_type),
                block[:, head_dim:],
                preferred_element_type=single_float_type,
            )
            state = (new_peak, total, gathered)
            return (state, None)

        carry, unused = lax.scan(attend_visit, carry, (blocks, offsets))
        peak, total, gathered = carry
        log_total = peak + jnp.log(total)
        attn_heads = jnp.transpose(gathered / total[..., None], (1, 0, 2))
        attn_rows = attn_heads.reshape(rows, heads * head_dim)
        attn_low = attn_rows.astype(bfloat_type)
        middle = x_rows + jnp.dot(attn_low, out_matrix, preferred_element_type=single_float_type)
        ffn_low = norm_rows(middle, gain_two).astype(bfloat_type)
        gate = jnp.dot(ffn_low, gate_matrix, preferred_element_type=single_float_type)
        lift = jnp.dot(ffn_low, lift_matrix, preferred_element_type=single_float_type)
        hidden_low = (jax.nn.gelu(gate, approximate=True) * lift).astype(bfloat_type)
        result = middle + jnp.dot(hidden_low, down_matrix, preferred_element_type=single_float_type)
        outputs.append(result.astype(bfloat_type))
        backward_set = fetch()
        (
            unused_one,
            query_back,
            adapter_first_backward,
            adapter_second_backward,
            pair_back,
            out_back,
            unused_two,
            gate_back,
            lift_back,
            down_back,
        ) = backward_set
        grad_out = cotangent[batch, 0]
        grad_down = jnp.einsum(
            "rf,rd->fd", hidden_low, grad_out, preferred_element_type=single_float_type
        )
        grad_hidden = jnp.einsum(
            "rd,fd->rf", grad_out, down_back, preferred_element_type=single_float_type
        )
        unused_value, geglu_pull = jax.vjp(
            lambda first, second: jax.nn.gelu(first, approximate=True) * second, gate, lift
        )
        grad_gate, grad_lift = geglu_pull(grad_hidden)
        grad_gate_low = grad_gate.astype(bfloat_type)
        grad_lift_low = grad_lift.astype(bfloat_type)
        grad_gate_w = jnp.einsum(
            "rd,rf->df", ffn_low, grad_gate_low, preferred_element_type=single_float_type
        )
        grad_lift_w = jnp.einsum(
            "rd,rf->df", ffn_low, grad_lift_low, preferred_element_type=single_float_type
        )
        grad_normed_ffn = jnp.einsum(
            "rf,df->rd", grad_gate_low, gate_back, preferred_element_type=single_float_type
        ) + jnp.einsum(
            "rf,df->rd", grad_lift_low, lift_back, preferred_element_type=single_float_type
        )
        unused_norm, ffn_norm_pull = jax.vjp(norm_rows, middle, gain_two)
        grad_middle_part, grad_gain_two = ffn_norm_pull(grad_normed_ffn)
        grad_middle = grad_out.astype(single_float_type) + grad_middle_part
        grad_branch_low = grad_middle.astype(bfloat_type)
        grad_out_w = jnp.einsum(
            "rc,rd->cd", attn_low, grad_branch_low, preferred_element_type=single_float_type
        )
        grad_attn_low = jnp.einsum(
            "rd,cd->rc", grad_branch_low, out_back, preferred_element_type=single_float_type
        ).astype(bfloat_type)
        grad_attn_heads = grad_attn_low.reshape(rows, heads, head_dim)
        delta = jnp.sum(
            jnp.transpose(grad_attn_heads.astype(single_float_type) * attn_heads, (1, 0, 2)),
            axis=-1,
        )

        def sweep(turn, state):
            piece, piece_grad, query_grad = state
            owner = (place - turn) % span
            blocks = piece.reshape(rows // width, width, 2 * head_dim)
            offsets = owner * rows + jnp.arange(rows // width, dtype=jnp.int32) * width

            def sweep_visit(query_grad, item):
                block, offset = item
                key_index = offset + jnp.arange(width, dtype=jnp.int32)
                key_label, unused_pos = doc_layout(lengths, key_index)
                mask = allowed(query_label, query_index, key_label, key_index)
                sweep_query_grad = query_grad
                keys = block[:, :head_dim]
                vals = block[:, head_dim:]
                scores = (
                    jnp.einsum(
                        "qhd,kd->hqk", query_low, keys, preferred_element_type=single_float_type
                    )
                    * scale
                )
                scores = jnp.where(mask[None], scores, MASKED)
                probs = jnp.where(mask[None], jnp.exp(scores - log_total[..., None]), 0.0)
                grad_vals = jnp.einsum(
                    "hqk,qhd->kd",
                    probs.astype(bfloat_type),
                    grad_attn_heads,
                    preferred_element_type=single_float_type,
                )
                grad_probs = jnp.einsum(
                    "qhd,kd->hqk", grad_attn_heads, vals, preferred_element_type=single_float_type
                )
                grad_scores = jnp.where(
                    mask[None], probs * (grad_probs - delta[..., None]), 0.0
                ).astype(bfloat_type)
                sweep_query_grad = (
                    sweep_query_grad
                    + jnp.einsum(
                        "hqk,kd->hqd", grad_scores, keys, preferred_element_type=single_float_type
                    )
                    * scale
                )
                grad_keys = (
                    jnp.einsum(
                        "hqk,qhd->kd",
                        grad_scores,
                        query_low,
                        preferred_element_type=single_float_type,
                    )
                    * scale
                )
                return (sweep_query_grad, jnp.concatenate([grad_keys, grad_vals], axis=1))

            query_grad, block_grads = lax.scan(sweep_visit, query_grad, (blocks, offsets))
            piece_grad = piece_grad + block_grads.reshape(rows, 2 * head_dim)
            piece = from_behind(piece, "seq", 1)
            piece_grad = from_behind_2(piece_grad.astype(jnp.bfloat16), "seq", 1).astype(
                piece_grad.dtype
            )
            return (piece, piece_grad, query_grad)

        start_back = (
            key_value,
            jnp.zeros((rows, 2 * head_dim), single_float_type),
            jnp.zeros((heads, rows, head_dim), single_float_type),
        )
        unused_piece, pair_grad, query_grad = lax.fori_loop(0, span, sweep, start_back)
        unused_rot, query_pull = jax.vjp(
            lambda value_rows: rotate(value_rows, query_pos), query_heads
        )
        (grad_query_heads,) = query_pull(jnp.transpose(query_grad, (1, 0, 2)))
        asker_reduced_deriv = grad_query_heads.reshape(rows, heads * head_dim).astype(bfloat_type)
        unused_key, key_pull = jax.vjp(
            lambda value_rows: rotate(value_rows, query_pos), pair_lin[:, :head_dim]
        )
        (grad_key_lin,) = key_pull(pair_grad[:, :head_dim])
        grad_pair_low = jnp.concatenate([grad_key_lin, pair_grad[:, head_dim:]], axis=1).astype(
            bfloat_type
        )
        grad_query_w = jnp.einsum(
            "rd,rc->dc",
            normalized_low,
            asker_reduced_deriv,
            preferred_element_type=single_float_type,
        )
        widening_factor_deriv = jnp.einsum(
            "wa,wy->ay", adapter_low, asker_reduced_deriv, preferred_element_type=single_float_type
        )
        adapter_low_gradient = jnp.einsum(
            "jx,dx->jd",
            asker_reduced_deriv,
            adapter_second_backward,
            preferred_element_type=single_float_type,
        ).astype(bfloat_type)
        adapter_first_gradient = jnp.einsum(
            "ih,iy->hy",
            normalized_low,
            adapter_low_gradient,
            preferred_element_type=single_float_type,
        )
        grad_pair_w = jnp.einsum(
            "rd,rc->dc", normalized_low, grad_pair_low, preferred_element_type=single_float_type
        )
        grad_normed = (
            jnp.einsum(
                "rc,dc->rd",
                asker_reduced_deriv,
                query_back,
                preferred_element_type=single_float_type,
            )
            + jnp.einsum(
                "lq,jq->lj",
                adapter_low_gradient,
                adapter_first_backward,
                preferred_element_type=single_float_type,
            )
            + jnp.einsum(
                "rc,dc->rd", grad_pair_low, pair_back, preferred_element_type=single_float_type
            )
        )
        unused_first, attn_norm_pull = jax.vjp(norm_rows, x_rows, gain_one)
        grad_input_part, grad_gain_one = attn_norm_pull(grad_normed)
        input_grads.append(grad_middle + grad_input_part)
        grads = (
            grad_gain_one,
            grad_query_w,
            adapter_first_gradient,
            widening_factor_deriv,
            grad_pair_w,
            grad_out_w,
            grad_gain_two,
            grad_gate_w,
            grad_lift_w,
            grad_down,
        )
        totals = (
            grads if batch == 0 else tuple((left + right for left, right in zip(totals, grads)))
        )
    shares = (
        lax.psum_scatter(
            totals[0].astype(jnp.bfloat16), "fsdp", scatter_dimension=0, tiled=True
        ).astype(jnp.float32),
        lax.psum_scatter(
            totals[1].astype(jnp.bfloat16), "fsdp", scatter_dimension=0, tiled=True
        ).astype(jnp.float32),
        lax.psum_scatter(
            totals[2].astype(jnp.bfloat16), "fsdp", scatter_dimension=0, tiled=True
        ).astype(jnp.float32),
        lax.psum_scatter(
            totals[3].astype(jnp.bfloat16), "fsdp", scatter_dimension=0, tiled=True
        ).astype(jnp.float32),
        lax.psum_scatter(
            totals[4].astype(jnp.bfloat16), "fsdp", scatter_dimension=0, tiled=True
        ).astype(jnp.float32),
        lax.psum_scatter(
            totals[5].astype(jnp.bfloat16), "fsdp", scatter_dimension=0, tiled=True
        ).astype(jnp.float32),
        lax.psum_scatter(
            totals[6].astype(jnp.bfloat16), "fsdp", scatter_dimension=0, tiled=True
        ).astype(jnp.float32),
        lax.psum_scatter(
            totals[7].astype(jnp.bfloat16), "fsdp", scatter_dimension=0, tiled=True
        ).astype(jnp.float32),
        lax.psum_scatter(
            totals[8].astype(jnp.bfloat16), "fsdp", scatter_dimension=0, tiled=True
        ).astype(jnp.float32),
        lax.psum_scatter(
            totals[9].astype(jnp.bfloat16), "fsdp", scatter_dimension=0, tiled=True
        ).astype(jnp.float32),
    )
    final = (
        lax.psum(shares[0].astype(jnp.bfloat16), "seq").astype(jnp.float32),
        lax.psum(shares[1].astype(jnp.bfloat16), "seq").astype(jnp.float32),
        lax.psum(shares[2].astype(jnp.bfloat16), "seq").astype(jnp.float32),
        lax.psum(shares[3].astype(jnp.bfloat16), "seq").astype(jnp.float32),
        lax.psum(shares[4].astype(jnp.bfloat16), "seq").astype(jnp.float32),
        lax.psum(shares[5].astype(jnp.bfloat16), "seq").astype(jnp.float32),
        lax.psum(shares[6].astype(jnp.bfloat16), "seq").astype(jnp.float32),
        lax.psum(shares[7].astype(jnp.bfloat16), "seq").astype(jnp.float32),
        lax.psum(shares[8].astype(jnp.bfloat16), "seq").astype(jnp.float32),
        lax.psum(shares[9].astype(jnp.bfloat16), "seq").astype(jnp.float32),
    )
    out_rows = jnp.stack(outputs)
    grad_rows = jnp.stack(input_grads)
    return (
        out_rows[:, None],
        grad_rows[:, None],
        final[0],
        final[1],
        final[2],
        final[3],
        final[4],
        final[5],
        final[6],
        final[7],
        final[8],
        final[9],
    )


def solution(mesh):
    in_specs = (
        P(None, "fsdp", "seq", None),
        P(None, "fsdp", None),
        P(None, "fsdp", "seq", None),
        P("fsdp"),
        P("fsdp", None),
        P("fsdp", None),
        P("fsdp", None),
        P("fsdp", None),
        P("fsdp", None),
        P("fsdp"),
        P("fsdp", None),
        P("fsdp", None),
        P("fsdp", None),
    )
    out_specs = (
        P(None, "fsdp", "seq", None),
        P(None, "fsdp", "seq", None),
        P("fsdp"),
        P("fsdp", None),
        P("fsdp", None),
        P("fsdp", None),
        P("fsdp", None),
        P("fsdp", None),
        P("fsdp"),
        P("fsdp", None),
        P("fsdp", None),
        P("fsdp", None),
    )
    return jax.shard_map(local, mesh=mesh, in_specs=in_specs, out_specs=out_specs, check_vma=False)
```

profile of v0, /device:TPU:0, one launch (start us, length us, event | category | flops | bytes accessed | tf_op | source)
XLA Modules:
  0.0 972.9 jit_solution(6410663819087342034)
XLA Ops:
  15.0 18.3 %all-reduce.13 = (bf16[640]{0:T(1024)(128)(2,1)S(1)}, bf16[640]{0:T(1024)(128)(2,1)S(1)}) all-reduce(bf16[640]{0:T(1024)(128)(2,1)S(1)} %dynamic-update-slice, bf16[640]{0:T(1024)(128)(2,1)S(1)} %dynamic-update-slice.1), channel_id=1, replica_groups=mesh['seq'=4,'fsdp'=8] {'fsdp'}, use_global_device_ids=true, to_apply=%add.8 | all-reduce | flops 1280 | bytes 5120
  33.3 15.5 %all_gather.25 = bf16[640,512]{1,0:T(8,128)(2,1)S(1)} all-gather(bf16[80,512]{1,0:T(8,128)(2,1)} %param.28), channel_id=1, replica_groups=mesh['seq'=4,'fsdp'=8] {'fsdp'}, dimensions={0}, use_global_device_ids=true | all-gather | bytes 737280 | tf_op jit(solution)/shard_map/all_gather | solution.py:100
  62.4 14.3 %all_gather.28 = bf16[640,256]{1,0:T(8,128)(2,1)S(1)} all-gather(bf16[80,256]{1,0:T(8,128)(2,1)S(1)} %copy-done.93), channel_id=1, replica_groups=mesh['seq'=4,'fsdp'=8] {'fsdp'}, dimensions={0}, use_global_device_ids=true | all-gather | bytes 368640 | tf_op jit(solution)/shard_map/all_gather | solution.py:98
  82.1 15.8 %all_gather.29 = bf16[256,1024]{1,0:T(8,128)(2,1)} all-gather(bf16[32,1024]{1,0:T(8,128)(2,1)S(1)} %copy-done.88), channel_id=1, replica_groups=mesh['seq'=4,'fsdp'=8] {'fsdp'}, dimensions={0}, use_global_device_ids=true | all-gather | bytes 589824 | tf_op jit(solution)/shard_map/all_gather | solution.py:99
  123.4 63.2 %while.97 = (s32[]{:T(128)}, f32[4,512]{1,0:T(4,128)S(1)}, f32[4,512]{1,0:T(4,128)S(1)}, f32[4,512,256]{2,1,0:T(8,128)}, s32[512]{0:T(512)S(1)}, /*index=5*/s32[...) while((s32[]{:T(128)}, f32[4,512]{1,0:T(4,128)S(1)}, ...), condition=%wide.region_18.19_spmd.clone, body=%wide.region_14.18_spmd.clone.sunk | while | flops 1089748480 | bytes 37376212 | solution.py:185
  190.5 63.5 %while.96 = (s32[]{:T(128)}, f32[4,512]{1,0:T(4,128)S(1)}, f32[4,512]{1,0:T(4,128)S(1)}, f32[4,512,256]{2,1,0:T(8,128)}, s32[512]{0:T(512)S(1)}, /*index=5*/s32[...) while((s32[]{:T(128)}, f32[4,512]{1,0:T(4,128)S(1)}, ...), condition=%wide.region_8.9_spmd.clone, body=%wide.region_4.8_spmd.clone.sunk | while | flops 1089748480 | bytes 37376212 | solution.py:185
  281.9 9.7 multiply_convert_fusion.1
  302.3 6.4 multiply_convert_fusion
  321.0 137.8 %while.99 = (s32[]{:T(128)}, bf16[512,512]{1,0:T(8,128)(2,1)S(1)}, f32[512,512]{0,1:T(8,128)}, f32[4,512,256]{2,1,0:T(8,128)S(1)}, s32[512]{0:T(512)S(1)}, /*ind...) while((s32[]{:T(128)}, bf16[512,512]{1,0:T(8,128)(2,1)S(1)}, ...), condition=%wide.region_30.31_spmd.clone, body=%wide.region_28.30_spmd.clone.sunk | while | flops 2701792768 | bytes 60338696 | solution.py:316
  339.7 7.1 collective-permute-done.3
  348.9 7.1 collective-permute-done.2
  383.8 7.2 collective-permute-done.2
  418.5 6.5 collective-permute-done.2
  473.5 126.9 %while.98 = (s32[]{:T(128)}, bf16[512,512]{1,0:T(8,128)(2,1)S(1)}, f32[512,512]{0,1:T(8,128)}, f32[4,512,256]{2,1,0:T(8,128)S(1)}, s32[512]{0:T(512)S(1)}, /*ind...) while((s32[]{:T(128)}, bf16[512,512]{1,0:T(8,128)(2,1)S(1)}, ...), condition=%wide.region_24.25_spmd.clone, body=%wide.region_22.24_spmd.clone.sunk | while | flops 2701792768 | bytes 60338696 | solution.py:316
  671.2 6.1 reduce-scatter.15.cloned.1.call-done
  677.4 33.5 %reduce-scatter.9.cloned.1.call-done = bf16[80,1024]{1,0:T(8,128)(2,1)} async-done(((bf16[640,1024]{1,0:T(8,128)(2,1)}), bf16[80,1024]{1,0:T(8,128)(2,1)}) %reduce-scatter.9.cloned.1.call-update) | async-done | bytes 163856 | tf_op jit(solution)/shard_map/reduce_scatter | solution.py:392
  710.8 33.8 %reduce-scatter.17.cloned.1.call-done = bf16[128,640]{1,0:T(8,128)(2,1)} async-done(((bf16[1024,640]{1,0:T(8,128)(2,1)}), bf16[128,640]{1,0:T(8,128)(2,1)}) %reduce-scatter.17.cloned.1.call-update) | async-done | bytes 163856 | tf_op jit(solution)/shard_map/reduce_scatter | solution.py:404
  744.7 38.5 %reduce-scatter.19.cloned.1.call-done = bf16[80,2048]{1,0:T(8,128)(2,1)} async-done(((bf16[640,2048]{1,0:T(8,128)(2,1)}), bf16[80,2048]{1,0:T(8,128)(2,1)}) %reduce-scatter.19.cloned.1.call-update) | async-done | bytes 327696 | tf_op jit(solution)/shard_map/reduce_scatter | solution.py:410
  783.1 38.9 %reduce-scatter.21.cloned.1.call-done = bf16[80,2048]{1,0:T(8,128)(2,1)} async-done(((bf16[640,2048]{1,0:T(8,128)(2,1)}), bf16[80,2048]{1,0:T(8,128)(2,1)}) %reduce-scatter.21.cloned.1.call-update) | async-done | bytes 327696 | tf_op jit(solution)/shard_map/reduce_scatter | solution.py:413
  822.1 38.9 %reduce-scatter.23.cloned.1.call-done = bf16[256,640]{1,0:T(8,128)(2,1)} async-done(((bf16[2048,640]{1,0:T(8,128)(2,1)}), bf16[256,640]{1,0:T(8,128)(2,1)}) %reduce-scatter.23.cloned.1.call-update) | async-done | bytes 327696 | tf_op jit(solution)/shard_map/reduce_scatter | solution.py:416
  861.0 15.0 %all-reduce.12 = (bf16[640]{0:T(1024)(128)(2,1)S(1)}, bf16[640]{0:T(1024)(128)(2,1)S(1)}) all-reduce(bf16[640]{0:T(1024)(128)(2,1)S(1)} %add_convert_fusion.12, bf16[640]{0:T(1024)(128)(2,1)S(1)} %add_convert_fusion.11), channel_id=2, replica_groups=mesh['seq'=4,'fsdp'=8] {'fsdp'}, use_global_device_ids=true, to_apply=%region_34.35.clone | all-reduce | flops 1280 | bytes 5120
  882.3 10.9 %reduce-scatter.11.cloned.1.call-done = bf16[80,256]{1,0:T(8,128)(2,1)} async-done(((bf16[640,256]{1,0:T(8,128)(2,1)}), bf16[80,256]{1,0:T(8,128)(2,1)}) %reduce-scatter.11.cloned.1.call-update) | async-done | bytes 40976 | tf_op jit(solution)/shard_map/reduce_scatter | solution.py:395
  893.2 17.9 %all-reduce.14 = (bf16[80]{0:T(256)(128)(2,1)S(1)}, bf16[80,256]{1,0:T(8,128)(2,1)S(1)}, bf16[80]{0:T(256)(128)(2,1)S(1)}) all-reduce(bf16[80]{0:T(256)(128)(2,1)S(1)} %dynamic-slice.5, bf16[80,256]{1,0:T(8,128)(2,1)} %reduce-scatter.11.cloned.1.call-done, bf16[80]{0:T(256)(128)(2,1)S(1)} %dynamic-slice.7), channel_id=1, replica_groups=mesh['seq'=4,'fsdp'=8] {'seq'}, use_global_device_ids=true, to_apply=%region_35.36 | all-reduce | flops 20640 | bytes 82560 | tf_op jit(solution)/shard_map/psum | solution.py:421
  912.8 43.2 %all-reduce.18.cloned.1.call-done = (bf16[80,1024]{1,0:T(8,128)(2,1)}, bf16[32,1024]{1,0:T(8,128)(2,1)}, bf16[80,512]{1,0:T(8,128)(2,1)}, bf16[128,640]{1,0:T(8,...) async-done(((bf16[80,1024]{1,0:T(8,128)(2,1)}, bf16[32,1024]{1,0:T(8,128)(2,1)}, bf16[80,512]{1,0:T(8,128)(2,1)}, ...) | async-done | bytes 1458192 | tf_op jit(solution)/shard_map/psum | solution.py:422
  (727 shorter events, 569.6 us)
Async XLA Ops:
  7.2 90.7 %all-gather.10.cloned.1.call-start = ((), (), s32[]{:S(2)}) async-start(), calls=%async_computation.9 | async-start | bytes 1474560 | tf_op jit(solution)/shard_map/all_gather | solution.py:97
  7.9 111.6 %all-gather.20.cloned.1.call-start = ((), (), s32[]{:S(2)}) async-start(), calls=%async_computation.14 | async-start | bytes 2621440 | tf_op jit(solution)/shard_map/all_gather | solution.py:150
  56.5 130.1 %all-gather.8.cloned.1.call-start = ((), (), s32[]{:S(2)}) async-start(), calls=%async_computation.8 | async-start | bytes 2621440 | tf_op jit(solution)/shard_map/all_gather | solution.py:150
  58.5 204.6 %all-gather.12.cloned.1.call-start = ((), (), s32[]{:S(2)}) async-start(), calls=%async_computation.10 | async-start | bytes 1474560 | tf_op jit(solution)/shard_map/all_gather | solution.py:101
  59.0 211.5 %all-gather.14.cloned.1.call-start = ((), (), s32[]{:S(2)}) async-start(), calls=%async_computation.11 | async-start | bytes 2949120 | tf_op jit(solution)/shard_map/all_gather | solution.py:103
  59.6 216.7 %all-gather.16.cloned.1.call-start = ((), (), s32[]{:S(2)}) async-start(), calls=%async_computation.12 | async-start | bytes 2949120 | tf_op jit(solution)/shard_map/all_gather | solution.py:104
  60.2 221.7 %all-gather.18.cloned.1.call-start = ((), (), s32[]{:S(2)}) async-start(), calls=%async_computation.13 | async-start | bytes 2949120 | tf_op jit(solution)/shard_map/all_gather | solution.py:105
  61.0 610.3 %reduce-scatter.13.cloned.1.call-start = ((), (), s32[]{:S(2)}) async-start(), calls=%async_computation.17 | async-start | bytes 589824 | tf_op jit(solution)/shard_map/reduce_scatter | solution.py:398
  333.0 23.0 %collective-permute-start.2 = (bf16[512,512]{1,0:T(8,128)(2,1)S(1)}, bf16[512,512]{1,0:T(8,128)(2,1)S(1)}, u32[]{:S(2)}, u32[]{:S(2)}) collective-permute-start(bf16[512,512]{1,0:T(8,128)(2,1)S(1)} %copy.202), channel_id=1, source_target_pairs={{0,8},{8,16},{16,24},{1,9},{9,17},{17,25},{2,10},{10,18},{18,26},{... | collective-permute-start | bytes 1572872 | tf_op jit(solution)/shard_map/while/body/eval_jaxpr/ppermute | solution.py:16
  368.7 22.2 %collective-permute-start.2 = (bf16[512,512]{1,0:T(8,128)(2,1)S(1)}, bf16[512,512]{1,0:T(8,128)(2,1)S(1)}, u32[]{:S(2)}, u32[]{:S(2)}) collective-permute-start(bf16[512,512]{1,0:T(8,128)(2,1)S(1)} %copy.202), channel_id=1, source_target_pairs={{0,8},{8,16},{16,24},{1,9},{9,17},{17,25},{2,10},{10,18},{18,26},{... | collective-permute-start | bytes 1572872 | tf_op jit(solution)/shard_map/while/body/eval_jaxpr/ppermute | solution.py:16
  403.7 21.3 %collective-permute-start.2 = (bf16[512,512]{1,0:T(8,128)(2,1)S(1)}, bf16[512,512]{1,0:T(8,128)(2,1)S(1)}, u32[]{:S(2)}, u32[]{:S(2)}) collective-permute-start(bf16[512,512]{1,0:T(8,128)(2,1)S(1)} %copy.202), channel_id=1, source_target_pairs={{0,8},{8,16},{16,24},{1,9},{9,17},{17,25},{2,10},{10,18},{18,26},{... | collective-permute-start | bytes 1572872 | tf_op jit(solution)/shard_map/while/body/eval_jaxpr/ppermute | solution.py:16
  438.4 20.3 %collective-permute-start.2 = (bf16[512,512]{1,0:T(8,128)(2,1)S(1)}, bf16[512,512]{1,0:T(8,128)(2,1)S(1)}, u32[]{:S(2)}, u32[]{:S(2)}) collective-permute-start(bf16[512,512]{1,0:T(8,128)(2,1)S(1)} %copy.202), channel_id=1, source_target_pairs={{0,8},{8,16},{16,24},{1,9},{9,17},{17,25},{2,10},{10,18},{18,26},{... | collective-permute-start | bytes 1572872 | tf_op jit(solution)/shard_map/while/body/eval_jaxpr/ppermute | solution.py:16
  487.4 19.4 %collective-permute-start = (bf16[512,512]{1,0:T(8,128)(2,1)S(1)}, bf16[512,512]{1,0:T(8,128)(2,1)S(1)}, u32[]{:S(2)}, u32[]{:S(2)}) collective-permute-start(bf16[512,512]{1,0:T(8,128)(2,1)S(1)} %copy.214), channel_id=1, source_target_pairs={{0,8},{8,16},{16,24},{1,9},{9,17},{17,25},{2,10},{10,18},{18,26},{... | collective-permute-start | bytes 1572872 | tf_op jit(solution)/shard_map/while/body/eval_jaxpr/ppermute | solution.py:16
  520.4 18.5 %collective-permute-start = (bf16[512,512]{1,0:T(8,128)(2,1)S(1)}, bf16[512,512]{1,0:T(8,128)(2,1)S(1)}, u32[]{:S(2)}, u32[]{:S(2)}) collective-permute-start(bf16[512,512]{1,0:T(8,128)(2,1)S(1)} %copy.214), channel_id=1, source_target_pairs={{0,8},{8,16},{16,24},{1,9},{9,17},{17,25},{2,10},{10,18},{18,26},{... | collective-permute-start | bytes 1572872 | tf_op jit(solution)/shard_map/while/body/eval_jaxpr/ppermute | solution.py:16
  552.5 17.6 %collective-permute-start = (bf16[512,512]{1,0:T(8,128)(2,1)S(1)}, bf16[512,512]{1,0:T(8,128)(2,1)S(1)}, u32[]{:S(2)}, u32[]{:S(2)}) collective-permute-start(bf16[512,512]{1,0:T(8,128)(2,1)S(1)} %copy.214), channel_id=1, source_target_pairs={{0,8},{8,16},{16,24},{1,9},{9,17},{17,25},{2,10},{10,18},{18,26},{... | collective-permute-start | bytes 1572872 | tf_op jit(solution)/shard_map/while/body/eval_jaxpr/ppermute | solution.py:16
  583.7 16.7 %collective-permute-start = (bf16[512,512]{1,0:T(8,128)(2,1)S(1)}, bf16[512,512]{1,0:T(8,128)(2,1)S(1)}, u32[]{:S(2)}, u32[]{:S(2)}) collective-permute-start(bf16[512,512]{1,0:T(8,128)(2,1)S(1)} %copy.214), channel_id=1, source_target_pairs={{0,8},{8,16},{16,24},{1,9},{9,17},{17,25},{2,10},{10,18},{18,26},{... | collective-permute-start | bytes 1572872 | tf_op jit(solution)/shard_map/while/body/eval_jaxpr/ppermute | solution.py:16
  610.3 67.1 %reduce-scatter.15.cloned.1.call-start = ((), (), s32[]{:S(2)}) async-start(), calls=%async_computation.18 | async-start | bytes 737280 | tf_op jit(solution)/shard_map/reduce_scatter | solution.py:401
  615.3 95.6 %reduce-scatter.9.cloned.1.call-start = ((), (), s32[]{:S(2)}) async-start(), calls=%async_computation.15 | async-start | bytes 1474560 | tf_op jit(solution)/shard_map/reduce_scatter | solution.py:392
  619.2 125.5 %reduce-scatter.17.cloned.1.call-start = ((), (), s32[]{:S(2)}) async-start(), calls=%async_computation.19 | async-start | bytes 1474560 | tf_op jit(solution)/shard_map/reduce_scatter | solution.py:404
  623.8 159.4 %reduce-scatter.19.cloned.1.call-start = ((), (), s32[]{:S(2)}) async-start(), calls=%async_computation.20 | async-start | bytes 2949120 | tf_op jit(solution)/shard_map/reduce_scatter | solution.py:410
  630.3 191.8 %reduce-scatter.21.cloned.1.call-start = ((), (), s32[]{:S(2)}) async-start(), calls=%async_computation.21 | async-start | bytes 2949120 | tf_op jit(solution)/shard_map/reduce_scatter | solution.py:413
  636.7 224.2 %reduce-scatter.23.cloned.1.call-start = ((), (), s32[]{:S(2)}) async-start(), calls=%async_computation.22 | async-start | bytes 2949120 | tf_op jit(solution)/shard_map/reduce_scatter | solution.py:416
  644.1 249.2 %reduce-scatter.11.cloned.1.call-start = ((), (), s32[]{:S(2)}) async-start(), calls=%async_computation.16 | async-start | bytes 368640 | tf_op jit(solution)/shard_map/reduce_scatter | solution.py:395
  657.7 298.4 %all-reduce.18.cloned.1.call-start = ((), (), s32[]{:S(2)}) async-start(), calls=%async_computation.23 | async-start | bytes 2916352 | tf_op jit(solution)/shard_map/psum | solution.py:422
  (158 other events, 1953.9 us)
Sparse Core Ops, SparseCore 0:
  9.7 26.4 all-gather.9
  56.6 33.5 all-gather.19
  92.6 35.1 all-gather.7
  129.3 23.4 all-gather.11
  154.3 33.3 all-gather.13
  189.2 32.8 all-gather.15
  223.8 32.8 all-gather.17
  610.4 34.3 reduce-scatter.12
  647.7 29.6 reduce-scatter.14
  679.6 31.2 reduce-scatter.8
  713.2 31.3 reduce-scatter.16
  747.5 35.5 reduce-scatter.18
  785.6 36.4 reduce-scatter.20
  824.3 36.5 reduce-scatter.22
  863.7 29.5 reduce-scatter.10
  897.1 58.9 all-reduce.17
where the time goes:
time: 983 us; the launch traced here: 973 us
  waiting for transfers between devices  323 us (33%)
  matrix products  254 us (26%)
  other arithmetic  129 us (13%)
  blocking collectives  96.8 us (10%)
  local copies, waits for them, and re-layouts  87.6 us (9%)
  starting transfers between devices  64.1 us (7%)
  between operations  17 us (2%)
    psum x1, waiting for transfers between devices, local(): lax.psum(shares[1].astype(jnp.bfloat16), 'seq').astype(jnp.float32)  43.2 us
    ppermute x8, waiting for transfers between devices, from_behind(): return lax.ppermute(block, axis, route)  41.2 us
    ppermute x8, starting transfers between devices, from_behind(): return lax.ppermute(block, axis, route)  39.4 us
    reduce_scatter x1, waiting for transfers between devices, local(): lax.psum_scatter(totals[8].astype(jnp.bfloat16), 'fsdp', scatter_dimensio...  38.9 us
    reduce_scatter x1, waiting for transfers between devices, local(): lax.psum_scatter(totals[9].astype(jnp.bfloat16), 'fsdp', scatter_dimensio...  38.9 us
    reduce_scatter x1, waiting for transfers between devices, local(): lax.psum_scatter(totals[7].astype(jnp.bfloat16), 'fsdp', scatter_dimensio...  38.5 us
    ppermute x8, waiting for transfers between devices, from_behind_2(): return lax.ppermute(x, axis, [(i, (i + by) % peers) for i in range(peers)])  34.6 us
    reduce_scatter x1, waiting for transfers between devices, local(): lax.psum_scatter(totals[5].astype(jnp.bfloat16), 'fsdp', scatter_dimensio...  33.8 us
  transfers between devices with their start and end apart: 32, of which 24 were waited for; matrix products, arithmetic and copies ran while one was open for 32% of the time, Pallas kernels for 0%

commit v1 on v0

v1 whole, which is shorter than its diff:
```python
import functools
import math

import jax
import jax.numpy as jnp
from jax import lax
from jax.experimental import pallas as pl
from jax.experimental.pallas import tpu as pltpu
from jax.sharding import PartitionSpec as P

EPSILON = 1e-06
THETA = 10000.0
F32 = jnp.float32
BF16 = jnp.bfloat16
GELU_C = math.sqrt(2.0 / math.pi)
GELU_A = 0.044715
LOWEST = -1e30
VMEM_LIMIT = 60 * 1024 * 1024


def mm(left, right):
    return lax.dot_general(left, right, (((1,), (0,)), ((), ())), preferred_element_type=F32)


def mm_nt(left, right):
    return lax.dot_general(left, right, (((1,), (1,)), ((), ())), preferred_element_type=F32)


def full(shape):
    return pl.BlockSpec(shape, lambda i: (0,) * len(shape))


def rows_of(tile, cols):
    return pl.BlockSpec((tile, cols), lambda i: (i, 0))


def params(**more):
    return pltpu.CompilerParams(vmem_limit_bytes=VMEM_LIMIT, **more)


def cost(flops, bytes_accessed, transcendentals=0):
    return pl.CostEstimate(
        flops=int(flops), bytes_accessed=int(bytes_accessed), transcendentals=int(transcendentals)
    )


def project_kernel(x_ref, gain_ref, cos_ref, sin_ref, wq_ref, wn_ref, ww_ref, wkv_ref,
                   normed_ref, lora_ref, q_ref, kv_ref, *, head_dim, scale):
    half = head_dim // 2
    x = x_ref[...].astype(F32)
    inv = lax.rsqrt(jnp.mean(x * x, axis=-1, keepdims=True) + EPSILON)
    normed = (x * inv * gain_ref[...]).astype(BF16)
    normed_ref[...] = normed
    cos, sin = cos_ref[...], sin_ref[...]
    pair = mm(normed, wkv_ref[...])
    a, b = pair[:, :half], pair[:, half:head_dim]
    kv_ref[:, :half] = (a * cos - b * sin).astype(BF16)
    kv_ref[:, half:head_dim] = (b * cos + a * sin).astype(BF16)
    kv_ref[:, head_dim:] = pair[:, head_dim:].astype(BF16)
    mid = mm(normed, wn_ref[...]).astype(BF16)
    lora_ref[...] = mid
    query = mm(normed, wq_ref[...]) + mm(mid, ww_ref[...])
    for h in range(query.shape[1] // head_dim):
        c = h * head_dim
        a, b = query[:, c : c + half], query[:, c + half : c + head_dim]
        q_ref[:, c : c + half] = ((a * cos - b * sin) * scale).astype(BF16)
        q_ref[:, c + half : c + head_dim] = ((b * cos + a * sin) * scale).astype(BF16)


def project(x, gain, cos, sin, wq, wn, ww, wkv, head_dim, scale):
    rows, width = x.shape
    tile = math.gcd(rows, 256)
    q_cols, mid, kv_cols = wq.shape[1], wn.shape[1], wkv.shape[1]
    return pl.pallas_call(
        functools.partial(project_kernel, head_dim=head_dim, scale=scale),
        grid=(rows // tile,),
        in_specs=[rows_of(tile, width), full(gain.shape), rows_of(tile, head_dim // 2),
                  rows_of(tile, head_dim // 2), full(wq.shape), full(wn.shape),
                  full(ww.shape), full(wkv.shape)],
        out_specs=[rows_of(tile, width), rows_of(tile, mid), rows_of(tile, q_cols),
                   rows_of(tile, kv_cols)],
        out_shape=[jax.ShapeDtypeStruct((rows, width), BF16),
                   jax.ShapeDtypeStruct((rows, mid), BF16),
                   jax.ShapeDtypeStruct((rows, q_cols), BF16),
                   jax.ShapeDtypeStruct((rows, kv_cols), BF16)],
        compiler_params=params(),
        cost_estimate=cost(2 * rows * (width * (q_cols + mid + kv_cols) + mid * q_cols), 8e6),
        name="project",
    )(x, gain, cos, sin, wq, wn, ww, wkv)


def attend_kernel(info_ref, low_ref, q_ref, kv_ref, o_ref, lse_ref, vt_ref, acc_ref,
                  *, head_dim, tile, block):
    heads = q_ref.shape[1] // head_dim
    base = info_ref[0]
    last = info_ref[1]

    def flip(kb, carry):
        at = pl.ds(pl.multiple_of(kb * block, block), block)
        vt_ref[:, at] = kv_ref[at, head_dim:].T
        return carry

    lax.fori_loop(info_ref[2], last, flip, 0)
    for t in range(q_ref.shape[0] // tile):
        q_rows = slice(t * tile, (t + 1) * tile)
        low = low_ref[:, q_rows]
        high = base + t * tile + lax.broadcasted_iota(jnp.int32, (1, tile), 1)
        acc_ref[...] = jnp.zeros_like(acc_ref)

        def visit(kb, carry):
            at = pl.ds(pl.multiple_of(kb * block, block), block)
            keys = kv_ref[at, :head_dim]
            vt = vt_ref[:, at]
            index = kb * block + lax.broadcasted_iota(jnp.int32, (block, tile), 0)
            mask = (index >= low) & (index <= high)
            out = []
            for h in range(heads):
                peak, total = carry[h]
                s = mm_nt(keys, q_ref[q_rows, h * head_dim : (h + 1) * head_dim])
                s = jnp.where(mask, s, -jnp.inf)
                new_peak = jnp.maximum(peak, jnp.max(s, axis=0, keepdims=True))
                factor = jnp.exp(peak - new_peak)
                p = jnp.exp(s - new_peak)
                total = total * factor + jnp.sum(p, axis=0, keepdims=True)
                acc_ref[h] = acc_ref[h] * factor + mm(vt, p.astype(BF16))
                out.append((new_peak, total))
            return tuple(out)

        start = tuple(
            (jnp.full((1, tile), LOWEST, F32), jnp.zeros((1, tile), F32)) for _ in range(heads)
        )
        stats = lax.fori_loop(info_ref[2 + t], (base + (t + 1) * tile + block - 1) // block,
                              visit, start)
        for h in range(heads):
            peak, total = stats[h]
            o_ref[q_rows, h * head_dim : (h + 1) * head_dim] = (acc_ref[h] / total).T.astype(BF16)
            lse_ref[h : h + 1, q_rows] = peak + jnp.log(total)


def attend(info, low, q, kv, head_dim, tile, block):
    rows, q_cols = q.shape
    heads = q_cols // head_dim
    vmem = pl.BlockSpec(memory_space=pltpu.VMEM)
    return pl.pallas_call(
        functools.partial(attend_kernel, head_dim=head_dim, tile=tile, block=block),
        in_specs=[pl.BlockSpec(memory_space=pltpu.SMEM), vmem, vmem, vmem],
        out_specs=[vmem, vmem],
        out_shape=[jax.ShapeDtypeStruct((rows, q_cols), BF16),
                   jax.ShapeDtypeStruct((heads, rows), F32)],
        scratch_shapes=[pltpu.VMEM((head_dim, kv.shape[0]), BF16),
                        pltpu.VMEM((heads, head_dim, tile), F32)],
        compiler_params=params(),
        cost_estimate=cost(4 * rows * kv.shape[0] * q_cols, 6e6, rows * kv.shape[0] * heads),
        name="attend",
    )(info, low, q, kv)


def middle_kernel(x_ref, attn_ref, g_ref, gain_ref, wo_ref, wg_ref, wu_ref, wd_ref,
                  out_ref, mid_grad_ref, branch_ref, attn_grad_ref, delta_ref, low_ref,
                  hidden_ref, gate_grad_ref, lift_grad_ref, gain_grad_ref,
                  *, head_dim, chunk):
    @pl.when(pl.program_id(0) == 0)
    def _():
        gain_grad_ref[...] = jnp.zeros_like(gain_grad_ref)

    gain = gain_ref[...]
    attn = attn_ref[...]
    middle = x_ref[...].astype(F32) + mm(attn, wo_ref[...])
    inv = lax.rsqrt(jnp.mean(middle * middle, axis=-1, keepdims=True) + EPSILON)
    unit = middle * inv
    low = (unit * gain).astype(BF16)
    low_ref[...] = low
    grad = g_ref[...]
    result = middle
    back = jnp.zeros_like(middle)
    for c in range(wg_ref.shape[1] // chunk):
        at = slice(c * chunk, (c + 1) * chunk)
        gate = mm(low, wg_ref[:, at])
        lift = mm(low, wu_ref[:, at])
        square = gate * gate
        bend = jnp.tanh(GELU_C * gate * (1.0 + GELU_A * square))
        cdf = 0.5 * (1.0 + bend)
        gelu = gate * cdf
        hidden = (gelu * lift).astype(BF16)
        hidden_ref[:, at] = hidden
        result = result + mm(hidden, wd_ref[at, :])
        hidden_grad = mm_nt(grad, wd_ref[at, :])
        slope = cdf + (0.5 * GELU_C) * gate * (1.0 - bend * bend) * (1.0 + 3.0 * GELU_A * square)
        gate_grad = (hidden_grad * lift * slope).astype(BF16)
        lift_grad = (hidden_grad * gelu).astype(BF16)
        gate_grad_ref[:, at] = gate_grad
        lift_grad_ref[:, at] = lift_grad
        back = back + mm_nt(gate_grad, wg_ref[:, at]) + mm_nt(lift_grad, wu_ref[:, at])
    out_ref[...] = result.astype(BF16)
    gain_grad_ref[...] += jnp.sum(unit * back, axis=0, keepdims=True)
    scaled = back * gain
    mid_grad = grad.astype(F32) + inv * (
        scaled - unit * jnp.mean(unit * scaled, axis=-1, keepdims=True)
    )
    mid_grad_ref[...] = mid_grad
    branch = mid_grad.astype(BF16)
    branch_ref[...] = branch
    attn_grad = mm_nt(branch, wo_ref[...]).astype(BF16)
    attn_grad_ref[...] = attn_grad
    product = attn_grad.astype(F32) * attn.astype(F32)
    half = head_dim // 2
    for h in range(attn.shape[1] // head_dim):
        c = h * head_dim
        folded = product[:, c : c + half] + product[:, c + half : c + head_dim]
        delta_ref[h : h + 1, :] = jnp.sum(folded.T, axis=0, keepdims=True)


def middle_part(x, attn, grad, gain, wo, wg, wu, wd, head_dim):
    rows, width = x.shape
    q_cols, hidden = attn.shape[1], wg.shape[1]
    heads = q_cols // head_dim
    tile = math.gcd(rows, 256)
    return pl.pallas_call(
        functools.partial(middle_kernel, head_dim=head_dim, chunk=512),
        grid=(rows // tile,),
        in_specs=[rows_of(tile, width), rows_of(tile, q_cols), rows_of(tile, width),
                  full(gain.shape), full(wo.shape), full(wg.shape), full(wu.shape), full(wd.shape)],
        out_specs=[rows_of(tile, width), rows_of(tile, width), rows_of(tile, width),
                   rows_of(tile, q_cols), pl.BlockSpec((heads, tile), lambda i: (0, i)),
                   rows_of(tile, width), rows_of(tile, hidden), rows_of(tile, hidden),
                   rows_of(tile, hidden), full((1, width))],
        out_shape=[jax.ShapeDtypeStruct((rows, width), BF16),
                   jax.ShapeDtypeStruct((rows, width), F32),
                   jax.ShapeDtypeStruct((rows, width), BF16),
                   jax.ShapeDtypeStruct((rows, q_cols), BF16),
                   jax.ShapeDtypeStruct((heads, rows), F32),
                   jax.ShapeDtypeStruct((rows, width), BF16),
                   jax.ShapeDtypeStruct((rows, hidden), BF16),
                   jax.ShapeDtypeStruct((rows, hidden), BF16),
                   jax.ShapeDtypeStruct((rows, hidden), BF16),
                   jax.ShapeDtypeStruct((1, width), F32)],
        compiler_params=params(),
        cost_estimate=cost(4 * rows * width * (q_cols + 3 * hidden), 40e6, rows * hidden),
        name="middle",
    )(x, attn, grad, gain, wo, wg, wu, wd)


def attend_back_kernel(info_ref, low_ref, lse_ref, delta_ref, q_ref, do_ref, kv_ref, cos_ref,
                       sin_ref, dq_ref, dkv_ref, kt_ref, acc_ref, *, head_dim, tile, block, scale):
    heads = q_ref.shape[1] // head_dim
    half = head_dim // 2
    base = info_ref[0]
    last = info_ref[1]
    tiles = q_ref.shape[0] // tile
    acc_ref[...] = jnp.zeros_like(acc_ref)
    dkv_ref[...] = jnp.zeros_like(dkv_ref)

    def visit(kb, carry):
        at = pl.ds(pl.multiple_of(kb * block, block), block)
        keys = kv_ref[at, :head_dim]
        vals = kv_ref[at, head_dim:]
        kt_ref[...] = keys.T
        dkv_ref[at, :] = jnp.zeros((block, 2 * head_dim), F32)
        for t in range(tiles):
            q_rows = slice(t * tile, (t + 1) * tile)

            @pl.when((kb >= info_ref[2 + t]) & (kb * block < base + (t + 1) * tile))
            def _():
                low = low_ref[:, q_rows]
                high = base + t * tile + lax.broadcasted_iota(jnp.int32, (1, tile), 1)
                index = kb * block + lax.broadcasted_iota(jnp.int32, (block, tile), 0)
                mask = (index >= low) & (index <= high)
                dk = jnp.zeros((block, head_dim), F32)
                dv = jnp.zeros((block, head_dim), F32)
                for h in range(heads):
                    cols = slice(h * head_dim, (h + 1) * head_dim)
                    q = q_ref[q_rows, cols]
                    do = do_ref[q_rows, cols]
                    s = mm_nt(keys, q)
                    p = jnp.where(mask, jnp.exp(s - lse_ref[h : h + 1, q_rows]), 0.0)
                    dv = dv + mm(p.astype(BF16), do)
                    ds = (p * (mm_nt(vals, do) - delta_ref[h : h + 1, q_rows])).astype(BF16)
                    dk = dk + mm(ds, q)
                    acc_ref[h, :, q_rows] += mm(kt_ref[...], ds)
                dkv_ref[at, :head_dim] += dk
                dkv_ref[at, head_dim:] += dv

        return carry

    lax.fori_loop(info_ref[2], last, visit, 0)
    cos, sin = cos_ref[...], sin_ref[...]
    for h in range(heads):
        c = h * head_dim
        dq = acc_ref[h].T * scale
        a, b = dq[:, :half], dq[:, half:]
        dq_ref[:, c : c + half] = (a * cos + b * sin).astype(BF16)
        dq_ref[:, c + half : c + head_dim] = (b * cos - a * sin).astype(BF16)


def attend_back(info, low, lse, delta, q, do, kv, cos, sin, head_dim, tile, block, scale):
    rows, q_cols = q.shape
    heads = q_cols // head_dim
    vmem = pl.BlockSpec(memory_space=pltpu.VMEM)
    return pl.pallas_call(
        functools.partial(attend_back_kernel, head_dim=head_dim, tile=tile, block=block,
                          scale=scale),
        in_specs=[pl.BlockSpec(memory_space=pltpu.SMEM)] + [vmem] * 8,
        out_specs=[vmem, vmem],
        out_shape=[jax.ShapeDtypeStruct((rows, q_cols), BF16),
                   jax.ShapeDtypeStruct(kv.shape, F32)],
        scratch_shapes=[pltpu.VMEM((head_dim, block), BF16),
                        pltpu.VMEM((heads, head_dim, rows), F32)],
        compiler_params=params(),
        cost_estimate=cost(10 * rows * kv.shape[0] * q_cols, 12e6, rows * kv.shape[0] * heads),
        name="attend_back",
    )(info, low, lse, delta, q, do, kv, cos, sin)


def project_back_kernel(x_ref, gain_ref, cos_ref, sin_ref, wq_ref, wn_ref, ww_ref, wkv_ref,
                        dq_ref, dkv_ref, mid_grad_ref,
                        lora_grad_ref, pair_grad_ref, in_grad_ref, gain_grad_ref, *, head_dim):
    @pl.when(pl.program_id(0) == 0)
    def _():
        gain_grad_ref[...] = jnp.zeros_like(gain_grad_ref)

    half = head_dim // 2
    gain = gain_ref[...]
    cos, sin = cos_ref[...], sin_ref[...]
    dq = dq_ref[...]
    lora_grad = mm_nt(dq, ww_ref[...]).astype(BF16)
    lora_grad_ref[...] = lora_grad
    a, b = dkv_ref[:, :half].astype(F32), dkv_ref[:, half:head_dim].astype(F32)
    pair_grad_ref[:, :half] = (a * cos + b * sin).astype(BF16)
    pair_grad_ref[:, half:head_dim] = (b * cos - a * sin).astype(BF16)
    pair_grad_ref[:, head_dim:] = dkv_ref[:, head_dim:].astype(BF16)
    back = (mm_nt(dq, wq_ref[...]) + mm_nt(lora_grad, wn_ref[...])
            + mm_nt(pair_grad_ref[...], wkv_ref[...]))
    x = x_ref[...].astype(F32)
    inv = lax.rsqrt(jnp.mean(x * x, axis=-1, keepdims=True) + EPSILON)
    unit = x * inv
    gain_grad_ref[...] += jnp.sum(unit * back, axis=0, keepdims=True)
    scaled = back * gain
    in_grad_ref[...] = mid_grad_ref[...] + inv * (
        scaled - unit * jnp.mean(unit * scaled, axis=-1, keepdims=True)
    )


def project_back(x, gain, cos, sin, wq, wn, ww, wkv, dq, dkv, mid_grad, head_dim):
    rows, width = x.shape
    tile = math.gcd(rows, 256)
    q_cols, mid, kv_cols = wq.shape[1], wn.shape[1], wkv.shape[1]
    return pl.pallas_call(
        functools.partial(project_back_kernel, head_dim=head_dim),
        grid=(rows // tile,),
        in_specs=[rows_of(tile, width), full(gain.shape), rows_of(tile, head_dim // 2),
                  rows_of(tile, head_dim // 2), full(wq.shape), full(wn.shape),
                  full(ww.shape), full(wkv.shape), rows_of(tile, q_cols),
                  rows_of(tile, kv_cols), rows_of(tile, width)],
        out_specs=[rows_of(tile, mid), rows_of(tile, kv_cols), rows_of(tile, width),
                   full((1, width))],
        out_shape=[jax.ShapeDtypeStruct((rows, mid), BF16),
                   jax.ShapeDtypeStruct((rows, kv_cols), BF16),
                   jax.ShapeDtypeStruct((rows, width), F32),
                   jax.ShapeDtypeStruct((1, width), F32)],
        compiler_params=params(),
        cost_estimate=cost(2 * rows * (width * (q_cols + mid + kv_cols) + mid * q_cols), 12e6),
        name="project_back",
    )(x, gain, cos, sin, wq, wn, ww, wkv, dq, dkv, mid_grad)


def weight_grad_kernel(x_ref, y_ref, out_ref, xt_ref):
    @pl.when(pl.program_id(0) == 0)
    def _():
        xt_ref[...] = x_ref[...].T

    out_ref[...] = mm(xt_ref[...], y_ref[...]).astype(BF16)


def weight_grad(x, y, tile=256):
    rows, width = x.shape
    cols = y.shape[1]
    tile = math.gcd(cols, tile)
    return pl.pallas_call(
        weight_grad_kernel,
        grid=(cols // tile,),
        in_specs=[full(x.shape), pl.BlockSpec((rows, tile), lambda i: (0, i))],
        out_specs=pl.BlockSpec((width, tile), lambda i: (0, i)),
        out_shape=jax.ShapeDtypeStruct((width, cols), BF16),
        scratch_shapes=[pltpu.VMEM((width, rows), BF16)],
        compiler_params=params(),
        cost_estimate=cost(2 * rows * width * cols, 2 * (rows * width + rows * cols + width * cols)),
        name="weight_grad",
    )(x, y)


def layout(lengths, index):
    ends = jnp.cumsum(lengths, dtype=jnp.int32)
    starts = ends - lengths
    number = jnp.sum((index[:, None] >= ends[None, :]).astype(jnp.int32), axis=1, dtype=jnp.int32)
    live = index < ends[-1]
    match = number[:, None] == jnp.arange(lengths.shape[0], dtype=jnp.int32)[None, :]
    begin = jnp.sum(jnp.where(match, starts[None, :], 0), axis=1, dtype=jnp.int32)
    return jnp.where(live, begin, index), jnp.where(live, index - begin, 0)


def local(tokens, document_lengths, cotangent, attention_gain, query_projection, narrowing_factor,
          widening_factor, key_value_projection, output_projection, feedforward_gain,
          gate_projection, up_projection, down_projection):
    batches, _, rows, width = tokens.shape
    head_dim = key_value_projection.shape[1] // 2
    q_cols = query_projection.shape[1]
    scale = head_dim ** (-0.5)
    parts = lax.axis_size("fsdp")
    place = lax.axis_index("seq")
    tile = math.gcd(rows, 256)
    block = math.gcd(rows, 512)

    def gather(x):
        return lax.all_gather(x, "fsdp", axis=0, tiled=True)

    piece = width // parts
    mid = narrowing_factor.shape[1]
    gains = jnp.stack([attention_gain, feedforward_gain], axis=1)
    first = gather(jnp.concatenate(
        [query_projection, key_value_projection, narrowing_factor,
         jnp.pad(gains, ((0, 0), (0, 126)))], axis=1))
    ww = gather(widening_factor)
    gate_up = gather(jnp.concatenate([gate_projection, up_projection], axis=1))
    wo = gather(output_projection)
    wd = gather(down_projection)
    kv_cols = 2 * head_dim
    hidden = gate_projection.shape[1]
    wq = first[:, :q_cols]
    wkv = first[:, q_cols : q_cols + kv_cols]
    wn = first[:, q_cols + kv_cols : q_cols + kv_cols + mid]
    gain_one = first[:, q_cols + kv_cols + mid].astype(F32)[None, :]
    gain_two = first[:, q_cols + kv_cols + mid + 1].astype(F32)[None, :]
    wg, wu = gate_up[:, :hidden], gate_up[:, hidden:]

    index = place * rows + jnp.arange(rows, dtype=jnp.int32)
    lows, positions = [], []
    for m in range(batches):
        low, position = layout(document_lengths[m, 0], index)
        lows.append(low)
        positions.append(position)
    position = jnp.concatenate(positions).astype(F32)
    half = head_dim // 2
    freqs = THETA ** (-(jnp.arange(half, dtype=F32) * 2.0 / head_dim))
    angles = position[:, None] * freqs[None, :]
    cos, sin = jnp.cos(angles), jnp.sin(angles)
    infos = []
    for m in range(batches):
        marks = [place * rows, ((place + 1) * rows + block - 1) // block]
        marks += [lows[m][t * tile] // block for t in range(rows // tile)]
        infos.append(jnp.stack(marks).astype(jnp.int32))

    x = tokens.reshape(batches * rows, width)
    grad = cotangent.reshape(batches * rows, width)
    normed, lora_mid, q, kv = project(x, gain_one, cos, sin, wq, wn, ww, wkv, head_dim, scale)
    kv_all, attended, lses = [], [], []
    for m in range(batches):
        at = slice(m * rows, (m + 1) * rows)
        kv_all.append(lax.all_gather(kv[at], "seq", axis=0, tiled=True))
    for m in range(batches):
        at = slice(m * rows, (m + 1) * rows)
        o, lse = attend(infos[m], lows[m][None, :], q[at], kv_all[m], head_dim, tile, block)
        attended.append(o)
        lses.append(lse)
    attended = jnp.concatenate(attended)
    (output, mid_grad, branch, attn_grad, delta, ffn_low, hidden_low, gate_grad, lift_grad,
     gain_two_grad) = middle_part(x, attended, grad, gain_two, wo, wg, wu, wd, head_dim)
    down_grad = weight_grad(grad, hidden_low)
    gate_w_grad = weight_grad(ffn_low, gate_grad)
    lift_w_grad = weight_grad(ffn_low, lift_grad)
    out_grad = weight_grad(branch, attended)
    dqs, dkvs = [], []
    for m in range(batches):
        at = slice(m * rows, (m + 1) * rows)
        dq, dkv = attend_back(infos[m], lows[m][None, :], lses[m], delta[:, at], q[at],
                              attn_grad[at], kv_all[m], cos[at], sin[at], head_dim, tile, block,
                              scale)
        dqs.append(dq)
        dkvs.append(lax.psum_scatter(dkv.astype(BF16), "seq", scatter_dimension=0, tiled=True))
    dq = jnp.concatenate(dqs)
    dkv = jnp.concatenate(dkvs)
    lora_grad, pair_grad, in_grad, gain_one_grad = project_back(
        x, gain_one, cos, sin, wq, wn, ww, wkv, dq, dkv, mid_grad, head_dim)
    query_grad = weight_grad(normed, dq)
    pair_w_grad = weight_grad(normed, pair_grad)
    narrow_grad = weight_grad(normed, lora_grad)
    widen_grad = weight_grad(lora_mid, dq)

    def scatter(x, dim=0):
        part = lax.psum_scatter(x.astype(BF16), "fsdp", scatter_dimension=dim, tiled=True)
        return part

    gain_pair = jnp.concatenate([gain_one_grad, gain_two_grad], axis=0)
    sums = [
        scatter(jnp.concatenate([query_grad, narrow_grad, pair_w_grad, gate_w_grad, lift_w_grad,
                                 jnp.pad(gain_pair.T.astype(BF16), ((0, 0), (0, 126)))], axis=1)),
        scatter(widen_grad),
        scatter(jnp.concatenate([down_grad.reshape(width, parts, -1),
                                 out_grad.reshape(width, parts, -1)], axis=2)
                .reshape(width, -1).T),
    ]
    sums = lax.psum(tuple(sums), "seq")
    wide, widen, turned = sums
    wide = wide.astype(F32)
    turned = turned.astype(F32)
    cuts = [0]
    for n in (q_cols, mid, kv_cols, hidden, hidden):
        cuts.append(cuts[-1] + n)
    pieces = [wide[:, cuts[i] : cuts[i + 1]] for i in range(5)]
    shard = hidden // parts
    return (
        output.reshape(batches, 1, rows, width),
        in_grad.reshape(batches, 1, rows, width),
        wide[:, cuts[5]],
        pieces[0],
        pieces[1],
        widen.astype(F32),
        pieces[2],
        turned[shard:],
        wide[:, cuts[5] + 1],
        pieces[3],
        pieces[4],
        turned[:shard],
    )


def solution(mesh):
    rows = P(None, "fsdp", "seq", None)
    vector, matrix = P("fsdp"), P("fsdp", None)
    in_specs = (rows, P(None, "fsdp", None), rows, vector) + (matrix,) * 5 + (vector,) + (matrix,) * 3
    out_specs = (rows, rows, vector) + (matrix,) * 5 + (vector,) + (matrix,) * 3
    return jax.shard_map(local, mesh=mesh, in_specs=in_specs, out_specs=out_specs, check_vma=False)
```

time: 983 us -> 647 us (0.66)
  matrix products: 254 us -> 0 us
  Pallas kernels: 0 us -> 138 us
  other arithmetic: 129 us -> 29.7 us
  blocking collectives: 96.8 us -> 19.6 us
  starting transfers between devices: 64.1 us -> 0.74 us
  waiting for transfers between devices: 323 us -> 367 us
  local copies, waits for them, and re-layouts: 87.6 us -> 58.4 us
    dot_general x104 -> x0, matrix products: 254 us -> none  [the longest x8 33 us: attend_visit(): jnp.einsum('qhd,kd->hqk', query_low, block[:, :head_dim], preferred_eleme...]
    all_gather x7 -> x6, waiting for transfers between devices: 0.03 us -> 156 us  [the longest x4 113 us: gather(): return lax.all_gather(x, 'fsdp', axis=0, tiled=True)]
    pallas_call x0 -> x15, Pallas kernels: none -> 138 us  [the longest x8 49 us: weight_grad(): pl.pallas_call(weight_grad_kernel, grid=(cols // tile,), in_specs=[full(x...]
    ppermute x16 -> x0, waiting for transfers between devices: 75.7 us -> none  [the longest x8 41.2 us: from_behind(): return lax.ppermute(block, axis, route)]
    ppermute x16 -> x0, starting transfers between devices: 62.6 us -> none  [the longest x8 39.4 us: from_behind(): return lax.ppermute(block, axis, route)]
    reduce_scatter x8 -> x5, waiting for transfers between devices: 201 us -> 147 us  [the longest x3 137 us: scatter(): lax.psum_scatter(x.astype(BF16), 'fsdp', scatter_dimension=dim, tiled=True)]
    reduce_sum x30 -> x2, other arithmetic: 35.2 us -> 0.18 us  [the longest x1 0.09 us: layout(): jnp.sum(jnp.where(match, starts[None, :], 0), axis=1, dtype=jnp.int32)]
    unnamed x2 -> x0, blocking collectives: 33.3 us -> none
  transfers between devices with their start and end apart: 32 -> 12, of which waited for: 24 -> 11; matrix products, arithmetic and copies ran while one was open for 32% -> 9% of each run, Pallas kernels for 0% -> 13%
where the time goes in v1:
time: 647 us; the launch traced here: 638 us
  waiting for transfers between devices  367 us (57%)
  Pallas kernels  138 us (21%)
  local copies, waits for them, and re-layouts  58.4 us (9%)
  other arithmetic  29.7 us (5%)
  between operations  25.3 us (4%)
  blocking collectives  19.6 us (3%)
    reduce_scatter x3, waiting for transfers between devices, scatter(): lax.psum_scatter(x.astype(BF16), 'fsdp', scatter_dimension=dim, tiled=True)  137 us
    all_gather x4, waiting for transfers between devices, gather(): return lax.all_gather(x, 'fsdp', axis=0, tiled=True)  113 us
    psum x1, waiting for transfers between devices, local(): sums = lax.psum(tuple(sums), 'seq')  62.3 us
    pallas_call x8, Pallas kernels, weight_grad(): pl.pallas_call(weight_grad_kernel, grid=(cols // tile,), in_specs=[full(x...  49 us
    all_gather x2, waiting for transfers between devices, local(): kv_all.append(lax.all_gather(kv[at], 'seq', axis=0, tiled=True))  42.3 us
    pallas_call x1, Pallas kernels, middle_part(): pl.pallas_call(functools.partial(middle_kernel, head_dim=head_dim, chunk=...  37.8 us
    all_gather x1, blocking collectives, gather(): return lax.all_gather(x, 'fsdp', axis=0, tiled=True)  19.6 us
    unnamed x39, local copies, waits for them, and re-layouts  18.9 us
  transfers between devices with their start and end apart: 12, of which 11 were waited for; matrix products, arithmetic and copies ran while one was open for 9% of the time, Pallas kernels for 13%

profile of v1, /device:TPU:0, one launch (start us, length us, event | category | flops | bytes accessed | tf_op | source)
XLA Modules:
  0.0 638.1 jit_solution(276602734862832905)
XLA Ops:
  14.2 19.6 %all_gather.22.ww_ref = bf16[256,1024]{1,0:T(8,128)(2,1)} all-gather(bf16[32,1024]{1,0:T(8,128)(2,1)} %param.19), channel_id=1, replica_groups=mesh['seq'=4,'fsdp'=8] {'fsdp'}, dimensions={0}, use_global_device_ids=true | all-gather | bytes 589824 | tf_op jit(solution)/shard_map/all_gather | solution.py:414
  36.8 10.6 %all-gather.7.cloned.1.call-done = bf16[640,1920]{1,0:T(8,128)(2,1)} async-done(((bf16[80,1920]{1,0:T(8,128)(2,1)}), bf16[640,1920]{1,0:T(8,128)(2,1)}) %all-gather.7.cloned.1.call-update) | async-done | bytes 2457616 | tf_op jit(solution)/shard_map/all_gather | solution.py:414
  55.4 9.8 %project.1 = (bf16[1024,640]{1,0:T(8,128)(2,1)}, bf16[1024,256]{1,0:T(8,128)(2,1)}, bf16[1024,1024]{1,0:T(8,128)(2,1)}, bf16[1024,512]{1,0:T(8,128)(2,1)}) custom-call(bf16[1024,640]{1,0:T(8,128)(2,1)} %bitcast.48, f32[1,640]{1,0:T(1,128)} %reshape.169.gain_ref, f32[1024,128]{1,0:T(8,128)} %get-tuple-element.138.cos_ref, ...), custom_call_target="tpu_custom_call" | custom-call | flops 2885681152 | bytes 8000000 | tf_op jit(solution)/shard_map/project/pallas_call | solution.py:74
  90.3 13.0 %all-gather.9.cloned.1.call-done.kv_ref = bf16[2048,512]{1,0:T(8,128)(2,1)} async-done(((bf16[512,512]{1,0:T(8,128)(2,1)}), bf16[2048,512]{1,0:T(8,128)(2,1)}) %all-gather.9.cloned.1.call-update) | async-done | bytes 2097168 | tf_op jit(solution)/shard_map/all_gather | solution.py:458
  103.3 6.7 %attend.2 = (bf16[512,1024]{1,0:T(8,128)(2,1)}, f32[4,512]{1,0:T(4,128)}) custom-call(s32[4]{0:T(128)} %pad_add_fusion.info_ref, s32[1,512]{1,0:T(1,128)} %compare_select_fusion.1.low_ref, bf16[512,1024]{1,0:T(8,128)(2,1)} %get-tuple-element.126.q_ref, bf16[2048,512]{1,0:T(8,128)(2,1)} %all-gather.9.cloned.1.call-done.kv_ref), custom_call_target="tpu_custom_call" | custom-call | flops 4294967296 | bytes 6000000 | tf_op jit(solution)/shard_map/attend/pallas_call | solution.py:144
  111.3 29.2 %all-gather.11.cloned.1.call-done.kv_ref = bf16[2048,512]{1,0:T(8,128)(2,1)} async-done(((bf16[512,512]{1,0:T(8,128)(2,1)}), bf16[2048,512]{1,0:T(8,128)(2,1)}) %all-gather.11.cloned.1.call-update) | async-done | bytes 2097168 | tf_op jit(solution)/shard_map/all_gather | solution.py:458
  140.5 6.8 %attend.3 = (bf16[512,1024]{1,0:T(8,128)(2,1)}, f32[4,512]{1,0:T(4,128)}) custom-call(s32[4]{0:T(128)} %pad_add_fusion.2.info_ref, s32[1,512]{1,0:T(1,128)} %compare_select_fusion.low_ref, bf16[512,1024]{1,0:T(8,128)(2,1)} %get-tuple-element.125.q_ref, bf16[2048,512]{1,0:T(8,128)(2,1)} %all-gather.11.cloned.1.call-done.kv_ref), custom_call_target="tpu_custom_call" | custom-call | flops 4294967296 | bytes 6000000 | tf_op jit(solution)/shard_map/attend/pallas_call | solution.py:144
  148.7 50.0 %all-gather.15.cloned.1.call-done = bf16[640,4096]{1,0:T(8,128)(2,1)} async-done(((bf16[80,4096]{1,0:T(8,128)(2,1)}), bf16[640,4096]{1,0:T(8,128)(2,1)}) %all-gather.15.cloned.1.call-update) | async-done | bytes 5242896 | tf_op jit(solution)/shard_map/all_gather | solution.py:414
  198.7 5.8 fusion.6
  204.5 17.9 %all-gather.13.cloned.1.call-done.wo_ref = bf16[1024,640]{1,0:T(8,128)(2,1)} async-done(((bf16[128,640]{1,0:T(8,128)(2,1)}), bf16[1024,640]{1,0:T(8,128)(2,1)}) %all-gather.13.cloned.1.call-update) | async-done | bytes 1310736 | tf_op jit(solution)/shard_map/all_gather | solution.py:414
  222.4 34.9 %all-gather.17.cloned.1.call-done.wd_ref = bf16[2048,640]{1,0:T(8,128)(2,1)} async-done(((bf16[256,640]{1,0:T(8,128)(2,1)}), bf16[2048,640]{1,0:T(8,128)(2,1)}) %all-gather.17.cloned.1.call-update) | async-done | bytes 2621456 | tf_op jit(solution)/shard_map/all_gather | solution.py:414
  257.3 37.8 %middle.1 = (bf16[1024,640]{1,0:T(8,128)(2,1)}, f32[1024,640]{1,0:T(8,128)}, bf16[1024,640]{1,0:T(8,128)(2,1)}, bf16[1024,1024]{1,0:T(8,128)(2,1)}, f32[4,1024]{...) custom-call(bf16[1024,640]{1,0:T(8,128)(2,1)} %bitcast.49, ...), custom_call_target="tpu_custom_call" | custom-call | flops 18790481920 | bytes 40000000 | tf_op jit(solution)/shard_map/middle/pallas_call | solution.py:218
  298.8 8.9 %attend_back.3 = (bf16[512,1024]{1,0:T(8,128)(2,1)}, f32[2048,512]{1,0:T(8,128)}) custom-call(s32[4]{0:T(128)} %pad_add_fusion.2.info_ref, s32[1,512]{1,0:T(1,128)} %compare_select_fusion.low_ref, f32[4,512]{1,0:T(4,128)} %get-tuple-element.47.lse_ref, f32[4,512]{1,0:T(4,128)} %get-tuple-element.135.delta_ref, bf16[512,1024]{1,0:T(8,128)(2,1)} %get-tuple-element.125.q_ref, ...), custom_call_target="tpu_custom_call" | custom-call | flops 10737418240 | bytes 12000000 | tf_op jit(solution)/shard_map/attend_back/pallas_call | solution.py:299
  311.7 8.7 %attend_back.2 = (bf16[512,1024]{1,0:T(8,128)(2,1)}, f32[2048,512]{1,0:T(8,128)}) custom-call(s32[4]{0:T(128)} %pad_add_fusion.info_ref, s32[1,512]{1,0:T(1,128)} %compare_select_fusion.1.low_ref, f32[4,512]{1,0:T(4,128)} %get-tuple-element.43.lse_ref, f32[4,512]{1,0:T(4,128)} %get-tuple-element.136.delta_ref, bf16[512,1024]{1,0:T(8,128)(2,1)} %get-tuple-element.126.q_ref, ...), custom_call_target="tpu_custom_call" | custom-call | flops 10737418240 | bytes 12000000 | tf_op jit(solution)/shard_map/attend_back/pallas_call | solution.py:299
  331.7 5.5 weight_grad.15
  338.9 8.9 %weight_grad.14 = bf16[640,2048]{1,0:T(8,128)(2,1)} custom-call(bf16[1024,640]{1,0:T(8,128)(2,1)} %bitcast.59, bf16[1024,2048]{1,0:T(8,128)(2,1)} %get-tuple-element.62.y_ref), custom_call_target="tpu_custom_call" | custom-call | flops 2684354560 | bytes 8126464 | tf_op jit(solution)/shard_map/weight_grad/pallas_call | solution.py:378
  352.7 6.4 %copy.46 = bf16[640,8,384]{0,2,1:T(8,128)(2,1)} copy(bf16[640,8,384]{2,1,0:T(8,128)(2,1)} %pad_maximum_fusion) | data formatting | bytes 7864320 | tf_op jit(solution)/shard_map/concatenate | solution.py:497
  367.9 9.1 %weight_grad.11 = bf16[640,2048]{1,0:T(8,128)(2,1)} custom-call(bf16[1024,640]{1,0:T(8,128)(2,1)} %get-tuple-element.56.x_ref, bf16[1024,2048]{1,0:T(8,128)(2,1)} %get-tuple-element.57.y_ref), custom_call_target="tpu_custom_call" | custom-call | flops 2684354560 | bytes 8126464 | tf_op jit(solution)/shard_map/weight_grad/pallas_call | solution.py:378
  377.0 9.0 %weight_grad.12 = bf16[640,2048]{1,0:T(8,128)(2,1)} custom-call(bf16[1024,640]{1,0:T(8,128)(2,1)} %get-tuple-element.56.x_ref, bf16[1024,2048]{1,0:T(8,128)(2,1)} %get-tuple-element.58.y_ref), custom_call_target="tpu_custom_call" | custom-call | flops 2684354560 | bytes 8126464 | tf_op jit(solution)/shard_map/weight_grad/pallas_call | solution.py:378
  386.0 9.5 %reduce-scatter.6.cloned.1.call-done = bf16[512,512]{1,0:T(8,128)(2,1)} async-done(((bf16[2048,512]{1,0:T(8,128)(2,1)}), bf16[512,512]{1,0:T(8,128)(2,1)}) %reduce-scatter.6.cloned.1.call-update) | async-done | bytes 524304 | tf_op jit(solution)/shard_map/reduce_scatter | solution.py:478
  397.7 9.9 %project_back.1 = (bf16[1024,256]{1,0:T(8,128)(2,1)}, bf16[1024,512]{1,0:T(8,128)(2,1)}, f32[1024,640]{1,0:T(8,128)}, f32[1,640]{1,0:T(1,128)}) custom-call(bf16[1024,640]{1,0:T(8,128)(2,1)} %bitcast.50, f32[1,640]{1,0:T(1,128)} %reshape.169.gain_ref, f32[1024,128]{1,0:T(8,128)} %get-tuple-element.138.cos_ref, f32[1024,128]{1,0:T(8,128)} %get-tuple-element.137.sin_ref, ...), custom_call_target="tpu_custom_call" | custom-call | flops 2885681152 | bytes 12000000 | tf_op jit(solution)/shard_map/project_back/pallas_call | solution.py:347
  428.6 48.1 %reduce-scatter.14.cloned.1.call-done = bf16[384,640]{1,0:T(8,128)(2,1)} async-done(((bf16[3072,640]{1,0:T(8,128)(2,1)}), bf16[384,640]{1,0:T(8,128)(2,1)}) %reduce-scatter.14.cloned.1.call-update) | async-done | bytes 491536 | tf_op jit(solution)/shard_map/reduce_scatter | solution.py:489
  476.7 84.0 %reduce-scatter.10.cloned.1.call-done = bf16[80,6016]{1,0:T(8,128)(2,1)} async-done(((bf16[640,6016]{1,0:T(8,128)(2,1)}), bf16[80,6016]{1,0:T(8,128)(2,1)}) %reduce-scatter.10.cloned.1.call-update) | async-done | bytes 962576 | tf_op jit(solution)/shard_map/reduce_scatter | solution.py:489
  560.7 62.3 %all-reduce.5.cloned.1.call-done = (bf16[384,640]{1,0:T(8,128)(2,1)}, bf16[80,6016]{1,0:T(8,128)(2,1)}, bf16[32,1024]{1,0:T(8,128)(2,1)}) async-done(((bf16[384,640]{1,0:T(8,128)(2,1)}, bf16[80,6016]{1,0:T(8,128)(2,1)}, bf16[32,1024]{1,0:T(8,128)(2,1)}), (bf16[384,640]{1,0:T(8,128)(2,1)}, bf16[80,6016]{1,0:T(8,128)(2,1)}, bf16[32,1024]{1,0:T(8,128)(2,1)})) %all-reduce.5.cloned.1.call-update) | async-done | bytes 1519632 | tf_op jit(solution)/shard_map/psum | solution.py:501
  (125 shorter events, 100.4 us)
Async XLA Ops:
  7.2 40.2 %all-gather.7.cloned.1.call-start = ((), (), s32[]{:S(2)}) async-start(), calls=%async_computation.5 | async-start | bytes 2764800 | tf_op jit(solution)/shard_map/all_gather | solution.py:414
  9.8 93.6 %all-gather.9.cloned.1.call-start = ((), (), s32[]{:S(2)}) async-start(), calls=%async_computation.6 | async-start | bytes 2621440 | tf_op jit(solution)/shard_map/all_gather | solution.py:458
  65.2 3.1 copy-start.11
  65.2 21.4 %copy-start.2 = (f32[1024,128]{1,0:T(8,128)S(1)}, f32[1024,128]{1,0:T(8,128)}, u32[]{:S(2)}) copy-start(f32[1024,128]{1,0:T(8,128)} %get-tuple-element.137.sin_ref) | copy-start | bytes 1572868
  67.5 19.9 %copy-start.3 = (f32[1024,128]{1,0:T(8,128)S(1)}, f32[1024,128]{1,0:T(8,128)}, u32[]{:S(2)}) copy-start(f32[1024,128]{1,0:T(8,128)} %get-tuple-element.138.cos_ref) | copy-start | bytes 1572868
  67.5 73.0 %all-gather.11.cloned.1.call-start = ((), (), s32[]{:S(2)}) async-start(), calls=%async_computation.7 | async-start | bytes 2621440 | tf_op jit(solution)/shard_map/all_gather | solution.py:458
  67.6 21.2 %copy-start.6 = (bf16[1024,1024]{1,0:T(8,128)(2,1)S(1)}, bf16[1024,1024]{1,0:T(8,128)(2,1)}, u32[]{:S(2)}) copy-start(bf16[1024,1024]{1,0:T(8,128)(2,1)} %get-tuple-element.38) | copy-start | bytes 6291460
  68.3 130.4 %all-gather.15.cloned.1.call-start = ((), (), s32[]{:S(2)}) async-start(), calls=%async_computation.9 | async-start | bytes 5898240 | tf_op jit(solution)/shard_map/all_gather | solution.py:414
  70.2 152.2 %all-gather.13.cloned.1.call-start = ((), (), s32[]{:S(2)}) async-start(), calls=%async_computation.8 | async-start | bytes 1474560 | tf_op jit(solution)/shard_map/all_gather | solution.py:414
  70.8 186.5 %all-gather.17.cloned.1.call-start = ((), (), s32[]{:S(2)}) async-start(), calls=%async_computation.10 | async-start | bytes 2949120 | tf_op jit(solution)/shard_map/all_gather | solution.py:414
  71.4 314.6 %reduce-scatter.8.cloned.1.call-start = ((), (), s32[]{:S(2)}) async-start(), calls=%async_computation.12 | async-start | bytes 2621440 | tf_op jit(solution)/shard_map/reduce_scatter | solution.py:478
  148.7 55.8 %copy-start.10 = (bf16[1024,1024]{1,0:T(8,128)(2,1)}, bf16[1024,1024]{1,0:T(8,128)(2,1)S(1)}, u32[]{:S(2)}) copy-start(bf16[1024,1024]{1,0:T(8,128)(2,1)S(1)} %constant_dynamic-update-slice_fusion.attn_ref.y_ref) | copy-start | bytes 6291460
  295.1 3.1 copy-start.13
  311.6 83.8 %reduce-scatter.6.cloned.1.call-start = ((), (), s32[]{:S(2)}) async-start(), calls=%async_computation.11 | async-start | bytes 2621440 | tf_op jit(solution)/shard_map/reduce_scatter | solution.py:478
  324.2 1.5 copy-start.9
  324.2 104.4 %reduce-scatter.12.cloned.1.call-start = ((), (), s32[]{:S(2)}) async-start(), calls=%async_computation.14 | async-start | bytes 589824 | tf_op jit(solution)/shard_map/reduce_scatter | solution.py:489
  331.6 145.1 %reduce-scatter.14.cloned.1.call-start = ((), (), s32[]{:S(2)}) async-start(), calls=%async_computation.15 | async-start | bytes 4423680 | tf_op jit(solution)/shard_map/reduce_scatter | solution.py:489
  359.2 201.5 %reduce-scatter.10.cloned.1.call-start = ((), (), s32[]{:S(2)}) async-start(), calls=%async_computation.13 | async-start | bytes 8663040 | tf_op jit(solution)/shard_map/reduce_scatter | solution.py:489
  411.2 3.8 copy-start.8
  411.2 6.6 %copy-start.5 = (bf16[640,2048]{1,0:T(8,128)(2,1)S(1)}, bf16[640,2048]{1,0:T(8,128)(2,1)}, u32[]{:S(2)}) copy-start(bf16[640,2048]{1,0:T(8,128)(2,1)} %weight_grad.11) | copy-start | bytes 7864324
  417.8 2.7 copy-start.4
  423.2 199.9 %all-reduce.5.cloned.1.call-start = ((), (), s32[]{:S(2)}) async-start(), calls=%async_computation.16 | async-start | bytes 3039232 | tf_op jit(solution)/shard_map/psum | solution.py:501
  623.0 3.4 copy-start.7
  624.5 5.6 copy-start.12
  (3 other events, 3.5 us)
Sparse Core Ops, SparseCore 0:
  10.2 37.0 all-gather.6
  67.7 35.6 all-gather.8
  105.2 35.2 all-gather.10
  142.6 56.0 all-gather.14
  200.2 22.2 all-gather.12
  223.9 33.3 all-gather.16
  311.7 45.1 reduce-scatter.7
  360.2 35.2 reduce-scatter.5
  397.7 30.8 reduce-scatter.11
  430.9 45.7 reduce-scatter.13
  479.1 81.5 reduce-scatter.9
  564.0 58.9 all-reduce.4

commit v2 on v1

v2 whole, which is shorter than its diff:
```python
import functools
import math

import jax
import jax.numpy as jnp
from jax import lax
from jax.experimental import pallas as pl
from jax.experimental.pallas import tpu as pltpu
from jax.sharding import PartitionSpec as P

EPSILON = 1e-06
THETA = 10000.0
F32 = jnp.float32
BF16 = jnp.bfloat16
GELU_C = math.sqrt(2.0 / math.pi)
GELU_A = 0.044715
LOWEST = -1e30
VMEM_LIMIT = 60 * 1024 * 1024
ANY = pl.BlockSpec(memory_space=pl.ANY)
VMEM = pl.BlockSpec(memory_space=pltpu.VMEM)
SMEM = pl.BlockSpec(memory_space=pltpu.SMEM)


def mm(left, right):
    return lax.dot_general(left, right, (((1,), (0,)), ((), ())), preferred_element_type=F32)


def mm_nt(left, right):
    return lax.dot_general(left, right, (((1,), (1,)), ((), ())), preferred_element_type=F32)


def full(shape):
    return pl.BlockSpec(shape, lambda i: (0,) * len(shape))


def rows_of(tile, cols):
    return pl.BlockSpec((tile, cols), lambda i: (i, 0))


def params(**more):
    return pltpu.CompilerParams(vmem_limit_bytes=VMEM_LIMIT, **more)


def cost(flops, bytes_accessed, transcendentals=0):
    return pl.CostEstimate(
        flops=int(flops), bytes_accessed=int(bytes_accessed), transcendentals=int(transcendentals)
    )


def like(shape, dtype):
    return jax.ShapeDtypeStruct(tuple(shape), dtype)


def swap(x, axis, by):
    return lax.ppermute(x, axis, [(i, i ^ by) for i in range(lax.axis_size(axis))])


def skipping(kernel, first, count):
    return lambda *refs: kernel(*refs[:first], *refs[first + count :])


def tree(values):
    while len(values) > 1:
        values = [values[i] + values[i + 1] for i in range(0, len(values), 2)]
    return values[0]


def add_kernel(*refs, count, groups):
    for out, group in zip(refs[count:], groups):
        values = [refs[i][...] if k is None else refs[i][k] for i, k in group]
        out[...] = tree([v.astype(F32) for v in values]).astype(out.dtype)


def add(arrays, groups, later=(), dtype=BF16):
    shapes = [arrays[g[0][0]].shape if g[0][1] is None else arrays[g[0][0]].shape[1:]
              for g in groups]
    count = len(arrays)
    later = list(later)
    return list(pl.pallas_call(
        skipping(functools.partial(add_kernel, count=count, groups=groups), count, len(later)),
        in_specs=[VMEM] * count + [ANY] * len(later),
        out_specs=[VMEM] * len(groups),
        out_shape=[like(s, dtype) for s in shapes],
        compiler_params=params(),
        cost_estimate=cost(0, sum(2 * a.size for a in arrays)),
        name="add",
    )(*arrays, *later))


class Whole:
    def __init__(self, array):
        self.arrays = [array]
        self.shape = array.shape
        self.count = 1

    def copies(self, where, refs, dst):
        return [(refs[0], dst)]


class Shards:
    def __init__(self, x):
        parts = lax.axis_size("fsdp")
        got = {0: x}
        for r in range(2, parts, 2):
            got[r] = swap(x, "fsdp", r)
        self.last = [got[r] for r in range(2, parts, 2)]
        for r in range(0, parts, 2):
            got[r + 1] = swap(got[r], "fsdp", 1)
        self.arrays = [got[r] for r in range(parts)]
        self.rows = x.shape[0]
        self.shape = (parts * x.shape[0], x.shape[1])
        self.count = parts

    def copies(self, where, refs, dst):
        out = []
        for r, ref in enumerate(refs):
            at = pl.multiple_of((where[0] ^ r) * self.rows, self.rows)
            out.append((ref, dst.at[pl.ds(at, self.rows), :]))
        return out


class Tiled:
    def __init__(self, gate_up, *tall):
        parts, span = lax.axis_size("fsdp"), lax.axis_size("seq")
        q = lax.axis_index("seq")
        piece = gate_up.shape[0]
        part = gate_up.shape[1] // span
        self.piece, self.part, self.parts, self.span = piece, part, parts, span
        self.heights = [t.shape[0] // span for t in tall]
        stack = jnp.concatenate([lax.dynamic_slice_in_dim(t, q * n, n, 0)
                                 for t, n in zip(tall, self.heights)])
        self.up, self.across = stack.shape[0] // 16, stack.shape[1] // 128
        stack = stack.reshape(self.up, 16, self.across, 128).transpose(2, 1, 0, 3)
        stack = stack.reshape(piece, self.up * 128)
        mine = lax.dynamic_slice_in_dim(gate_up, q * part, part, 1)
        packed = jnp.concatenate([mine, stack], axis=1)
        self.array = lax.all_gather(packed, ("seq", "fsdp"), axis=0, tiled=True)
        self.shape = (parts * piece, gate_up.shape[1])
        self.shapes = [(parts * t.shape[0], t.shape[1]) for t in tall]
        self.scratch = (span, parts * piece, self.up * 128)

    def copies(self, ref, dst, rest):
        out = []
        height = self.parts * self.piece
        for s in range(self.span):
            rows = pl.ds(s * height, height)
            out.append((ref.at[rows, pl.ds(0, self.part)],
                        dst.at[:, pl.ds(s * self.part, self.part)]))
            out.append((ref.at[rows, pl.ds(self.part, self.up * 128)], rest.at[s]))
        return out

    def unfold(self, rest, dsts):
        starts, tops = [], 0
        for n in self.heights:
            starts.append(tops)
            tops += n // 16

        def shard(d, carry):
            for s in range(self.span):
                for n, first, dst in zip(self.heights, starts, dsts):
                    for i in range(n // 16):
                        at = pl.ds(pl.multiple_of(d * n * self.span + s * n + i * 16, 16), 16)
                        for j in range(self.across):
                            row = pl.ds(pl.multiple_of(d * self.piece + 16 * j, 16), 16)
                            col = (first + i) * 128
                            dst[at, j * 128 : (j + 1) * 128] = rest[s, row, col : col + 128]
            return carry

        lax.fori_loop(0, self.parts, shard, 0)


def carry_out(copies, sem):
    made = [pltpu.make_async_copy(src, dst, sem.at[i]) for i, (src, dst) in enumerate(copies)]
    for c in made:
        c.start()
    for c in made:
        c.wait()


def project_kv_kernel(*refs, held, head_dim, mid_rows):
    where, x_ref, cos_ref, sin_ref = refs[:4]
    pieces = refs[4 : 4 + len(held.arrays)]
    normed_ref, kv_ref, w_ref, gains_ref, sem = refs[4 + len(held.arrays) :]
    kv_cols = 2 * head_dim

    @pl.when(pl.program_id(0) == 0)
    def _():
        carry_out(held.copies(where, pieces, w_ref), sem)
        gains_ref[...] = w_ref[:, kv_cols:].astype(F32).T[:8]

    half = head_dim // 2
    x = x_ref[...].astype(F32)
    inv = lax.rsqrt(jnp.mean(x * x, axis=-1, keepdims=True) + EPSILON)
    normed = (x * inv * gains_ref[0:1, :]).astype(BF16)
    normed_ref[...] = normed
    cos, sin = cos_ref[...], sin_ref[...]
    pair = mm(normed, w_ref[:, :kv_cols])
    a, b = pair[:, :half], pair[:, half:head_dim]
    kv_ref[:, :half] = (a * cos - b * sin).astype(BF16)
    kv_ref[:, half:head_dim] = (b * cos + a * sin).astype(BF16)
    kv_ref[:, head_dim:] = pair[:, head_dim:].astype(BF16)


def project_kv(where, x, cos, sin, held, head_dim):
    rows, width = x.shape
    tile = math.gcd(rows, 256)
    half = head_dim // 2
    return pl.pallas_call(
        functools.partial(project_kv_kernel, held=held, head_dim=head_dim, mid_rows=0),
        grid=(rows // tile,),
        in_specs=[SMEM, rows_of(tile, width), rows_of(tile, half), rows_of(tile, half)]
        + [ANY] * len(held.arrays),
        out_specs=[rows_of(tile, width), rows_of(tile, 2 * head_dim), full(held.shape),
                   full((8, width))],
        out_shape=[like((rows, width), BF16), like((rows, 2 * head_dim), BF16),
                   like(held.shape, BF16), like((8, width), F32)],
        scratch_shapes=[pltpu.SemaphoreType.DMA((held.count,))],
        compiler_params=params(),
        cost_estimate=cost(4 * rows * width * head_dim, 6e6),
        name="project_kv",
    )(where, x, cos, sin, *held.arrays)


def project_q_kernel(*refs, held, head_dim, q_cols, mid, scale):
    where, normed_ref, cos_ref, sin_ref = refs[:4]
    pieces = refs[4 : 4 + len(held.arrays)]
    lora_ref, q_ref, w_ref, ww_ref, sem = refs[4 + len(held.arrays) :]
    half = head_dim // 2
    fold = (held.shape[1] - q_cols - mid)
    parts = q_cols // fold

    @pl.when(pl.program_id(0) == 0)
    def _():
        carry_out(held.copies(where, pieces, w_ref), sem)
        shards = held.shape[0] // held.rows if hasattr(held, "rows") else 0
        count = mid // shards
        for d in range(shards):
            for j in range(parts):
                ww_ref[d * count : (d + 1) * count, j * fold : (j + 1) * fold] = w_ref[
                    d * held.rows + j * count : d * held.rows + (j + 1) * count, q_cols + mid :]

    normed = normed_ref[...]
    cos, sin = cos_ref[...], sin_ref[...]
    low = mm(normed, w_ref[:, q_cols : q_cols + mid]).astype(BF16)
    lora_ref[...] = low
    query = mm(normed, w_ref[:, :q_cols]) + mm(low, ww_ref[...])
    for h in range(q_cols // head_dim):
        c = h * head_dim
        a, b = query[:, c : c + half], query[:, c + half : c + head_dim]
        q_ref[:, c : c + half] = ((a * cos - b * sin) * scale).astype(BF16)
        q_ref[:, c + half : c + head_dim] = ((b * cos + a * sin) * scale).astype(BF16)


def project_q(where, normed, cos, sin, held, head_dim, q_cols, mid, scale):
    rows, width = normed.shape
    tile = math.gcd(rows, 256)
    half = head_dim // 2
    return pl.pallas_call(
        functools.partial(project_q_kernel, held=held, head_dim=head_dim, q_cols=q_cols, mid=mid,
                          scale=scale),
        grid=(rows // tile,),
        in_specs=[SMEM, rows_of(tile, width), rows_of(tile, half), rows_of(tile, half)]
        + [ANY] * len(held.arrays),
        out_specs=[rows_of(tile, mid), rows_of(tile, q_cols), full(held.shape),
                   full((mid, q_cols))],
        out_shape=[like((rows, mid), BF16), like((rows, q_cols), BF16), like(held.shape, BF16),
                   like((mid, q_cols), BF16)],
        scratch_shapes=[pltpu.SemaphoreType.DMA((held.count,))],
        compiler_params=params(),
        cost_estimate=cost(2 * rows * (width * (q_cols + mid) + mid * q_cols), 8e6),
        name="project_q",
    )(where, normed, cos, sin, *held.arrays)


def attend_kernel(*refs, head_dim, tile, block, span):
    info_ref, low_ref, q_ref = refs[:3]
    kvs = refs[3 : 3 + span]
    o_ref, lse_ref, kv_ref, vt_ref, acc_ref, sem = refs[-6:]
    heads = q_ref.shape[1] // head_dim
    rows = q_ref.shape[0]
    base, last, place = info_ref[0], info_ref[1], info_ref[2]

    def copy(s):
        at = pl.multiple_of((place ^ s) * rows, rows)
        return pltpu.make_async_copy(kvs[s], kv_ref.at[pl.ds(at, rows), :], sem.at[s])

    for s in range(span):
        pl.when((place ^ s) <= place)(lambda s=s: copy(s).start())
    for s in range(span):
        pl.when((place ^ s) <= place)(lambda s=s: copy(s).wait())

    def flip(kb, carry):
        at = pl.ds(pl.multiple_of(kb * block, block), block)
        vt_ref[:, at] = kv_ref[at, head_dim:].T
        return carry

    lax.fori_loop(info_ref[3], last, flip, 0)
    for t in range(rows // tile):
        q_rows = slice(t * tile, (t + 1) * tile)
        low = low_ref[:, q_rows]
        high = base + t * tile + lax.broadcasted_iota(jnp.int32, (1, tile), 1)
        acc_ref[...] = jnp.zeros_like(acc_ref)

        def visit(kb, carry):
            at = pl.ds(pl.multiple_of(kb * block, block), block)
            keys = kv_ref[at, :head_dim]
            vt = vt_ref[:, at]
            index = kb * block + lax.broadcasted_iota(jnp.int32, (block, tile), 0)
            mask = (index >= low) & (index <= high)
            out = []
            for h in range(heads):
                peak, total = carry[h]
                s = mm_nt(keys, q_ref[q_rows, h * head_dim : (h + 1) * head_dim])
                s = jnp.where(mask, s, -jnp.inf)
                new_peak = jnp.maximum(peak, jnp.max(s, axis=0, keepdims=True))
                factor = jnp.exp(peak - new_peak)
                p = jnp.exp(s - new_peak)
                total = total * factor + jnp.sum(p, axis=0, keepdims=True)
                acc_ref[h] = acc_ref[h] * factor + mm(vt, p.astype(BF16))
                out.append((new_peak, total))
            return tuple(out)

        start = tuple(
            (jnp.full((1, tile), LOWEST, F32), jnp.zeros((1, tile), F32)) for _ in range(heads)
        )
        stats = lax.fori_loop(info_ref[3 + t], (base + (t + 1) * tile + block - 1) // block,
                              visit, start)
        for h in range(heads):
            peak, total = stats[h]
            o_ref[q_rows, h * head_dim : (h + 1) * head_dim] = (acc_ref[h] / total).T.astype(BF16)
            lse_ref[h : h + 1, q_rows] = peak + jnp.log(total)


def attend(info, low, q, kvs, head_dim, tile, block, m, batches, before=None):
    q_cols = q.shape[1]
    rows = q.shape[0] // batches
    heads = q_cols // head_dim
    span = len(kvs)
    group = span * rows
    here = pl.BlockSpec((rows, q_cols), lambda i: (m, 0))
    more = [] if before is None else [before]
    return pl.pallas_call(
        functools.partial(attend_kernel, head_dim=head_dim, tile=tile, block=block, span=span),
        grid=(1,),
        in_specs=[SMEM, VMEM, here] + [ANY] * (span + len(more)),
        out_specs=[here, VMEM, VMEM],
        out_shape=[like(q.shape, BF16), like((heads, rows), F32),
                   like((group, 2 * head_dim), BF16)],
        scratch_shapes=[pltpu.VMEM((head_dim, group), BF16),
                        pltpu.VMEM((heads, head_dim, tile), F32),
                        pltpu.SemaphoreType.DMA((span,))],
        input_output_aliases={3 + span: 0} if more else {},
        compiler_params=params(),
        cost_estimate=cost(4 * rows * group * q_cols, 6e6, rows * group * heads),
        name="attend",
    )(info, low, q, *kvs, *more)


def middle_kernel(*refs, held, head_dim, chunk):
    x_ref, attn_ref, g_ref, gains_ref = refs[:4]
    if held is None:
        w_ref, wd_ref, wo_ref = refs[4:7]
    else:
        w_ref, wd_ref, wo_ref, rest_ref, sem = refs[-5:]
    (out_ref, mid_grad_ref, branch_ref, attn_grad_ref, delta_ref, low_ref, hidden_ref, grads_ref,
     gain_grad_ref) = refs[5:14] if held is not None else refs[7:16]

    @pl.when(pl.program_id(0) == 0)
    def _():
        if held is not None:
            carry_out(held.copies(refs[4], w_ref, rest_ref), sem)
            held.unfold(rest_ref, [wd_ref, wo_ref])
        gain_grad_ref[...] = jnp.zeros_like(gain_grad_ref)

    gain = gains_ref[1:2, :]
    attn = attn_ref[...]
    middle = x_ref[...].astype(F32) + mm(attn, wo_ref[...])
    inv = lax.rsqrt(jnp.mean(middle * middle, axis=-1, keepdims=True) + EPSILON)
    unit = middle * inv
    low = (unit * gain).astype(BF16)
    low_ref[...] = low
    grad = g_ref[...]
    result = middle
    back = jnp.zeros_like(middle)
    wide = wd_ref.shape[0]
    for c in range(wide // chunk):
        at = slice(c * chunk, (c + 1) * chunk)
        to = slice(wide + c * chunk, wide + (c + 1) * chunk)
        gate = mm(low, w_ref[:, at])
        lift = mm(low, w_ref[:, to])
        square = gate * gate
        bend = jnp.tanh(GELU_C * gate * (1.0 + GELU_A * square))
        cdf = 0.5 * (1.0 + bend)
        gelu = gate * cdf
        hidden = (gelu * lift).astype(BF16)
        hidden_ref[:, at] = hidden
        result = result + mm(hidden, wd_ref[at, :])
        hidden_grad = mm_nt(grad, wd_ref[at, :])
        slope = cdf + (0.5 * GELU_C) * gate * (1.0 - bend * bend) * (1.0 + 3.0 * GELU_A * square)
        gate_grad = (hidden_grad * lift * slope).astype(BF16)
        lift_grad = (hidden_grad * gelu).astype(BF16)
        grads_ref[:, at] = gate_grad
        grads_ref[:, to] = lift_grad
        back = back + mm_nt(gate_grad, w_ref[:, at]) + mm_nt(lift_grad, w_ref[:, to])
    out_ref[...] = result.astype(BF16)
    gain_grad_ref[...] += jnp.sum(unit * back, axis=0, keepdims=True)
    scaled = back * gain
    mid_grad = grad.astype(F32) + inv * (
        scaled - unit * jnp.mean(unit * scaled, axis=-1, keepdims=True)
    )
    mid_grad_ref[...] = mid_grad
    branch = mid_grad.astype(BF16)
    branch_ref[...] = branch
    attn_grad = mm_nt(branch, wo_ref[...]).astype(BF16)
    attn_grad_ref[...] = attn_grad
    product = attn_grad.astype(F32) * attn.astype(F32)
    half = head_dim // 2
    for h in range(attn.shape[1] // head_dim):
        c = h * head_dim
        folded = product[:, c : c + half] + product[:, c + half : c + head_dim]
        delta_ref[h : h + 1, :] = jnp.sum(folded.T, axis=0, keepdims=True)


def middle_part(x, attn, grad, gains, held, weights, head_dim):
    rows, width = x.shape
    q_cols = attn.shape[1]
    hidden = (weights[0].shape if held is None else held.shape)[1] // 2
    heads = q_cols // head_dim
    tile = math.gcd(rows, 256)
    if held is None:
        more, specs, scratch = weights, [full(w.shape) for w in weights], []
    else:
        more, specs = [held.array], [ANY]
        scratch = [pltpu.VMEM(held.shape, BF16)] + [pltpu.VMEM(s, BF16) for s in held.shapes]
        scratch += [pltpu.VMEM(held.scratch, BF16), pltpu.SemaphoreType.DMA((2 * held.span,))]
    return pl.pallas_call(
        functools.partial(middle_kernel, held=held, head_dim=head_dim, chunk=512),
        grid=(rows // tile,),
        in_specs=[rows_of(tile, width), rows_of(tile, q_cols), rows_of(tile, width),
                  full(gains.shape)] + specs,
        out_specs=[rows_of(tile, width), rows_of(tile, width), rows_of(tile, width),
                   rows_of(tile, q_cols), pl.BlockSpec((heads, tile), lambda i: (0, i)),
                   rows_of(tile, width), rows_of(tile, hidden), rows_of(tile, 2 * hidden),
                   full((1, width))],
        out_shape=[like((rows, width), BF16), like((rows, width), F32), like((rows, width), BF16),
                   like((rows, q_cols), BF16), like((heads, rows), F32),
                   like((rows, width), BF16), like((rows, hidden), BF16),
                   like((rows, 2 * hidden), BF16), like((1, width), F32)],
        scratch_shapes=scratch,
        compiler_params=params(),
        cost_estimate=cost(4 * rows * width * (q_cols + 3 * hidden), 40e6, rows * hidden),
        name="middle",
    )(x, attn, grad, gains, *more)


def attend_back_kernel(*refs, head_dim, tile, block, scale):
    info_ref, low_ref, lse_ref, delta_ref, q_ref, do_ref, kv_ref, cos_ref, sin_ref = refs[:9]
    span = kv_ref.shape[0] // q_ref.shape[0]
    sends = refs[-3 - (span - 1) : -3]
    dq_ref, own_ref = refs[-3 - span - 1 : -3 - span + 1]
    dkv_ref, kt_ref, acc_ref = refs[-3:]
    heads = q_ref.shape[1] // head_dim
    half = head_dim // 2
    rows = q_ref.shape[0]
    base, last, place = info_ref[0], info_ref[1], info_ref[2]
    tiles = rows // tile
    acc_ref[...] = jnp.zeros_like(acc_ref)
    dkv_ref[...] = jnp.zeros_like(dkv_ref)

    def visit(kb, carry):
        at = pl.ds(pl.multiple_of(kb * block, block), block)
        keys = kv_ref[at, :head_dim]
        vals = kv_ref[at, head_dim:]
        kt_ref[...] = keys.T
        for t in range(tiles):
            q_rows = slice(t * tile, (t + 1) * tile)

            @pl.when((kb >= info_ref[3 + t]) & (kb * block < base + (t + 1) * tile))
            def _():
                low = low_ref[:, q_rows]
                high = base + t * tile + lax.broadcasted_iota(jnp.int32, (1, tile), 1)
                index = kb * block + lax.broadcasted_iota(jnp.int32, (block, tile), 0)
                mask = (index >= low) & (index <= high)
                dk = jnp.zeros((block, head_dim), F32)
                dv = jnp.zeros((block, head_dim), F32)
                for h in range(heads):
                    cols = slice(h * head_dim, (h + 1) * head_dim)
                    q = q_ref[q_rows, cols]
                    do = do_ref[q_rows, cols]
                    s = mm_nt(keys, q)
                    p = jnp.where(mask, jnp.exp(s - lse_ref[h : h + 1, q_rows]), 0.0)
                    dv = dv + mm(p.astype(BF16), do)
                    ds = (p * (mm_nt(vals, do) - delta_ref[h : h + 1, q_rows])).astype(BF16)
                    dk = dk + mm(ds, q)
                    acc_ref[h, :, q_rows] += mm(kt_ref[...], ds)
                dkv_ref[at, :head_dim] += dk
                dkv_ref[at, head_dim:] += dv

        return carry

    lax.fori_loop(info_ref[3], last, visit, 0)
    cos, sin = cos_ref[...], sin_ref[...]
    for h in range(heads):
        c = h * head_dim
        dq = acc_ref[h].T * scale
        a, b = dq[:, :half], dq[:, half:]
        dq_ref[:, c : c + half] = (a * cos + b * sin).astype(BF16)
        dq_ref[:, c + half : c + head_dim] = (b * cos - a * sin).astype(BF16)
    own_ref[...] = dkv_ref[pl.ds(pl.multiple_of(place * rows, rows), rows), :]
    for s, send_ref in enumerate(sends, 1):
        at = pl.multiple_of((place ^ s) * rows, rows)
        send_ref[...] = dkv_ref[pl.ds(at, rows), :].astype(BF16)


def attend_back(info, low, lse, delta, q, do, kv, cos, sin, head_dim, tile, block, scale, m,
                batches, before, later):
    q_cols = q.shape[1]
    rows = q.shape[0] // batches
    heads = q_cols // head_dim
    span = kv.shape[0] // rows
    half = head_dim // 2
    here = pl.BlockSpec((rows, q_cols), lambda i: (m, 0))
    angle = pl.BlockSpec((rows, half), lambda i: (m, 0))
    more = ([] if before is None else [before]) + later
    return pl.pallas_call(
        functools.partial(attend_back_kernel, head_dim=head_dim, tile=tile, block=block,
                          scale=scale),
        grid=(1,),
        in_specs=[SMEM, VMEM, VMEM, pl.BlockSpec((heads, rows), lambda i: (0, m)), here, here,
                  VMEM, angle, angle] + [ANY] * len(more),
        out_specs=[here] + [VMEM] * span,
        out_shape=[like(q.shape, BF16), like((rows, 2 * head_dim), F32)]
        + [like((rows, 2 * head_dim), BF16)] * (span - 1),
        scratch_shapes=[pltpu.VMEM(kv.shape, F32), pltpu.VMEM((head_dim, block), BF16),
                        pltpu.VMEM((heads, head_dim, rows), F32)],
        input_output_aliases={} if before is None else {9: 0},
        compiler_params=params(),
        cost_estimate=cost(10 * rows * kv.shape[0] * q_cols, 12e6, rows * kv.shape[0] * heads),
        name="attend_back",
    )(info, low, lse, delta, q, do, kv, cos, sin, *more)


def query_back_kernel(dq_ref, w_ref, ww_ref, lora_grad_ref, back_ref, *, q_cols, mid):
    dq = dq_ref[...]
    lora_grad = mm_nt(dq, ww_ref[...]).astype(BF16)
    lora_grad_ref[...] = lora_grad
    back_ref[...] = (mm_nt(dq, w_ref[:, :q_cols])
                     + mm_nt(lora_grad, w_ref[:, q_cols : q_cols + mid]))


def query_back(dq, w, ww, later=()):
    rows, q_cols = dq.shape
    mid, width = ww.shape[0], w.shape[0]
    tile = math.gcd(rows, 256)
    return pl.pallas_call(
        skipping(functools.partial(query_back_kernel, q_cols=q_cols, mid=mid), 3, len(later)),
        grid=(rows // tile,),
        in_specs=[rows_of(tile, q_cols), full(w.shape), full(ww.shape)] + [ANY] * len(later),
        out_specs=[rows_of(tile, mid), rows_of(tile, width)],
        out_shape=[like((rows, mid), BF16), like((rows, width), F32)],
        compiler_params=params(),
        cost_estimate=cost(2 * rows * (width * (q_cols + mid) + mid * q_cols), 9e6),
        name="query_back",
    )(dq, w, ww, *later)


def pair_back_kernel(*refs, head_dim, others):
    x_ref, gains_ref, cos_ref, sin_ref, w_ref, back_ref, mid_grad_ref, own_ref = refs[:8]
    pair_grad_ref, in_grad_ref, gain_grad_ref = refs[-3:]

    @pl.when(pl.program_id(0) == 0)
    def _():
        gain_grad_ref[...] = jnp.zeros_like(gain_grad_ref)

    half = head_dim // 2
    gain = gains_ref[0:1, :]
    cos, sin = cos_ref[...], sin_ref[...]
    dkv = own_ref[...]
    for ref in refs[8 : 8 + others]:
        dkv = dkv + ref[...].astype(F32)
    a, b = dkv[:, :half], dkv[:, half:head_dim]
    pair_grad_ref[:, :half] = (a * cos + b * sin).astype(BF16)
    pair_grad_ref[:, half:head_dim] = (b * cos - a * sin).astype(BF16)
    pair_grad_ref[:, head_dim:] = dkv[:, head_dim:].astype(BF16)
    back = back_ref[...] + mm_nt(pair_grad_ref[...], w_ref[:, : 2 * head_dim])
    x = x_ref[...].astype(F32)
    inv = lax.rsqrt(jnp.mean(x * x, axis=-1, keepdims=True) + EPSILON)
    unit = x * inv
    gain_grad_ref[...] += jnp.sum(unit * back, axis=0, keepdims=True)
    scaled = back * gain
    in_grad_ref[...] = mid_grad_ref[...] + inv * (
        scaled - unit * jnp.mean(unit * scaled, axis=-1, keepdims=True)
    )


def pair_back(x, gains, cos, sin, w, own, others, back, mid_grad, head_dim, m, batches, before=None,
              later=()):
    width = x.shape[1]
    rows = x.shape[0] // batches
    tile = math.gcd(rows, 256)
    half, cols = head_dim // 2, 2 * head_dim
    count = rows // tile

    def here(n):
        return pl.BlockSpec((tile, n), lambda i: (m * count + i, 0))

    more = ([] if before is None else [before]) + list(later)
    return pl.pallas_call(
        functools.partial(pair_back_kernel, head_dim=head_dim, others=len(others)),
        grid=(count,),
        in_specs=[here(width), full(gains.shape), here(half), here(half), full(w.shape),
                  here(width), here(width)] + [rows_of(tile, cols)] * (1 + len(others))
        + [ANY] * len(more),
        out_specs=[rows_of(tile, cols), here(width), full((1, width))],
        out_shape=[like((rows, cols), BF16), like(x.shape, F32), like((1, width), F32)],
        input_output_aliases={} if before is None else {8 + len(others): 1},
        compiler_params=params(),
        cost_estimate=cost(2 * rows * width * cols, 7e6),
        name="pair_back",
    )(x, gains, cos, sin, w, back, mid_grad, own, *others, *more)


def weight_grad_kernel(x_ref, y_ref, out_ref, xt_ref):
    @pl.when(pl.program_id(0) == 0)
    def _():
        xt_ref[...] = x_ref[...].T

    out_ref[...] = mm(xt_ref[...], y_ref[...]).astype(BF16)


def weight_grad(x, y, tile=256, later=()):
    rows, width = x.shape
    cols = y.shape[1]
    tile = math.gcd(cols, tile)
    return pl.pallas_call(
        skipping(weight_grad_kernel, 2, len(later)),
        grid=(cols // tile,),
        in_specs=[full(x.shape), pl.BlockSpec((rows, tile), lambda i: (0, i))] + [ANY] * len(later),
        out_specs=pl.BlockSpec((width, tile), lambda i: (0, i)),
        out_shape=like((width, cols), BF16),
        scratch_shapes=[pltpu.VMEM((width, rows), BF16)],
        compiler_params=params(),
        cost_estimate=cost(2 * rows * width * cols, 2 * (rows * width + rows * cols + width * cols)),
        name="weight_grad",
    )(x, y, *later)


def turn(x_ref, flat_ref, xt_ref, me, parts):
    flat_ref[...] = x_ref[...].T
    piece = flat_ref.shape[0] // parts
    for r in range(parts):
        at = pl.multiple_of((me ^ r) * piece, piece)
        to = (r % 2) * (parts // 2) + r // 2
        xt_ref[to * piece : (to + 1) * piece, :] = flat_ref[pl.ds(at, piece), :]


def column_grads_kernel(where, g_ref, b_ref, hidden_ref, attn_ref, keep_ref, send_ref, gt_ref,
                        bt_ref, *, piece):
    r = pl.program_id(0)

    @pl.when(r == 0)
    def _():
        gt_ref[...] = g_ref[...].T
        bt_ref[...] = b_ref[...].T

    down = mm(gt_ref[...], hidden_ref[...]).astype(BF16)
    out = mm(bt_ref[...], attn_ref[...]).astype(BF16)

    def put(ref):
        span = ref.shape[0]
        per = down.shape[0] // piece // span
        n, k = down.shape[1], out.shape[1]
        for s in range(span):
            to = s ^ where[1]
            for i in range(per):
                at = slice((s * per + i) * piece, (s * per + i + 1) * piece)
                ref[to, 0, :, i * n : (i + 1) * n] = down[at]
                ref[to, 0, :, per * n + i * k : per * n + (i + 1) * k] = out[at]

    pl.when(r % 2 == 0)(lambda: put(keep_ref))
    pl.when(r % 2 == 1)(lambda: put(send_ref))


def column_grads(where, grad, hidden, branch, attn, parts, span):
    rows, width = grad.shape
    piece = width // parts
    n, k = hidden.shape[1] // parts, attn.shape[1] // parts
    cols = (n + k) * (parts // span)
    block = pl.BlockSpec((span, 1, piece, cols), lambda r, where: (0, r // 2, 0, 0))
    shape = like((span, parts // 2, piece, cols), BF16)
    whole = pl.BlockSpec((rows, width), lambda r, where: (0, 0))
    return pl.pallas_call(
        functools.partial(column_grads_kernel, piece=piece),
        grid_spec=pltpu.PrefetchScalarGridSpec(
            num_scalar_prefetch=1,
            grid=(parts,),
            in_specs=[whole, whole,
                      pl.BlockSpec((rows, n), lambda r, where: (0, where[0] ^ r)),
                      pl.BlockSpec((rows, k), lambda r, where: (0, where[0] ^ r))],
            out_specs=[block, block],
            scratch_shapes=[pltpu.VMEM((width, rows), BF16)] * 2,
        ),
        out_shape=[shape, shape],
        compiler_params=params(),
        cost_estimate=cost(2 * rows * width * cols * span, 16e6),
        name="column_grads",
    )(where, grad, branch, hidden, attn)


def query_grads_kernel(normed_ref, lora_ref, dq_ref, lora_grad_ref, out_ref, xt_ref, xt2_ref,
                       *, parts, fold):
    xt_ref[...] = normed_ref[...].T
    xt2_ref[...] = lora_ref[...].T
    piece, count = xt_ref.shape[0] // parts, xt2_ref.shape[0] // parts
    q_cols, mid = dq_ref.shape[1], lora_grad_ref.shape[1]
    step = math.gcd(q_cols, 512)
    for c in range(0, q_cols, step):
        out_ref[:, c : c + step] = mm(xt_ref[...], dq_ref[:, c : c + step]).astype(BF16)
    out_ref[:, q_cols : q_cols + mid] = mm(xt_ref[...], lora_grad_ref[...]).astype(BF16)
    for j in range(q_cols // fold):
        out = mm(xt2_ref[...], dq_ref[:, j * fold : (j + 1) * fold]).astype(BF16)
        for d in range(parts):
            at = d * piece + j * count
            out_ref[at : at + count, q_cols + mid :] = out[d * count : (d + 1) * count]
    rest = (q_cols // fold) * count
    for d in range(parts):
        out_ref[d * piece + rest : (d + 1) * piece, q_cols + mid :] = jnp.zeros(
            (piece - rest, fold), BF16)


def query_grads(normed, lora_mid, dq, lora_grad, parts, fold):
    rows, width = normed.shape
    mid, q_cols = lora_mid.shape[1], dq.shape[1]
    return pl.pallas_call(
        functools.partial(query_grads_kernel, parts=parts, fold=fold),
        in_specs=[VMEM] * 4,
        out_specs=VMEM,
        out_shape=like((width, q_cols + mid + fold), BF16),
        scratch_shapes=[pltpu.VMEM((width, rows), BF16), pltpu.VMEM((mid, rows), BF16)],
        compiler_params=params(),
        cost_estimate=cost(2 * rows * (width * (q_cols + mid) + mid * q_cols), 10e6),
        name="query_grads",
    )(normed, lora_mid, dq, lora_grad)


def pair_grads_kernel(where, normed_ref, *refs, parts, batches):
    pairs, ones = refs[:batches], refs[batches : 2 * batches]
    two_ref = refs[2 * batches]
    outs, (flat_ref, xt_ref, gain_ref) = refs[2 * batches + 1 : -3], refs[-3:]
    send_ref, keeps = outs[0], outs[1:]
    turn(normed_ref, flat_ref, xt_ref, where[0], parts)
    width = flat_ref.shape[0]
    piece, half, cols = width // parts, parts // 2, pairs[0].shape[1]
    pair = jnp.concatenate([p[...] for p in pairs])
    out = mm(xt_ref[...], pair).astype(BF16)
    pad = jnp.zeros((126, width), F32)
    one = ones[0][...]
    for ref in ones[1:]:
        one = one + ref[...]
    gain_ref[...] = jnp.concatenate([one, two_ref[...], pad], axis=0).T.astype(BF16)
    for k in range(half):
        keeps[k][:, :cols] = out[k * piece : (k + 1) * piece]
        send_ref[k, :, :cols] = out[(half + k) * piece : (half + k + 1) * piece]
        at = pl.multiple_of((where[0] ^ (2 * k)) * piece, piece)
        keeps[k][:, cols:] = gain_ref[pl.ds(at, piece), :]
        at = pl.multiple_of((where[0] ^ (2 * k + 1)) * piece, piece)
        send_ref[k, :, cols:] = gain_ref[pl.ds(at, piece), :]


def pair_grads(where, normed, pairs, ones, two, parts):
    rows, width = normed.shape
    cols = pairs[0].shape[1]
    piece = width // parts
    batches = len(pairs)
    return pl.pallas_call(
        functools.partial(pair_grads_kernel, parts=parts, batches=batches),
        in_specs=[SMEM] + [VMEM] * (2 + 2 * batches),
        out_specs=[VMEM] * (1 + parts // 2),
        out_shape=[like((parts // 2, piece, cols + 128), BF16)]
        + [like((piece, cols + 128), BF16)] * (parts // 2),
        scratch_shapes=[pltpu.VMEM((width, rows), BF16)] * 2 + [pltpu.VMEM((width, 128), BF16)],
        compiler_params=params(),
        cost_estimate=cost(2 * rows * width * cols, 4e6),
        name="pair_grads",
    )(where, normed, *pairs, *ones, two)


def sum_owned(send, keeps):
    got = swap(send, "fsdp", 1)
    count = len(keeps)
    shards = add([*keeps, got], [[(k, None), (count, k)] for k in range(count)])
    there = [shards[0]] + [swap(a, "fsdp", 2 * k) for k, a in enumerate(shards) if k > 0]
    return add(there, [[(i, None) for i in range(count)]])[0]


class QuarterSum:
    def __init__(self, keep, send):
        self.keep, self.got = keep, swap(send, "fsdp", 1)

    def cores(self, *later):
        self.parts = add([self.keep, self.got],
                         [[(0, s), (1, s)] for s in range(self.keep.shape[0])], later)
        self.there = [self.parts[0]] + [
            swap(a, "seq", s) for s, a in enumerate(self.parts) if s > 0]
        return self

    def chips(self, *later):
        count, span = self.keep.shape[1], len(self.there)
        self.shards = add(self.there, [[(s, k) for s in range(span)] for k in range(count)], later)
        self.here = [self.shards[0]] + [
            swap(a, "fsdp", 2 * k) for k, a in enumerate(self.shards) if k > 0]
        return self

    def total(self, *later):
        return add(self.here, [[(k, None) for k in range(len(self.here))]], later)[0]


def cut_kernel(where, x_ref, *outs):
    part = outs[0].shape[1]
    for s, out in enumerate(outs):
        at = pl.multiple_of((where[1] ^ s) * part, part)
        out[...] = x_ref[:, pl.ds(at, part)]


def sum_parts(where, x, later=()):
    span = lax.axis_size("seq")
    rows, part = x.shape[0], x.shape[1] // span
    cut = pl.pallas_call(
        skipping(cut_kernel, 2, len(later)),
        in_specs=[SMEM, VMEM] + [ANY] * len(later),
        out_specs=[VMEM] * span,
        out_shape=[like((rows, part), x.dtype)] * span,
        compiler_params=params(),
        cost_estimate=cost(0, 4 * x.size),
        name="cut",
    )(where, x, *later)
    there = [cut[0]] + [swap(cut[s], "seq", s) for s in range(1, span)]
    return add(there, [[(s, None) for s in range(span)]])[0]


def lay_kernel(where, *refs, n, k):
    span = (len(refs) - 6) // 2
    parts, columns = refs[:span], refs[span : 2 * span]
    gate_ref, up_ref, down_ref, out_ref, tall_ref, tall2_ref = refs[-6:]
    piece = parts[0].shape[0]
    half = span // 2
    wide = parts[0].shape[1]
    per = columns[0].shape[1] // (n + k)
    for s in range(span):
        ref, col_ref = parts[s], columns[s]
        q = where[1] ^ s
        for i, out in enumerate((gate_ref, up_ref)):
            @pl.when(q // half == i)
            def _():
                at = pl.multiple_of((q % half) * wide, wide)
                out[:, pl.ds(at, wide)] = ref[...].astype(F32)
        for i in range(per):
            at = pl.ds(pl.multiple_of((q * per + i) * piece, piece), piece)
            tall_ref[at, :] = col_ref[:, i * n : (i + 1) * n].astype(F32)
            first = per * n + i * k
            tall2_ref[at, :] = col_ref[:, first : first + k].astype(F32)
    down_ref[...] = tall_ref[...].T
    out_ref[...] = tall2_ref[...].T


def lay(where, parts, columns, hidden, n, k, later=()):
    piece = parts[0].shape[0]
    width = piece * lax.axis_size("fsdp")
    return pl.pallas_call(
        skipping(functools.partial(lay_kernel, n=n, k=k), 1 + 2 * len(parts), len(later)),
        in_specs=[SMEM] + [VMEM] * (2 * len(parts)) + [ANY] * len(later),
        out_specs=[VMEM] * 4,
        out_shape=[like((piece, hidden), F32)] * 2 + [like((n, width), F32), like((k, width), F32)],
        scratch_shapes=[pltpu.VMEM((width, n), F32), pltpu.VMEM((width, k), F32)],
        compiler_params=params(),
        cost_estimate=cost(0, 6e6),
        name="lay",
    )(where, *parts, *columns, *later)


def layout(lengths, index):
    ends = jnp.cumsum(lengths, dtype=jnp.int32)
    starts = ends - lengths
    number = jnp.sum((index[:, None] >= ends[None, :]).astype(jnp.int32), axis=1, dtype=jnp.int32)
    live = index < ends[-1]
    match = number[:, None] == jnp.arange(lengths.shape[0], dtype=jnp.int32)[None, :]
    begin = jnp.sum(jnp.where(match, starts[None, :], 0), axis=1, dtype=jnp.int32)
    return jnp.where(live, begin, index), jnp.where(live, index - begin, 0)


def local(tokens, document_lengths, cotangent, attention_gain, query_projection, narrowing_factor,
          widening_factor, key_value_projection, output_projection, feedforward_gain,
          gate_projection, up_projection, down_projection):
    batches, _, rows, width = tokens.shape
    head_dim = key_value_projection.shape[1] // 2
    q_cols = query_projection.shape[1]
    mid = narrowing_factor.shape[1]
    hidden = gate_projection.shape[1]
    kv_cols = 2 * head_dim
    scale = head_dim ** (-0.5)
    parts, span = lax.axis_size("fsdp"), lax.axis_size("seq")
    place = lax.axis_index("seq")
    tile = math.gcd(rows, 256)
    block = math.gcd(rows, 512)
    where = jnp.stack([lax.axis_index("fsdp"), place]).astype(jnp.int32)
    piece = width // parts
    direct = piece % 16 == 0
    fold = 512
    folds = q_cols // fold

    first = jnp.concatenate(
        [key_value_projection,
         jnp.pad(jnp.stack([attention_gain, feedforward_gain], axis=1), ((0, 0), (0, 126)))],
        axis=1)
    turned = jnp.concatenate([widening_factor[:, j * fold : (j + 1) * fold] for j in range(folds)])
    turned = jnp.pad(turned, ((0, piece - turned.shape[0]), (0, 0)))
    second = jnp.concatenate([query_projection, narrowing_factor, turned], axis=1)
    gate_up = jnp.concatenate([gate_projection, up_projection], axis=1)
    if direct:
        held, weights = Tiled(gate_up, down_projection, output_projection), None
        first = Shards(first)
        second = Shards(second)
    else:
        def gather(x):
            return lax.all_gather(x, "fsdp", axis=0, tiled=True)

        first, second = Whole(gather(first)), Whole(gather(second))
        second.rows = piece
        held = None
        weights = [gather(gate_up), gather(down_projection), gather(output_projection)]

    index = place * rows + jnp.arange(rows, dtype=jnp.int32)
    lows, positions = [], []
    for m in range(batches):
        low, position = layout(document_lengths[m, 0], index)
        lows.append(low)
        positions.append(position)
    position = jnp.concatenate(positions).astype(F32)
    half = head_dim // 2
    freqs = THETA ** (-(jnp.arange(half, dtype=F32) * 2.0 / head_dim))
    angles = position[:, None] * freqs[None, :]
    cos, sin = jnp.cos(angles), jnp.sin(angles)
    infos = []
    for m in range(batches):
        marks = [place * rows, ((place + 1) * rows + block - 1) // block, place]
        marks += [lows[m][t * tile] // block for t in range(rows // tile)]
        infos.append(jnp.stack(marks).astype(jnp.int32))

    x = tokens.reshape(batches * rows, width)
    grad = cotangent.reshape(batches * rows, width)
    normed, kv, w_pair, gains = project_kv(where, x, cos, sin, first, head_dim)
    cuts = [slice(m * rows, (m + 1) * rows) for m in range(batches)]
    kvs = []
    for at in cuts:
        kvs.append([kv[at]] + [swap(kv[at], "seq", s) for s in range(1, span)])
    lora_mid, q, w_query, ww = project_q(where, normed, cos, sin, second, head_dim, q_cols, mid,
                                         scale)
    attended, lses, groups = None, [], []
    for m in range(batches):
        attended, lse, group = attend(infos[m], lows[m][None, :], q, kvs[m], head_dim, tile, block,
                                      m, batches, attended)
        lses.append(lse)
        groups.append(group)
    (output, mid_grad, branch, attn_grad, delta, ffn_low, hidden_low, lift_grads,
     gain_two_grad) = middle_part(x, attended, grad, gains, held, weights, head_dim)

    if direct:
        columns = QuarterSum(*column_grads(where, grad, hidden_low, branch, attended, parts, span))
        lifts = weight_grad(ffn_low, lift_grads, 512, [columns.keep])
        columns.cores(lifts)
        lifts_sum = lax.psum_scatter(lifts, "fsdp", scatter_dimension=0, tiled=True)
    dq, owns, others = None, [], []
    for m in range(batches):
        later = []
        if direct and m == 0:
            later = columns.parts + [lifts]
        if direct and m == 1:
            later = columns.chips(dq).shards
        dq, own, *sends = attend_back(infos[m], lows[m][None, :], lses[m], delta, q, attn_grad,
                                      groups[m], cos, sin, head_dim, tile, block, scale, m, batches,
                                      dq, later)
        owns.append(own)
        others.append([swap(a, "seq", s) for s, a in enumerate(sends, 1)])
    later = []
    if direct:
        columns_sum = columns.total(dq)
        later = others[0] + [columns_sum]
    lora_grad, back = query_back(dq, w_query, ww, later)
    later = [], []
    if direct:
        queries = query_grads(normed, lora_mid, dq, lora_grad, parts, fold)
        queries_sum = lax.psum_scatter(queries, "fsdp", scatter_dimension=0, tiled=True)
        lifts_part = sum_parts(where, lifts_sum, [lora_grad])
        later = [queries], [lifts_part]
    in_grad, pairs, ones = None, [], []
    for m in range(batches):
        pair, in_grad, one = pair_back(x, gains, cos, sin, w_pair, owns[m], others[m], back,
                                       mid_grad, head_dim, m, batches, in_grad, later[m])
        pairs.append(pair)
        ones.append(one)
    if direct:
        send, *keeps = pair_grads(where, normed, pairs, ones, gain_two_grad, parts)
        pairs_sum = sum_owned(send, keeps)

        def share(x):
            return [x] + [swap(x, "seq", s) for s in range(1, span)]

        gate_grad, up_grad, down_grad, out_grad = lay(
            where, share(lifts_part), share(columns_sum), hidden, hidden // parts, q_cols // parts,
            [send])
        mine = jnp.concatenate([queries_sum, pairs_sum], axis=1)
        last = add(share(mine), [[(s, None) for s in range(span)]], dtype=F32)[0]
        query_grad = last[:, :q_cols]
        narrow_grad = last[:, q_cols : q_cols + mid]
        count = mid // parts
        widen_grad = jnp.concatenate(
            [last[j * count : (j + 1) * count, q_cols + mid : q_cols + mid + fold]
             for j in range(folds)], axis=1)
        first = q_cols + mid + fold
        key_value_grad = last[:, first : first + kv_cols]
        gain_one_grad = last[:, first + kv_cols]
        gain_two_grad = last[:, first + kv_cols + 1]
    else:
        def scatter(x):
            part = lax.psum_scatter(x.astype(BF16), "fsdp", scatter_dimension=0, tiled=True)
            return lax.psum(part, "seq").astype(F32)

        pair_grad = jnp.concatenate(pairs)
        gain_one_grad = sum(ones)
        down_grad = scatter(weight_grad(grad, hidden_low).T)
        out_grad = scatter(weight_grad(branch, attended).T)
        lift_w = scatter(weight_grad(ffn_low, lift_grads))
        gate_grad, up_grad = lift_w[:, :hidden], lift_w[:, hidden:]
        query_grad = scatter(weight_grad(normed, dq))
        narrow_grad = scatter(weight_grad(normed, lora_grad))
        widen_grad = scatter(weight_grad(lora_mid, dq))
        key_value_grad = scatter(weight_grad(normed, pair_grad))
        gains_grad = scatter(jnp.concatenate([gain_one_grad, gain_two_grad]).T)
        gain_one_grad, gain_two_grad = gains_grad[:, 0], gains_grad[:, 1]
    return (output.reshape(batches, 1, rows, width), in_grad.reshape(batches, 1, rows, width),
            gain_one_grad, query_grad, narrow_grad, widen_grad, key_value_grad, out_grad,
            gain_two_grad, gate_grad, up_grad, down_grad)


def solution(mesh):
    rows = P(None, "fsdp", "seq", None)
    vector, matrix = P("fsdp"), P("fsdp", None)
    in_specs = (rows, P(None, "fsdp", None), rows, vector) + (matrix,) * 5 + (vector,) + (matrix,) * 3
    out_specs = (rows, rows, vector) + (matrix,) * 5 + (vector,) + (matrix,) * 3
    return jax.shard_map(local, mesh=mesh, in_specs=in_specs, out_specs=out_specs, check_vma=False)
```

time: 647 us -> 420 us (0.65)
  waiting for transfers between devices: 367 us -> 111 us
  starting transfers between devices: 0.74 us -> 79.3 us
  local copies, waits for them, and re-layouts: 58.4 us -> 25.2 us
  Pallas kernels: 138 us -> 161 us
  blocking collectives: 19.6 us -> 0 us
  other arithmetic: 29.7 us -> 11.4 us
    all_gather x6 -> x1, waiting for transfers between devices: 156 us -> 4.12 us  [__init__(): self.array = lax.all_gather(packed, ('seq', 'fsdp'), axis=0, tiled=True)]
    reduce_scatter x5 -> x2, waiting for transfers between devices: 147 us -> 0.01 us  [the longest x1 0.01 us: local(): lifts_sum = lax.psum_scatter(lifts, 'fsdp', scatter_dimension=0, tiled=True)]
    ppermute x0 -> x49, waiting for transfers between devices: none -> 107 us  [swap(): lax.ppermute(x, axis, [(i, i ^ by) for i in range(lax.axis_size(axis))])]
    ppermute x0 -> x49, starting transfers between devices: none -> 79.2 us  [swap(): lax.ppermute(x, axis, [(i, i ^ by) for i in range(lax.axis_size(axis))])]
    psum x1 -> x0, waiting for transfers between devices: 62.3 us -> none  [local(): sums = lax.psum(tuple(sums), 'seq')]
    pallas_call x11 -> x19, Pallas kernels: 106 us -> 127 us  [the longest x1 39.6 us: middle_part(): pl.pallas_call(functools.partial(middle_kernel, held=held, head_dim=head_...]
    all_gather x1 -> x0, blocking collectives: 19.6 us -> none  [gather(): return lax.all_gather(x, 'fsdp', axis=0, tiled=True)]
    slice x17 -> x7, local copies, waits for them, and re-layouts: 26.6 us -> 8.55 us  [the longest x1 1.72 us: local(): query_grad = last[:, :q_cols]]
  transfers between devices with their start and end apart: 12 -> 52, of which waited for: 11 -> 20; matrix products, arithmetic and copies ran while one was open for 9% -> 3% of each run, Pallas kernels for 13% -> 23%
where the time goes in v2:
time: 420 us; the launch traced here: 413 us
  Pallas kernels  161 us (38%)
  waiting for transfers between devices  111 us (26%)
  starting transfers between devices  79.3 us (19%)
  between operations  25.4 us (6%)
  local copies, waits for them, and re-layouts  25.2 us (6%)
  other arithmetic  11.4 us (3%)
    ppermute x49, waiting for transfers between devices, swap(): lax.ppermute(x, axis, [(i, i ^ by) for i in range(lax.axis_size(axis))])  107 us
    ppermute x49, starting transfers between devices, swap(): lax.ppermute(x, axis, [(i, i ^ by) for i in range(lax.axis_size(axis))])  79.2 us
    pallas_call x1, Pallas kernels, middle_part(): pl.pallas_call(functools.partial(middle_kernel, held=held, head_dim=head_...  39.6 us
    pallas_call x2, Pallas kernels, attend_back(): pl.pallas_call(functools.partial(attend_back_kernel, head_dim=head_dim, t...  18.2 us
    pallas_call x7, Pallas kernels, add(): pl.pallas_call(skipping(functools.partial(add_kernel, count=count, groups...  15.7 us
    pallas_call x2, Pallas kernels, attend(): pl.pallas_call(functools.partial(attend_kernel, head_dim=head_dim, tile=t...  15.6 us
    pallas_call x1, Pallas kernels, column_grads(): pl.pallas_call(functools.partial(column_grads_kernel, piece=piece), grid_...  13.5 us
    pallas_call x1, Pallas kernels, weight_grad(): pl.pallas_call(skipping(weight_grad_kernel, 2, len(later)), grid=(cols //...  11.9 us
  transfers between devices with their start and end apart: 52, of which 20 were waited for; matrix products, arithmetic and copies ran while one was open for 3% of the time, Pallas kernels for 23%

profile of v2, /device:TPU:0, one launch (start us, length us, event | category | flops | bytes accessed | tf_op | source)
XLA Modules:
  0.0 413.0 jit_solution(12320969402328201886)
XLA Ops:
  10.6 5.1 %collective-permute-start.5 = (bf16[80,640]{1,0:T(8,128)(2,1)S(1)}, bf16[80,640]{1,0:T(8,128)(2,1)S(1)}, u32[]{:S(2)}, u32[]{:S(2)}) collective-permute-start(bf16[80,640]{1,0:T(8,128)(2,1)S(1)} %fusion.4.refs_4_), channel_id=1, source_target_pairs={{0,6},{1,7},{2,4},{3,5},{4,2},{5,3},{6,0},{7,1},{8,14},{9,15},{10,... | collective-permute-start | bytes 307208 | tf_op jit(solution)/shard_map/ppermute | solution.py:55
  39.4 5.8 %project_kv.1 = (bf16[1024,640]{1,0:T(8,128)(2,1)}, bf16[1024,512]{1,0:T(8,128)(2,1)}, bf16[640,640]{1,0:T(8,128)(2,1)}, f32[8,640]{1,0:T(8,128)}) custom-call(s32[2]{0:T(128)} %pad_add_fusion.refs_0_.where, bf16[1024,640]{1,0:T(8,128)(2,1)} %bitcast.44, f32[1024,128]{1,0:T(8,128)} %get-tuple-element.207.refs_2_.refs_7_, ...), custom_call_target="tpu_custom_call" | custom-call | flops 671088640 | bytes 6000000 | tf_op jit(solution)/shard_map/project_kv/pallas_call | solution.py:208
  50.8 5.5 %collective-permute-done.10.refs_8_ = bf16[80,1792]{1,0:T(8,128)(2,1)S(1)} collective-permute-done((bf16[80,1792]{1,0:T(8,128)(2,1)S(1)}, bf16[80,1792]{1,0:T(8,128)(2,1)S(1)}, u32[]{:S(2)}, u32[]{:S(2)}) %collective-permute-start.10) | collective-permute-done | bytes 286752 | tf_op jit(solution)/shard_map/ppermute | solution.py:55
  72.5 8.3 %project_q.1 = (bf16[1024,256]{1,0:T(8,128)(2,1)}, bf16[1024,1024]{1,0:T(8,128)(2,1)}, bf16[640,1792]{1,0:T(8,128)(2,1)}, bf16[256,1024]{1,0:T(8,128)(2,1)}) custom-call(s32[2]{0:T(128)} %pad_add_fusion.refs_0_.where, bf16[1024,640]{1,0:T(8,128)(2,1)} %get-tuple-element.80.refs_1_.normed_ref, f32[1024,128]{1,0:T(8,128)} %get-tuple-element.207.refs_2_.refs_7_, ...), custom_call_target="tpu_custom_call" | custom-call | flops 2214592512 | bytes 8000000 | tf_op jit(solution)/shard_map/project_q/pallas_call | solution.py:258
  83.1 7.7 %attend.2 = (bf16[1024,1024]{1,0:T(8,128)(2,1)}, f32[4,512]{1,0:T(4,128)}, bf16[2048,512]{1,0:T(8,128)(2,1)}) custom-call(s32[5]{0:T(128)} %stack.59.refs_0_, s32[1,512]{1,0:T(1,128)} %compare_select_fusion.refs_1_, bf16[1024,1024]{1,0:T(8,128)(2,1)} %get-tuple-element.81.refs_2_.refs_4_, bf16[512,512]{1,0:T(8,128)(2,1)} %copy-done.12, ...), custom_call_target="tpu_custom_call" | custom-call | flops 4294967296 | bytes 6000000 | tf_op jit(solution)/shard_map/attend/pallas_call | solution.py:342
  90.8 12.1 %collective-permute-done.16.refs_6_ = bf16[512,512]{1,0:T(8,128)(2,1)S(1)} collective-permute-done((bf16[512,512]{1,0:T(8,128)(2,1)S(1)}, bf16[512,512]{1,0:T(8,128)(2,1)S(1)}, u32[]{:S(2)}, u32[]{:S(2)}) %collective-permute-start.16) | collective-permute-done | bytes 524320 | tf_op jit(solution)/shard_map/ppermute | solution.py:55
  107.3 13.1 %collective-permute-done.14.refs_4_ = bf16[512,512]{1,0:T(8,128)(2,1)} collective-permute-done((bf16[512,512]{1,0:T(8,128)(2,1)S(1)}, bf16[512,512]{1,0:T(8,128)(2,1)}, u32[]{:S(2)}, u32[]{:S(2)}) %collective-permute-start.14) | collective-permute-done | bytes 524320 | tf_op jit(solution)/shard_map/ppermute | solution.py:55
  120.4 7.9 %attend.3 = (bf16[1024,1024]{1,0:T(8,128)(2,1)}, f32[4,512]{1,0:T(4,128)}, bf16[2048,512]{1,0:T(8,128)(2,1)}) custom-call(s32[5]{0:T(128)} %stack.51.refs_0_, s32[1,512]{1,0:T(1,128)} %compare_select_fusion.1.refs_1_, bf16[1024,1024]{1,0:T(8,128)(2,1)} %get-tuple-element.81.refs_2_.refs_4_, ...), custom_call_target="tpu_custom_call", output_to_operand_aliasing={{0}: (7, {})} | custom-call | flops 4294967296 | bytes 6000000 | tf_op jit(solution)/shard_map/attend/pallas_call | solution.py:342
  132.4 39.6 %middle.1 = (bf16[1024,640]{1,0:T(8,128)(2,1)}, f32[1024,640]{1,0:T(8,128)}, bf16[1024,640]{1,0:T(8,128)(2,1)}, bf16[1024,1024]{1,0:T(8,128)(2,1)}, f32[4,1024]{...) custom-call(bf16[1024,640]{1,0:T(8,128)(2,1)} %bitcast.45, ...), custom_call_target="tpu_custom_call" | custom-call | flops 18790481920 | bytes 40000000 | tf_op jit(solution)/shard_map/middle/pallas_call | solution.py:436
  172.0 13.5 %column_grads.1 = (bf16[4,4,80,768]{3,2,1,0:T(8,128)(2,1)}, bf16[4,4,80,768]{3,2,1,0:T(8,128)(2,1)}) custom-call(s32[2]{0:T(128)} %pad_add_fusion.refs_0_.where, bf16[1024,640]{1,0:T(8,128)(2,1)} %bitcast.57, bf16[1024,640]{1,0:T(8,128)(2,1)} %get-tuple-element.94.b_ref, bf16[1024,2048]{1,0:T(8,128)(2,1)} %get-tuple-element.95.hidden_ref, ...), custom_call_target="tpu_custom_call" | custom-call | flops 4026531840 | bytes 16000000 | tf_op jit(solution)/shard_map/column_grads/pallas_call | solution.py:692
  185.6 11.9 %weight_grad.1.refs_2_.refs_13_ = bf16[640,4096]{1,0:T(8,128)(2,1)} custom-call(bf16[1024,640]{1,0:T(8,128)(2,1)} %get-tuple-element.98.refs_0_, bf16[1024,4096]{1,0:T(8,128)(2,1)} %get-tuple-element.99.refs_1_, bf16[4,4,80,768]{3,2,1,0:T(8,128)(2,1)} %get-tuple-element.96.refs_2_.refs_0_), custom_call_target="tpu_custom_call" | custom-call | flops 5368709120 | bytes 14942208 | tf_op jit(solution)/shard_map/weight_grad/pallas_call | solution.py:635
  208.0 6.5 %collective-permute-start.22 = (bf16[4,80,768]{2,1,0:T(8,128)(2,1)}, bf16[4,80,768]{2,1,0:T(8,128)(2,1)S(1)}, u32[]{:S(2)}, u32[]{:S(2)}) collective-permute-start(bf16[4,80,768]{2,1,0:T(8,128)(2,1)} %get-tuple-element.102.refs_11_), channel_id=1, source_target_pairs={{0,16},{8,24},{16,0},{24,8},{1,17},{9,25},{17,1},{25,9},{2,18},{10... | collective-permute-start | bytes 1474568 | tf_op jit(solution)/shard_map/ppermute | solution.py:55
  214.5 9.1 %attend_back.2 = (bf16[1024,1024]{1,0:T(8,128)(2,1)}, f32[512,512]{1,0:T(8,128)}, bf16[512,512]{1,0:T(8,128)(2,1)}, bf16[512,512]{1,0:T(8,128)(2,1)}, bf16[512,512]{1,0:T(8,128)(2,1)}) custom-call(s32[5]{0:T(128)} %stack.59.refs_0_, s32[1,512]{1,0:T(1,128)} %compare_select_fusion.refs_1_, f32[4,512]{1,0:T(4,128)} %get-tuple-element.92.refs_2_, ...), custom_call_target="tpu_custom_call" | custom-call | flops 10737418240 | bytes 12000000 | tf_op jit(solution)/shard_map/attend_back/pallas_call | solution.py:525
  223.7 12.8 %collective-permute-done.22.refs_2_ = bf16[4,80,768]{2,1,0:T(8,128)(2,1)S(1)} collective-permute-done((bf16[4,80,768]{2,1,0:T(8,128)(2,1)}, bf16[4,80,768]{2,1,0:T(8,128)(2,1)S(1)}, u32[]{:S(2)}, u32[]{:S(2)}) %collective-permute-start.22) | collective-permute-done | bytes 491552 | tf_op jit(solution)/shard_map/ppermute | solution.py:55
  239.8 5.1 %collective-permute-start.27 = (bf16[80,768]{1,0:T(8,128)(2,1)}, bf16[80,768]{1,0:T(8,128)(2,1)S(1)}, u32[]{:S(2)}, u32[]{:S(2)}) collective-permute-start(bf16[80,768]{1,0:T(8,128)(2,1)} %get-tuple-element.106.refs_11_), channel_id=1, source_target_pairs={{0,2},{1,3},{2,0},{3,1},{4,6},{5,7},{6,4},{7,5},{8,10},{9,11},{10,... | collective-permute-start | bytes 368648 | tf_op jit(solution)/shard_map/ppermute | solution.py:55
  254.9 9.1 %attend_back.3 = (bf16[1024,1024]{1,0:T(8,128)(2,1)}, f32[512,512]{1,0:T(8,128)}, bf16[512,512]{1,0:T(8,128)(2,1)}, bf16[512,512]{1,0:T(8,128)(2,1)}, bf16[512,512]{1,0:T(8,128)(2,1)}) custom-call(s32[5]{0:T(128)} %stack.51.refs_0_, s32[1,512]{1,0:T(1,128)} %compare_select_fusion.1.refs_1_, ...), custom_call_target="tpu_custom_call", output_to_operand_aliasing={{0}: (9, {})} | custom-call | flops 10737418240 | bytes 12000000 | tf_op jit(solution)/shard_map/attend_back/pallas_call | solution.py:525
  270.8 7.7 %query_back.1 = (bf16[1024,256]{1,0:T(8,128)(2,1)}, f32[1024,640]{1,0:T(8,128)}) custom-call(bf16[1024,1024]{1,0:T(8,128)(2,1)} %get-tuple-element.109.refs_4_.refs_0_.dq_ref, bf16[640,1792]{1,0:T(8,128)(2,1)} %get-tuple-element.110.refs_1_, bf16[256,1024]{1,0:T(8,128)(2,1)} %get-tuple-element.111.refs_2_, bf16[512,512]{1,0:T(8,128)(2,1)} %copy-done.5, ...), custom_call_target="tpu_custom_call" | custom-call | flops 2214592512 | bytes 9000000 | tf_op jit(solution)/shard_map/query_back/pallas_call | solution.py:555
  278.5 6.0 %query_grads.1.refs_11_ = bf16[640,1792]{1,0:T(8,128)(2,1)} custom-call(bf16[1024,640]{1,0:T(8,128)(2,1)} %get-tuple-element.80.refs_1_.normed_ref, bf16[1024,256]{1,0:T(8,128)(2,1)} %get-tuple-element.122.lora_ref, bf16[1024,1024]{1,0:T(8,128)(2,1)} %get-tuple-element.109.refs_4_.refs_0_.dq_ref, bf16[1024,256]{1,0:T(8,128)(2,1)} %get-tuple-element.123.lora_grad_ref.refs_2_), custom_call_target="tpu_custom_call" | custom-call | flops 2214592512 | bytes 10000000 | tf_op jit(solution)/shard_map/query_grads/pallas_call | solution.py:734
  287.3 8.1 %collective-permute-start.31 = (bf16[512,512]{1,0:T(8,128)(2,1)S(1)}, bf16[512,512]{1,0:T(8,128)(2,1)S(1)}, u32[]{:S(2)}, u32[]{:S(2)}) collective-permute-start(bf16[512,512]{1,0:T(8,128)(2,1)S(1)} %copy-done.54), channel_id=1, source_target_pairs={{0,16},{8,24},{16,0},{24,8},{1,17},{9,25},{17,1},{25,9},{2,18},{10... | collective-permute-start | bytes 1572872 | tf_op jit(solution)/shard_map/ppermute | solution.py:55
  300.9 12.1 %collective-permute-done.33.refs_1_ = bf16[80,1024]{1,0:T(8,128)(2,1)S(1)} collective-permute-done((bf16[80,1024]{1,0:T(8,128)(2,1)}, bf16[80,1024]{1,0:T(8,128)(2,1)S(1)}, u32[]{:S(2)}, u32[]{:S(2)}) %collective-permute-start.33) | collective-permute-done | bytes 163872 | tf_op jit(solution)/shard_map/ppermute | solution.py:55
  313.0 9.6 %collective-permute-start.35 = (bf16[80,1024]{1,0:T(8,128)(2,1)}, bf16[80,1024]{1,0:T(8,128)(2,1)S(1)}, u32[]{:S(2)}, u32[]{:S(2)}) collective-permute-start(bf16[80,1024]{1,0:T(8,128)(2,1)} %get-tuple-element.128), channel_id=1, source_target_pairs={{0,24},{8,16},{16,8},{24,0},{1,25},{9,17},{17,9},{25,1},{2,26},{10... | collective-permute-start | bytes 491528 | tf_op jit(solution)/shard_map/ppermute | solution.py:55
  331.2 4.8 %pair_back.3 = (bf16[512,512]{1,0:T(8,128)(2,1)}, f32[1024,640]{1,0:T(8,128)}, f32[1,640]{1,0:T(1,128)}) custom-call(bf16[1024,640]{1,0:T(8,128)(2,1)} %bitcast.47, f32[8,640]{1,0:T(8,128)} %get-tuple-element.85.refs_3_.refs_1_, f32[1024,128]{1,0:T(8,128)} %get-tuple-element.207.refs_2_.refs_7_, ...), custom_call_target="tpu_custom_call", output_to_operand_aliasing={{1}: (11, {})} | custom-call | flops 335544320 | bytes 7000000 | tf_op jit(solution)/shard_map/pair_back/pallas_call | solution.py:608
  350.5 5.7 %collective-permute-done.38.refs_2_ = bf16[80,640]{1,0:T(8,128)(2,1)S(1)} collective-permute-done((bf16[80,640]{1,0:T(8,128)(2,1)}, bf16[80,640]{1,0:T(8,128)(2,1)S(1)}, u32[]{:S(2)}, u32[]{:S(2)}) %collective-permute-start.38) | collective-permute-done | bytes 102432 | tf_op jit(solution)/shard_map/ppermute | solution.py:55
  364.9 17.8 %collective-permute-done.46.refs_6_ = bf16[80,768]{1,0:T(8,128)(2,1)S(1)} collective-permute-done((bf16[80,768]{1,0:T(8,128)(2,1)S(1)}, bf16[80,768]{1,0:T(8,128)(2,1)S(1)}, u32[]{:S(2)}, u32[]{:S(2)}) %collective-permute-start.46) | collective-permute-done | bytes 122912 | tf_op jit(solution)/shard_map/ppermute | solution.py:55
  (283 shorter events, 142.5 us)
Async XLA Ops:
  7.3 125.2 %all-gather.2.cloned.1.call-start = ((), (), s32[]{:S(2)}) async-start(), calls=%async_computation.2 | async-start | bytes 9461760 | tf_op jit(solution)/shard_map/all_gather | solution.py:137
  10.4 285.1 %reduce-scatter.3.cloned.1.call-start = ((), (), s32[]{:S(2)}) async-start(), calls=%async_computation.3 | async-start | bytes 5898240 | tf_op jit(solution)/shard_map/reduce_scatter | solution.py:971
  16.4 28.8 %collective-permute-start.12 = (bf16[80,1792]{1,0:T(8,128)(2,1)S(1)}, bf16[80,1792]{1,0:T(8,128)(2,1)S(1)}, u32[]{:S(2)}, u32[]{:S(2)}) collective-permute-start(bf16[80,1792]{1,0:T(8,128)(2,1)S(1)} %pad_maximum_fusion.1.refs_4_), channel_id=1, source_target_pairs={{0,6},{1,7},{2,4},{3,5},{4,2},{5,3},{6,0},{7,1},{8,14},{9,15},{10,... | collective-permute-start | bytes 860168 | tf_op jit(solution)/shard_map/ppermute | solution.py:55
  36.3 21.6 %collective-permute-start.8 = (bf16[80,1792]{1,0:T(8,128)(2,1)S(1)}, bf16[80,1792]{1,0:T(8,128)(2,1)}, u32[]{:S(2)}, u32[]{:S(2)}) collective-permute-start(bf16[80,1792]{1,0:T(8,128)(2,1)S(1)} %pad_maximum_fusion.1.refs_4_), channel_id=1, source_target_pairs={{0,2},{1,3},{2,0},{3,1},{4,6},{5,7},{6,4},{7,5},{8,10},{9,11},{10,... | collective-permute-start | bytes 860168 | tf_op jit(solution)/shard_map/ppermute | solution.py:55
  47.1 23.9 %collective-permute-start.19 = (bf16[512,512]{1,0:T(8,128)(2,1)S(1)}, bf16[512,512]{1,0:T(8,128)(2,1)S(1)}, u32[]{:S(2)}, u32[]{:S(2)}) collective-permute-start(bf16[512,512]{1,0:T(8,128)(2,1)S(1)} %get-tuple-element.200.refs_3_), channel_id=1, source_target_pairs={{0,24},{8,16},{16,8},{24,0},{1,25},{9,17},{17,9},{25,1},{2,26},{10... | collective-permute-start | bytes 1572872 | tf_op jit(solution)/shard_map/ppermute | solution.py:55
  56.3 24.6 %collective-permute-start.18 = (bf16[512,512]{1,0:T(8,128)(2,1)S(1)}, bf16[512,512]{1,0:T(8,128)(2,1)S(1)}, u32[]{:S(2)}, u32[]{:S(2)}) collective-permute-start(bf16[512,512]{1,0:T(8,128)(2,1)S(1)} %get-tuple-element.200.refs_3_), channel_id=1, source_target_pairs={{0,16},{8,24},{16,0},{24,8},{1,17},{9,25},{17,1},{25,9},{2,18},{10... | collective-permute-start | bytes 1572872 | tf_op jit(solution)/shard_map/ppermute | solution.py:55
  57.9 24.5 %collective-permute-start.17 = (bf16[512,512]{1,0:T(8,128)(2,1)S(1)}, bf16[512,512]{1,0:T(8,128)(2,1)S(1)}, u32[]{:S(2)}, u32[]{:S(2)}) collective-permute-start(bf16[512,512]{1,0:T(8,128)(2,1)S(1)} %get-tuple-element.200.refs_3_), channel_id=1, source_target_pairs={{0,8},{8,0},{16,24},{24,16},{1,9},{9,1},{17,25},{25,17},{2,10},{10... | collective-permute-start | bytes 1572872 | tf_op jit(solution)/shard_map/ppermute | solution.py:55
  68.4 34.5 %collective-permute-start.16 = (bf16[512,512]{1,0:T(8,128)(2,1)S(1)}, bf16[512,512]{1,0:T(8,128)(2,1)S(1)}, u32[]{:S(2)}, u32[]{:S(2)}) collective-permute-start(bf16[512,512]{1,0:T(8,128)(2,1)S(1)} %get-tuple-element.201.refs_3_), channel_id=1, source_target_pairs={{0,24},{8,16},{16,8},{24,0},{1,25},{9,17},{17,9},{25,1},{2,26},{10... | collective-permute-start | bytes 1572872 | tf_op jit(solution)/shard_map/ppermute | solution.py:55
  68.7 38.6 %collective-permute-start.15 = (bf16[512,512]{1,0:T(8,128)(2,1)S(1)}, bf16[512,512]{1,0:T(8,128)(2,1)S(1)}, u32[]{:S(2)}, u32[]{:S(2)}) collective-permute-start(bf16[512,512]{1,0:T(8,128)(2,1)S(1)} %get-tuple-element.201.refs_3_), channel_id=1, source_target_pairs={{0,16},{8,24},{16,0},{24,8},{1,17},{9,25},{17,1},{25,9},{2,18},{10... | collective-permute-start | bytes 1572872 | tf_op jit(solution)/shard_map/ppermute | solution.py:55
  71.0 49.3 %collective-permute-start.14 = (bf16[512,512]{1,0:T(8,128)(2,1)S(1)}, bf16[512,512]{1,0:T(8,128)(2,1)}, u32[]{:S(2)}, u32[]{:S(2)}) collective-permute-start(bf16[512,512]{1,0:T(8,128)(2,1)S(1)} %get-tuple-element.201.refs_3_), channel_id=1, source_target_pairs={{0,8},{8,0},{16,24},{24,16},{1,9},{9,1},{17,25},{25,17},{2,10},{10... | collective-permute-start | bytes 1572872 | tf_op jit(solution)/shard_map/ppermute | solution.py:55
  197.5 161.1 %reduce-scatter.5.cloned.1.call-start = ((), (), s32[]{:S(2)}) async-start(), calls=%async_computation.4 | async-start | bytes 2580480 | tf_op jit(solution)/shard_map/reduce_scatter | solution.py:992
  208.0 28.5 %collective-permute-start.22 = (bf16[4,80,768]{2,1,0:T(8,128)(2,1)}, bf16[4,80,768]{2,1,0:T(8,128)(2,1)S(1)}, u32[]{:S(2)}, u32[]{:S(2)}) collective-permute-start(bf16[4,80,768]{2,1,0:T(8,128)(2,1)} %get-tuple-element.102.refs_11_), channel_id=1, source_target_pairs={{0,16},{8,24},{16,0},{24,8},{1,17},{9,25},{17,1},{25,9},{2,18},{10... | collective-permute-start | bytes 1474568 | tf_op jit(solution)/shard_map/ppermute | solution.py:55
  214.5 22.0 %collective-permute-start.23 = (bf16[4,80,768]{2,1,0:T(8,128)(2,1)}, bf16[4,80,768]{2,1,0:T(8,128)(2,1)S(1)}, u32[]{:S(2)}, u32[]{:S(2)}) collective-permute-start(bf16[4,80,768]{2,1,0:T(8,128)(2,1)} %get-tuple-element.103.refs_12_), channel_id=1, source_target_pairs={{0,24},{8,16},{16,8},{24,0},{1,25},{9,17},{17,9},{25,1},{2,26},{10... | collective-permute-start | bytes 1474568 | tf_op jit(solution)/shard_map/ppermute | solution.py:55
  244.9 23.5 %collective-permute-start.24 = (bf16[512,512]{1,0:T(8,128)(2,1)S(1)}, bf16[512,512]{1,0:T(8,128)(2,1)S(1)}, u32[]{:S(2)}, u32[]{:S(2)}) collective-permute-start(bf16[512,512]{1,0:T(8,128)(2,1)S(1)} %copy-done.58), channel_id=1, source_target_pairs={{0,8},{8,0},{16,24},{24,16},{1,9},{9,1},{17,25},{25,17},{2,10},{10... | collective-permute-start | bytes 1572872 | tf_op jit(solution)/shard_map/ppermute | solution.py:55
  246.2 22.2 %collective-permute-start.25 = (bf16[512,512]{1,0:T(8,128)(2,1)S(1)}, bf16[512,512]{1,0:T(8,128)(2,1)S(1)}, u32[]{:S(2)}, u32[]{:S(2)}) collective-permute-start(bf16[512,512]{1,0:T(8,128)(2,1)S(1)} %copy-done.57), channel_id=1, source_target_pairs={{0,16},{8,24},{16,0},{24,8},{1,17},{9,25},{17,1},{25,9},{2,18},{10... | collective-permute-start | bytes 1572872 | tf_op jit(solution)/shard_map/ppermute | solution.py:55
  246.9 23.1 %collective-permute-start.26 = (bf16[512,512]{1,0:T(8,128)(2,1)S(1)}, bf16[512,512]{1,0:T(8,128)(2,1)S(1)}, u32[]{:S(2)}, u32[]{:S(2)}) collective-permute-start(bf16[512,512]{1,0:T(8,128)(2,1)S(1)} %copy-done.56), channel_id=1, source_target_pairs={{0,24},{8,16},{16,8},{24,0},{1,25},{9,17},{17,9},{25,1},{2,26},{10... | collective-permute-start | bytes 1572872 | tf_op jit(solution)/shard_map/ppermute | solution.py:55
  285.6 44.4 %collective-permute-start.30 = (bf16[512,512]{1,0:T(8,128)(2,1)S(1)}, bf16[512,512]{1,0:T(8,128)(2,1)S(1)}, u32[]{:S(2)}, u32[]{:S(2)}) collective-permute-start(bf16[512,512]{1,0:T(8,128)(2,1)S(1)} %copy-done.55), channel_id=1, source_target_pairs={{0,8},{8,0},{16,24},{24,16},{1,9},{9,1},{17,25},{25,17},{2,10},{10... | collective-permute-start | bytes 1572872 | tf_op jit(solution)/shard_map/ppermute | solution.py:55
  287.3 42.7 %collective-permute-start.31 = (bf16[512,512]{1,0:T(8,128)(2,1)S(1)}, bf16[512,512]{1,0:T(8,128)(2,1)S(1)}, u32[]{:S(2)}, u32[]{:S(2)}) collective-permute-start(bf16[512,512]{1,0:T(8,128)(2,1)S(1)} %copy-done.54), channel_id=1, source_target_pairs={{0,16},{8,24},{16,0},{24,8},{1,17},{9,25},{17,1},{25,9},{2,18},{10... | collective-permute-start | bytes 1572872 | tf_op jit(solution)/shard_map/ppermute | solution.py:55
  295.4 34.6 %collective-permute-start.32 = (bf16[512,512]{1,0:T(8,128)(2,1)S(1)}, bf16[512,512]{1,0:T(8,128)(2,1)S(1)}, u32[]{:S(2)}, u32[]{:S(2)}) collective-permute-start(bf16[512,512]{1,0:T(8,128)(2,1)S(1)} %copy-done.53), channel_id=1, source_target_pairs={{0,24},{8,16},{16,8},{24,0},{1,25},{9,17},{17,9},{25,1},{2,26},{10... | collective-permute-start | bytes 1572872 | tf_op jit(solution)/shard_map/ppermute | solution.py:55
  298.9 28.4 %collective-permute-start.34 = (bf16[80,1024]{1,0:T(8,128)(2,1)}, bf16[80,1024]{1,0:T(8,128)(2,1)S(1)}, u32[]{:S(2)}, u32[]{:S(2)}) collective-permute-start(bf16[80,1024]{1,0:T(8,128)(2,1)} %get-tuple-element.127), channel_id=1, source_target_pairs={{0,16},{8,24},{16,0},{24,8},{1,17},{9,25},{17,1},{25,9},{2,18},{10... | collective-permute-start | bytes 491528 | tf_op jit(solution)/shard_map/ppermute | solution.py:55
  359.6 34.4 %collective-permute-start.42 = (bf16[80,2432]{1,0:T(8,128)(2,1)S(1)}, bf16[80,2432]{1,0:T(8,128)(2,1)S(1)}, u32[]{:S(2)}, u32[]{:S(2)}) collective-permute-start(bf16[80,2432]{1,0:T(8,128)(2,1)S(1)} %pad_maximum_fusion.refs_0_), channel_id=1, source_target_pairs={{0,24},{8,16},{16,8},{24,0},{1,25},{9,17},{17,9},{25,1},{2,26},{10... | collective-permute-start | bytes 1167368 | tf_op jit(solution)/shard_map/ppermute | solution.py:55
  361.3 32.8 %collective-permute-start.41 = (bf16[80,2432]{1,0:T(8,128)(2,1)S(1)}, bf16[80,2432]{1,0:T(8,128)(2,1)S(1)}, u32[]{:S(2)}, u32[]{:S(2)}) collective-permute-start(bf16[80,2432]{1,0:T(8,128)(2,1)S(1)} %pad_maximum_fusion.refs_0_), channel_id=1, source_target_pairs={{0,16},{8,24},{16,0},{24,8},{1,17},{9,25},{17,1},{25,9},{2,18},{10... | collective-permute-start | bytes 1167368 | tf_op jit(solution)/shard_map/ppermute | solution.py:55
  361.3 32.8 %collective-permute-start.40 = (bf16[80,2432]{1,0:T(8,128)(2,1)S(1)}, bf16[80,2432]{1,0:T(8,128)(2,1)S(1)}, u32[]{:S(2)}, u32[]{:S(2)}) collective-permute-start(bf16[80,2432]{1,0:T(8,128)(2,1)S(1)} %pad_maximum_fusion.refs_0_), channel_id=1, source_target_pairs={{0,8},{8,0},{16,24},{24,16},{1,9},{9,1},{17,25},{25,17},{2,10},{10... | collective-permute-start | bytes 1167368 | tf_op jit(solution)/shard_map/ppermute | solution.py:55
  363.2 21.9 %collective-permute-start.45 = (bf16[80,1024]{1,0:T(8,128)(2,1)S(1)}, bf16[80,1024]{1,0:T(8,128)(2,1)S(1)}, u32[]{:S(2)}, u32[]{:S(2)}) collective-permute-start(bf16[80,1024]{1,0:T(8,128)(2,1)S(1)} %copy-done.4), channel_id=1, source_target_pairs={{0,24},{8,16},{16,8},{24,0},{1,25},{9,17},{17,9},{25,1},{2,26},{10... | collective-permute-start | bytes 491528 | tf_op jit(solution)/shard_map/ppermute | solution.py:55
  (95 other events, 927.2 us)
Sparse Core Ops, SparseCore 0:
  10.9 121.4 all-gather.1
  197.6 75.9 reduce-scatter.2
  284.7 42.8 reduce-scatter.4

commit v3 on v2

v3 whole, which is shorter than its diff:
```python
import functools
import math

import jax
import jax.numpy as jnp
from jax import lax
from jax.experimental import pallas as pl
from jax.experimental.pallas import tpu as pltpu
from jax.sharding import PartitionSpec as P

EPSILON = 1e-06
THETA = 10000.0
F32 = jnp.float32
BF16 = jnp.bfloat16
GELU_C = math.sqrt(2.0 / math.pi)
GELU_A = 0.044715
LOWEST = -1e30
VMEM_LIMIT = 60 * 1024 * 1024
ANY = pl.BlockSpec(memory_space=pl.ANY)
VMEM = pl.BlockSpec(memory_space=pltpu.VMEM)
SMEM = pl.BlockSpec(memory_space=pltpu.SMEM)


def mm(left, right):
    return lax.dot_general(left, right, (((1,), (0,)), ((), ())), preferred_element_type=F32)


def mm_nt(left, right):
    return lax.dot_general(left, right, (((1,), (1,)), ((), ())), preferred_element_type=F32)


def full(shape):
    return pl.BlockSpec(shape, lambda i: (0,) * len(shape))


def rows_of(tile, cols):
    return pl.BlockSpec((tile, cols), lambda i: (i, 0))


def params(**more):
    return pltpu.CompilerParams(vmem_limit_bytes=VMEM_LIMIT, **more)


def cost(flops, bytes_accessed, transcendentals=0):
    return pl.CostEstimate(
        flops=int(flops), bytes_accessed=int(bytes_accessed), transcendentals=int(transcendentals)
    )


def took(us):
    return cost(us * 1.1e9, 1)


LONG = 10**12


def like(shape, dtype):
    return jax.ShapeDtypeStruct(tuple(shape), dtype)


def swap(x, axis, by):
    return lax.ppermute(x, axis, [(i, i ^ by) for i in range(lax.axis_size(axis))])


def skipping(kernel, first, count):
    return lambda *refs: kernel(*refs[:first], *refs[first + count :])


def tree(values):
    while len(values) > 1:
        values = [values[i] + values[i + 1] for i in range(0, len(values), 2)]
    return values[0]


def add_kernel(*refs, count, groups):
    for out, group in zip(refs[count:], groups):
        values = [refs[i][...] if k is None else refs[i][k] for i, k in group]
        out[...] = tree([v.astype(F32) for v in values]).astype(out.dtype)


def add(arrays, groups, later=(), dtype=BF16):
    shapes = [arrays[g[0][0]].shape if g[0][1] is None else arrays[g[0][0]].shape[1:]
              for g in groups]
    count = len(arrays)
    later = list(later)
    return list(pl.pallas_call(
        skipping(functools.partial(add_kernel, count=count, groups=groups), count, len(later)),
        in_specs=[VMEM] * count + [ANY] * len(later),
        out_specs=[VMEM] * len(groups),
        out_shape=[like(s, dtype) for s in shapes],
        compiler_params=params(),
        cost_estimate=took(3.5),
        name="add",
    )(*arrays, *later))


class Whole:
    def __init__(self, array):
        self.arrays = [array]
        self.shape = array.shape
        self.count = 1

    def copies(self, where, refs, dst):
        return [(refs[0], dst)]


class Shards:
    def __init__(self, x, relay=False):
        parts = lax.axis_size("fsdp")
        got = {0: x}
        for r in range(2, parts, 2):
            low = r & -r
            near = relay and r != low
            got[r] = swap(got[r - low], "fsdp", low) if near else swap(x, "fsdp", r)
        for r in range(0, parts, 2):
            got[r + 1] = swap(got[r], "fsdp", 1)
        self.arrays = [got[r] for r in range(parts)]
        self.rows = x.shape[0]
        self.shape = (parts * x.shape[0], x.shape[1])
        self.count = parts

    def copies(self, where, refs, dst):
        out = []
        for r, ref in enumerate(refs):
            at = pl.multiple_of((where[0] ^ r) * self.rows, self.rows)
            out.append((ref, dst.at[pl.ds(at, self.rows), :]))
        return out


def pack_pair_kernel(kv_ref, one_ref, two_ref, out_ref):
    piece, kv_cols = kv_ref.shape
    out_ref[:, :kv_cols] = kv_ref[...]
    pad = jnp.zeros((126, piece), F32)
    gains = jnp.concatenate([one_ref[...].astype(F32), two_ref[...].astype(F32), pad], axis=0)
    out_ref[:, kv_cols:] = gains.T.astype(BF16)


def pack_pair(kv, one, two):
    piece = kv.shape[0]
    return pl.pallas_call(
        pack_pair_kernel,
        in_specs=[VMEM] * 3,
        out_specs=VMEM,
        out_shape=like((piece, kv.shape[1] + 128), BF16),
        compiler_params=params(),
        cost_estimate=took(1.6),
        name="pack_pair",
    )(kv, one.reshape(1, piece), two.reshape(1, piece))


def pack_kernel(where, gate_ref, up_ref, down_ref, out_ref, third_ref, *, span):
    piece = gate_ref.shape[0]
    hidden = gate_ref.shape[1]
    part = 2 * hidden // span
    for s in range(span):
        ref, at = (gate_ref, s * part) if s * part < hidden else (up_ref, s * part - hidden)

        @pl.when(where[1] == s)
        def _():
            third_ref[:, :part] = ref[:, at : at + part]

    col = part
    for ref in (down_ref, out_ref):
        n = ref.shape[0] // span
        for i in range(n // 16):
            row = pl.ds(pl.multiple_of(where[1] * n + 16 * i, 16), 16)
            for j in range(ref.shape[1] // 128):
                third_ref[16 * j : 16 * j + 16, col : col + 128] = ref[row, j * 128 : (j + 1) * 128]
            col += 128


def pack(where, gate, up, down, out, span, later):
    piece = gate.shape[0]
    third = (gate.shape[1] * 2 * piece + (down.shape[0] + out.shape[0]) * down.shape[1]) // span
    return pl.pallas_call(
        skipping(functools.partial(pack_kernel, span=span), 5, len(later)),
        in_specs=[SMEM] + [VMEM] * 4 + [ANY] * len(later),
        out_specs=VMEM,
        out_shape=like((piece, third // piece), BF16),
        compiler_params=params(),
        cost_estimate=took(2),
        name="pack",
    )(where, gate, up, down, out, *later)


def pack_query_kernel(q_ref, narrow_ref, widen_ref, out_ref, *, fold):
    q_cols, mid, count = q_ref.shape[1], narrow_ref.shape[1], widen_ref.shape[0]
    out_ref[:, :q_cols] = q_ref[...]
    out_ref[:, q_cols : q_cols + mid] = narrow_ref[...]
    folds = q_cols // fold
    for j in range(folds):
        out_ref[j * count : (j + 1) * count, q_cols + mid :] = widen_ref[
            :, j * fold : (j + 1) * fold]
    rest = out_ref.shape[0] - folds * count
    out_ref[folds * count :, q_cols + mid :] = jnp.zeros((rest, fold), BF16)


def pack_query(q, narrow, widen, fold, later):
    return pl.pallas_call(
        skipping(functools.partial(pack_query_kernel, fold=fold), 3, len(later)),
        in_specs=[VMEM] * 3 + [ANY] * len(later),
        out_specs=VMEM,
        out_shape=like((q.shape[0], q.shape[1] + narrow.shape[1] + fold), BF16),
        compiler_params=params(),
        cost_estimate=took(1.7),
        name="pack_query",
    )(q, narrow, widen, *later)


class Tiled:
    def __init__(self, packed, gate_up, *tall):
        parts, span = lax.axis_size("fsdp"), lax.axis_size("seq")
        piece = packed.shape[0]
        self.piece, self.part, self.parts, self.span = piece, gate_up // span, parts, span
        self.heights = [t.shape[0] // span for t in tall]
        self.up, self.across = sum(self.heights) // 16, tall[0].shape[1] // 128
        self.array = lax.all_gather(packed, ("seq", "fsdp"), axis=0, tiled=True)
        self.shape = (parts * piece, gate_up)
        self.shapes = [(parts * t.shape[0], t.shape[1]) for t in tall]
        self.scratch = (span, parts * piece, self.up * 128)

    def copies(self, ref, dst, rest):
        height = self.parts * self.piece
        rows = [pl.ds(s * height, height) for s in range(self.span)]
        return [(ref.at[at, pl.ds(self.part, self.up * 128)], rest.at[s])
                for s, at in enumerate(rows)] + [
            (ref.at[at, pl.ds(0, self.part)], dst.at[:, pl.ds(s * self.part, self.part)])
            for s, at in enumerate(rows)]

    def unfold(self, rest, dsts):
        starts, tops = [], 0
        for n in self.heights:
            starts.append(tops)
            tops += n // 16

        def shard(d, carry):
            for s in range(self.span):
                for n, first, dst in zip(self.heights, starts, dsts):
                    for i in range(n // 16):
                        at = pl.ds(pl.multiple_of(d * n * self.span + s * n + i * 16, 16), 16)
                        for j in range(self.across):
                            row = pl.ds(pl.multiple_of(d * self.piece + 16 * j, 16), 16)
                            col = (first + i) * 128
                            dst[at, j * 128 : (j + 1) * 128] = rest[s, row, col : col + 128]
            return carry

        lax.fori_loop(0, self.parts, shard, 0)


def carry_out(copies, sem):
    made = [pltpu.make_async_copy(src, dst, sem.at[i]) for i, (src, dst) in enumerate(copies)]
    for c in made:
        c.start()
    for c in made:
        c.wait()


def normalize(x_ref, gains_ref):
    x = x_ref[...].astype(F32)
    inv = lax.rsqrt(jnp.mean(x * x, axis=-1, keepdims=True) + EPSILON)
    return (x * inv * gains_ref[0:1, :]).astype(BF16)


def put_pair(kv_ref, pair, cos, sin, head_dim):
    half = head_dim // 2
    a, b = pair[:, :half], pair[:, half:head_dim]
    kv_ref[:, :half] = (a * cos - b * sin).astype(BF16)
    kv_ref[:, half:head_dim] = (b * cos + a * sin).astype(BF16)
    kv_ref[:, head_dim:] = pair[:, head_dim:].astype(BF16)


def project_kv_kernel(*refs, held, head_dim):
    where, x_ref, cos_ref, sin_ref = refs[:4]
    pieces = refs[4 : 4 + len(held.arrays)]
    normed_ref, kv_ref, w_ref, gains_ref, sem = refs[4 + len(held.arrays) :]
    kv_cols = 2 * head_dim

    @pl.when(pl.program_id(0) == 0)
    def _():
        carry_out(held.copies(where, pieces, w_ref), sem)
        gains_ref[...] = w_ref[:, kv_cols:].astype(F32).T[:8]

    normed = normalize(x_ref, gains_ref)
    normed_ref[...] = normed
    put_pair(kv_ref, mm(normed, w_ref[:, :kv_cols]), cos_ref[...], sin_ref[...], head_dim)


def project_kv(where, x, cos, sin, held, head_dim):
    rows, width = x.shape
    tile = math.gcd(rows, 512)
    half = head_dim // 2
    return pl.pallas_call(
        functools.partial(project_kv_kernel, held=held, head_dim=head_dim),
        grid=(rows // tile,),
        in_specs=[SMEM, rows_of(tile, width), rows_of(tile, half), rows_of(tile, half)]
        + [ANY] * len(held.arrays),
        out_specs=[rows_of(tile, width), rows_of(tile, 2 * head_dim), full(held.shape),
                   full((8, width))],
        out_shape=[like((rows, width), BF16), like((rows, 2 * head_dim), BF16),
                   like(held.shape, BF16), like((8, width), F32)],
        scratch_shapes=[pltpu.SemaphoreType.DMA((held.count,))],
        compiler_params=params(),
        cost_estimate=took(5),
        name="project_kv",
    )(where, x, cos, sin, *held.arrays)


def project_q_kernel(*refs, held, head_dim, q_cols, mid, scale):
    where, normed_ref, cos_ref, sin_ref = refs[:4]
    pieces = refs[4 : 4 + len(held.arrays)]
    lora_ref, q_ref, w_ref, ww_ref, sem = refs[4 + len(held.arrays) :]
    half = head_dim // 2
    fold = held.shape[1] - q_cols - mid
    parts = q_cols // fold

    @pl.when(pl.program_id(0) == 0)
    def _():
        carry_out(held.copies(where, pieces, w_ref), sem)
        shards = held.shape[0] // held.rows
        count = mid // shards
        for d in range(shards):
            for j in range(parts):
                ww_ref[d * count : (d + 1) * count, j * fold : (j + 1) * fold] = w_ref[
                    d * held.rows + j * count : d * held.rows + (j + 1) * count, q_cols + mid :]

    normed = normed_ref[...]
    cos, sin = cos_ref[...], sin_ref[...]
    low = mm(normed, w_ref[:, q_cols : q_cols + mid]).astype(BF16)
    lora_ref[...] = low
    query = mm(normed, w_ref[:, :q_cols]) + mm(low, ww_ref[...])
    for h in range(q_cols // head_dim):
        c = h * head_dim
        a, b = query[:, c : c + half], query[:, c + half : c + head_dim]
        q_ref[:, c : c + half] = ((a * cos - b * sin) * scale).astype(BF16)
        q_ref[:, c + half : c + head_dim] = ((b * cos + a * sin) * scale).astype(BF16)


def project_q(where, normed, cos, sin, held, head_dim, q_cols, mid, scale, later):
    rows, width = normed.shape
    tile = math.gcd(rows, 256)
    half = head_dim // 2
    count = 4 + len(held.arrays)
    return pl.pallas_call(
        skipping(functools.partial(project_q_kernel, held=held, head_dim=head_dim, q_cols=q_cols,
                                   mid=mid, scale=scale), count, len(later)),
        grid=(rows // tile,),
        in_specs=[SMEM, rows_of(tile, width), rows_of(tile, half), rows_of(tile, half)]
        + [ANY] * (len(held.arrays) + len(later)),
        out_specs=[rows_of(tile, mid), rows_of(tile, q_cols), full(held.shape),
                   full((mid, q_cols))],
        out_shape=[like((rows, mid), BF16), like((rows, q_cols), BF16), like(held.shape, BF16),
                   like((mid, q_cols), BF16)],
        scratch_shapes=[pltpu.SemaphoreType.DMA((held.count,))],
        compiler_params=params(),
        cost_estimate=took(8.5),
        name="project_q",
    )(where, normed, cos, sin, *held.arrays, *later)


def attend_kernel(*refs, head_dim, tile, block, span):
    where, lengths_ref, q_ref = refs[:3]
    kvs = refs[3 : 3 + span]
    o_ref, lse_ref, kv_ref, vt_ref, acc_ref, sem = refs[-6:]
    heads = q_ref.shape[1] // head_dim
    rows = q_ref.shape[0]
    m = pl.program_id(0)
    place = where[1]
    base = place * rows
    lengths = [lengths_ref[m, d] for d in range(lengths_ref.shape[1])]

    def first(t):
        return lax.div(begin_of(base + t * tile, lengths), block)

    def copy(n, s):
        at = pl.multiple_of((place ^ s) * rows, rows)
        return pltpu.make_async_copy(kvs[s].at[pl.ds(n * rows, rows)],
                                     kv_ref.at[n, pl.ds(at, rows), :], sem.at[n, s])

    @pl.when(m == 0)
    def _():
        for n in range(kv_ref.shape[0]):
            for s in range(span):
                pl.when((place ^ s) <= place)(lambda n=n, s=s: copy(n, s).start())

    for n in range(kv_ref.shape[0]):
        for s in range(span):
            pl.when((m == n) & ((place ^ s) <= place))(lambda n=n, s=s: copy(n, s).wait())

    def flip(kb, carry):
        at = pl.ds(pl.multiple_of(kb * block, block), block)
        vt_ref[:, at] = kv_ref[m, at, head_dim:].T
        return carry

    lax.fori_loop(first(0), lax.div(base + rows + block - 1, block), flip, 0)
    for t in range(rows // tile):
        q_rows = slice(t * tile, (t + 1) * tile)
        high = base + t * tile + lax.broadcasted_iota(jnp.int32, (1, tile), 1)
        low = begin_of(high, lengths)
        acc_ref[...] = jnp.zeros_like(acc_ref)

        def visit(kb, carry):
            at = pl.ds(pl.multiple_of(kb * block, block), block)
            keys = kv_ref[m, at, :head_dim]
            vt = vt_ref[:, at]
            index = kb * block + lax.broadcasted_iota(jnp.int32, (block, tile), 0)
            mask = (index >= low) & (index <= high)
            out = []
            for h in range(heads):
                peak, total = carry[h]
                s = mm_nt(keys, q_ref[q_rows, h * head_dim : (h + 1) * head_dim])
                s = jnp.where(mask, s, -jnp.inf)
                new_peak = jnp.maximum(peak, jnp.max(s, axis=0, keepdims=True))
                factor = jnp.exp(peak - new_peak)
                p = jnp.exp(s - new_peak)
                total = total * factor + jnp.sum(p, axis=0, keepdims=True)
                acc_ref[h] = acc_ref[h] * factor + mm(vt, p.astype(BF16))
                out.append((new_peak, total))
            return tuple(out)

        start = tuple(
            (jnp.full((1, tile), LOWEST, F32), jnp.zeros((1, tile), F32)) for _ in range(heads)
        )
        stats = lax.fori_loop(first(t), lax.div(base + (t + 1) * tile + block - 1, block), visit,
                              start)
        for h in range(heads):
            peak, total = stats[h]
            o_ref[q_rows, h * head_dim : (h + 1) * head_dim] = (acc_ref[h] / total).T.astype(BF16)
            lse_ref[0, h : h + 1, q_rows] = peak + jnp.log(total)


def attend(where, lengths, q, kvs, head_dim, tile, block):
    total, q_cols = q.shape
    batches = lengths.shape[0]
    rows = total // batches
    heads = q_cols // head_dim
    span = len(kvs)
    group = span * rows
    return pl.pallas_call(
        functools.partial(attend_kernel, head_dim=head_dim, tile=tile, block=block, span=span),
        grid=(batches,),
        in_specs=[SMEM, SMEM, rows_of(rows, q_cols)] + [ANY] * span,
        out_specs=[rows_of(rows, q_cols), pl.BlockSpec((1, heads, rows), lambda i: (i, 0, 0))],
        out_shape=[like(q.shape, BF16), like((batches, heads, rows), F32)],
        scratch_shapes=[pltpu.VMEM((batches, group, 2 * head_dim), BF16),
                        pltpu.VMEM((head_dim, group), BF16),
                        pltpu.VMEM((heads, head_dim, tile), F32),
                        pltpu.SemaphoreType.DMA((batches, span))],
        compiler_params=params(),
        cost_estimate=took(18),
        name="attend",
    )(where, lengths, q, *kvs)


def middle_kernel(*refs, held, head_dim, chunk):
    x_ref, attn_ref, g_ref, gains_ref = refs[:4]
    if held is None:
        w_ref, wd_ref, wo_ref = refs[4:7]
    else:
        w_ref, wd_ref, wo_ref, rest_ref, sem = refs[-5:]
    (out_ref, mid_grad_ref, branch_ref, attn_grad_ref, delta_ref, low_ref, hidden_ref, grads_ref,
     gain_grad_ref) = refs[5:14] if held is not None else refs[7:16]

    @pl.when(pl.program_id(0) == 0)
    def _():
        if held is not None:
            f = Fetch(held.copies(refs[4], w_ref, rest_ref), sem)
            f.wait(*range(held.span))
            held.unfold(rest_ref, [wd_ref, wo_ref])
            f.wait(*range(held.span, 2 * held.span))
        gain_grad_ref[...] = jnp.zeros_like(gain_grad_ref)

    gain = gains_ref[1:2, :]
    attn = attn_ref[...]
    middle = x_ref[...].astype(F32) + mm(attn, wo_ref[...])
    inv = lax.rsqrt(jnp.mean(middle * middle, axis=-1, keepdims=True) + EPSILON)
    unit = middle * inv
    low = (unit * gain).astype(BF16)
    low_ref[...] = low
    grad = g_ref[...]
    result = middle
    back = jnp.zeros_like(middle)
    wide = wd_ref.shape[0]
    for c in range(wide // chunk):
        at = slice(c * chunk, (c + 1) * chunk)
        to = slice(wide + c * chunk, wide + (c + 1) * chunk)
        gate = mm(low, w_ref[:, at])
        lift = mm(low, w_ref[:, to])
        square = gate * gate
        bend = jnp.tanh(GELU_C * gate * (1.0 + GELU_A * square))
        cdf = 0.5 * (1.0 + bend)
        gelu = gate * cdf
        hidden = (gelu * lift).astype(BF16)
        hidden_ref[:, at] = hidden
        result = result + mm(hidden, wd_ref[at, :])
        hidden_grad = mm_nt(grad, wd_ref[at, :])
        slope = cdf + (0.5 * GELU_C) * gate * (1.0 - bend * bend) * (1.0 + 3.0 * GELU_A * square)
        gate_grad = (hidden_grad * lift * slope).astype(BF16)
        lift_grad = (hidden_grad * gelu).astype(BF16)
        grads_ref[:, at] = gate_grad
        grads_ref[:, to] = lift_grad
        back = back + mm_nt(gate_grad, w_ref[:, at]) + mm_nt(lift_grad, w_ref[:, to])
    out_ref[...] = result.astype(BF16)
    gain_grad_ref[...] += jnp.sum(unit * back, axis=0, keepdims=True)
    scaled = back * gain
    mid_grad = grad.astype(F32) + inv * (
        scaled - unit * jnp.mean(unit * scaled, axis=-1, keepdims=True)
    )
    mid_grad_ref[...] = mid_grad
    branch = mid_grad.astype(BF16)
    branch_ref[...] = branch
    attn_grad = mm_nt(branch, wo_ref[...]).astype(BF16)
    attn_grad_ref[...] = attn_grad
    product = attn_grad.astype(F32) * attn.astype(F32)
    half = head_dim // 2
    for h in range(attn.shape[1] // head_dim):
        c = h * head_dim
        folded = product[:, c : c + half] + product[:, c + half : c + head_dim]
        delta_ref[h : h + 1, :] = jnp.sum(folded.T, axis=0, keepdims=True)


def middle_part(x, attn, grad, gains, held, weights, head_dim):
    rows, width = x.shape
    q_cols = attn.shape[1]
    hidden = (weights[0].shape if held is None else held.shape)[1] // 2
    heads = q_cols // head_dim
    tile = math.gcd(rows, 512)
    if held is None:
        more, specs, scratch = weights, [full(w.shape) for w in weights], []
    else:
        more, specs = [held.array], [ANY]
        scratch = [pltpu.VMEM(held.shape, BF16)] + [pltpu.VMEM(s, BF16) for s in held.shapes]
        scratch += [pltpu.VMEM(held.scratch, BF16), pltpu.SemaphoreType.DMA((2 * held.span,))]
    return pl.pallas_call(
        functools.partial(middle_kernel, held=held, head_dim=head_dim, chunk=512),
        grid=(rows // tile,),
        in_specs=[rows_of(tile, width), rows_of(tile, q_cols), rows_of(tile, width),
                  full(gains.shape)] + specs,
        out_specs=[rows_of(tile, width), rows_of(tile, width), rows_of(tile, width),
                   rows_of(tile, q_cols), pl.BlockSpec((heads, tile), lambda i: (0, i)),
                   rows_of(tile, width), rows_of(tile, hidden), rows_of(tile, 2 * hidden),
                   full((1, width))],
        out_shape=[like((rows, width), BF16), like((rows, width), F32), like((rows, width), BF16),
                   like((rows, q_cols), BF16), like((heads, rows), F32),
                   like((rows, width), BF16), like((rows, hidden), BF16),
                   like((rows, 2 * hidden), BF16), like((1, width), F32)],
        scratch_shapes=scratch,
        compiler_params=params(),
        cost_estimate=took(39),
        name="middle",
    )(x, attn, grad, gains, *more)


def attend_back_kernel(*refs, head_dim, tile, block, scale, m, span):
    where, lengths_ref, lse_ref, delta_ref, q_ref, do_ref, cos_ref, sin_ref = refs[:8]
    kvs = refs[8 : 8 + span]
    kv_ref, dkv_ref, kt_ref, acc_ref, sem = refs[-5:]
    sends = refs[-5 - (span - 1) : -5]
    dq_ref, own_ref = refs[-5 - span - 1 : -5 - span + 1]
    heads = q_ref.shape[1] // head_dim
    half = head_dim // 2
    rows = q_ref.shape[0]
    place = where[1]
    base = place * rows
    lengths = [lengths_ref[m, d] for d in range(lengths_ref.shape[1])]
    tiles = rows // tile
    firsts = [lax.div(begin_of(base + t * tile, lengths), block) for t in range(tiles)]

    def copy(s):
        at = pl.multiple_of((place ^ s) * rows, rows)
        return pltpu.make_async_copy(kvs[s].at[pl.ds(m * rows, rows)],
                                     kv_ref.at[pl.ds(at, rows), :], sem.at[s])

    for s in range(span):
        pl.when((place ^ s) <= place)(lambda s=s: copy(s).start())
    acc_ref[...] = jnp.zeros_like(acc_ref)
    dkv_ref[...] = jnp.zeros_like(dkv_ref)
    for s in range(span):
        pl.when((place ^ s) <= place)(lambda s=s: copy(s).wait())

    def visit(kb, carry):
        at = pl.ds(pl.multiple_of(kb * block, block), block)
        keys = kv_ref[at, :head_dim]
        vals = kv_ref[at, head_dim:]
        kt_ref[...] = keys.T
        for t in range(tiles):
            q_rows = slice(t * tile, (t + 1) * tile)

            @pl.when((kb >= firsts[t]) & (kb * block < base + (t + 1) * tile))
            def _():
                high = base + t * tile + lax.broadcasted_iota(jnp.int32, (1, tile), 1)
                low = begin_of(high, lengths)
                index = kb * block + lax.broadcasted_iota(jnp.int32, (block, tile), 0)
                mask = (index >= low) & (index <= high)
                dk = jnp.zeros((block, head_dim), F32)
                dv = jnp.zeros((block, head_dim), F32)
                for h in range(heads):
                    cols = slice(h * head_dim, (h + 1) * head_dim)
                    q = q_ref[q_rows, cols]
                    do = do_ref[q_rows, cols]
                    s = mm_nt(keys, q)
                    p = jnp.where(mask, jnp.exp(s - lse_ref[0, h : h + 1, q_rows]), 0.0)
                    dv = dv + mm(p.astype(BF16), do)
                    ds = (p * (mm_nt(vals, do) - delta_ref[h : h + 1, q_rows])).astype(BF16)
                    dk = dk + mm(ds, q)
                    acc_ref[h, :, q_rows] += mm(kt_ref[...], ds)
                dkv_ref[at, :head_dim] += dk
                dkv_ref[at, head_dim:] += dv

        return carry

    lax.fori_loop(firsts[0], lax.div(base + rows + block - 1, block), visit, 0)
    cos, sin = cos_ref[...], sin_ref[...]
    for h in range(heads):
        c = h * head_dim
        dq = acc_ref[h].T * scale
        a, b = dq[:, :half], dq[:, half:]
        dq_ref[:, c : c + half] = (a * cos + b * sin).astype(BF16)
        dq_ref[:, c + half : c + head_dim] = (b * cos - a * sin).astype(BF16)
    own_ref[...] = dkv_ref[pl.ds(pl.multiple_of(place * rows, rows), rows), :]
    for s, send_ref in enumerate(sends, 1):
        at = pl.multiple_of((place ^ s) * rows, rows)
        send_ref[...] = dkv_ref[pl.ds(at, rows), :].astype(BF16)


def attend_back(where, lengths, lse, delta, q, do, kvs, cos, sin, head_dim, tile, block, scale, m,
                before, later):
    q_cols = q.shape[1]
    rows = q.shape[0] // lengths.shape[0]
    heads = q_cols // head_dim
    span = len(kvs)
    group = span * rows
    half = head_dim // 2
    here = pl.BlockSpec((rows, q_cols), lambda i: (m, 0))
    angle = pl.BlockSpec((rows, half), lambda i: (m, 0))
    more = ([] if before is None else [before]) + later
    return pl.pallas_call(
        functools.partial(attend_back_kernel, head_dim=head_dim, tile=tile, block=block,
                          scale=scale, m=m, span=span),
        grid=(1,),
        in_specs=[SMEM, SMEM, pl.BlockSpec((1, heads, rows), lambda i: (m, 0, 0)),
                  pl.BlockSpec((heads, rows), lambda i: (0, m)), here, here, angle, angle]
        + [ANY] * (span + len(more)),
        out_specs=[here] + [VMEM] * span,
        out_shape=[like(q.shape, BF16), like((rows, 2 * head_dim), F32)]
        + [like((rows, 2 * head_dim), BF16)] * (span - 1),
        scratch_shapes=[pltpu.VMEM((group, 2 * head_dim), BF16),
                        pltpu.VMEM((group, 2 * head_dim), F32), pltpu.VMEM((head_dim, block), BF16),
                        pltpu.VMEM((heads, head_dim, rows), F32),
                        pltpu.SemaphoreType.DMA((span,))],
        input_output_aliases={} if before is None else {8 + span: 0},
        compiler_params=params(),
        cost_estimate=took(20),
        name="attend_back",
    )(where, lengths, lse, delta, q, do, cos, sin, *kvs, *more)


def query_back_kernel(dq_ref, w_ref, ww_ref, lora_grad_ref, back_ref, *, q_cols, mid):
    dq = dq_ref[...]
    lora_grad = mm_nt(dq, ww_ref[...]).astype(BF16)
    lora_grad_ref[...] = lora_grad
    back_ref[...] = (mm_nt(dq, w_ref[:, :q_cols])
                     + mm_nt(lora_grad, w_ref[:, q_cols : q_cols + mid]))


def query_back(dq, w, ww, later=()):
    rows, q_cols = dq.shape
    mid, width = ww.shape[0], w.shape[0]
    tile = math.gcd(rows, 256)
    return pl.pallas_call(
        skipping(functools.partial(query_back_kernel, q_cols=q_cols, mid=mid), 3, len(later)),
        grid=(rows // tile,),
        in_specs=[rows_of(tile, q_cols), full(w.shape), full(ww.shape)] + [ANY] * len(later),
        out_specs=[rows_of(tile, mid), rows_of(tile, width)],
        out_shape=[like((rows, mid), BF16), like((rows, width), F32)],
        compiler_params=params(),
        cost_estimate=cost(2 * rows * (width * (q_cols + mid) + mid * q_cols), 9e6),
        name="query_back",
    )(dq, w, ww, *later)


def pair_back_kernel(*refs, head_dim, others):
    x_ref, gains_ref, cos_ref, sin_ref, w_ref, back_ref, mid_grad_ref, own_ref = refs[:8]
    pair_grad_ref, in_grad_ref, gain_grad_ref = refs[-3:]

    @pl.when(pl.program_id(0) == 0)
    def _():
        gain_grad_ref[...] = jnp.zeros_like(gain_grad_ref)

    half = head_dim // 2
    gain = gains_ref[0:1, :]
    cos, sin = cos_ref[...], sin_ref[...]
    dkv = own_ref[...]
    for ref in refs[8 : 8 + others]:
        dkv = dkv + ref[...].astype(F32)
    a, b = dkv[:, :half], dkv[:, half:head_dim]
    pair_grad_ref[:, :half] = (a * cos + b * sin).astype(BF16)
    pair_grad_ref[:, half:head_dim] = (b * cos - a * sin).astype(BF16)
    pair_grad_ref[:, head_dim:] = dkv[:, head_dim:].astype(BF16)
    back = back_ref[...] + mm_nt(pair_grad_ref[...], w_ref[:, : 2 * head_dim])
    x = x_ref[...].astype(F32)
    inv = lax.rsqrt(jnp.mean(x * x, axis=-1, keepdims=True) + EPSILON)
    unit = x * inv
    gain_grad_ref[...] += jnp.sum(unit * back, axis=0, keepdims=True)
    scaled = back * gain
    in_grad_ref[...] = mid_grad_ref[...] + inv * (
        scaled - unit * jnp.mean(unit * scaled, axis=-1, keepdims=True)
    )


def pair_back(x, gains, cos, sin, w, own, others, back, mid_grad, head_dim, m, batches, before=None,
              later=()):
    width = x.shape[1]
    rows = x.shape[0] // batches
    tile = math.gcd(rows, 256)
    half, cols = head_dim // 2, 2 * head_dim
    count = rows // tile

    def here(n):
        return pl.BlockSpec((tile, n), lambda i: (m * count + i, 0))

    more = ([] if before is None else [before]) + list(later)
    return pl.pallas_call(
        functools.partial(pair_back_kernel, head_dim=head_dim, others=len(others)),
        grid=(count,),
        in_specs=[here(width), full(gains.shape), here(half), here(half), full(w.shape),
                  here(width), here(width)] + [rows_of(tile, cols)] * (1 + len(others))
        + [ANY] * len(more),
        out_specs=[rows_of(tile, cols), here(width), full((1, width))],
        out_shape=[like((rows, cols), BF16), like(x.shape, F32), like((1, width), F32)],
        input_output_aliases={} if before is None else {8 + len(others): 1},
        compiler_params=params(),
        cost_estimate=cost(2 * rows * width * cols, 7e6),
        name="pair_back",
    )(x, gains, cos, sin, w, back, mid_grad, own, *others, *more)


def weight_grad_kernel(x_ref, y_ref, out_ref, xt_ref):
    @pl.when(pl.program_id(0) == 0)
    def _():
        xt_ref[...] = x_ref[...].T

    out_ref[...] = mm(xt_ref[...], y_ref[...]).astype(BF16)


def weight_grad(x, y, tile=256, later=()):
    rows, width = x.shape
    cols = y.shape[1]
    tile = math.gcd(cols, tile)
    return pl.pallas_call(
        skipping(weight_grad_kernel, 2, len(later)),
        grid=(cols // tile,),
        in_specs=[full(x.shape), pl.BlockSpec((rows, tile), lambda i: (0, i))] + [ANY] * len(later),
        out_specs=pl.BlockSpec((width, tile), lambda i: (0, i)),
        out_shape=like((width, cols), BF16),
        scratch_shapes=[pltpu.VMEM((width, rows), BF16)],
        compiler_params=params(),
        cost_estimate=took(10.3),
        name="weight_grad",
    )(x, y, *later)


def turn(x_ref, flat_ref, xt_ref, me, parts):
    flat_ref[...] = x_ref[...].T
    piece = flat_ref.shape[0] // parts
    for r in range(parts):
        at = pl.multiple_of((me ^ r) * piece, piece)
        to = (r % 2) * (parts // 2) + r // 2
        xt_ref[to * piece : (to + 1) * piece, :] = flat_ref[pl.ds(at, piece), :]


def column_grads_kernel(where, g_in, hidden_in, b_in, attn_in, keep_ref, send_ref, g_ref, hidden_ref,
                        b_ref, attn_ref, sem, *, parts):
    f = Fetch([(g_in, g_ref), (hidden_in, hidden_ref), (b_in, b_ref), (attn_in, attn_ref)], sem)
    span, _, piece, _ = keep_ref.shape
    per = parts // span
    col = 0
    for pair, x_ref, y_ref in (((0, 1), g_ref, hidden_ref), ((2, 3), b_ref, attn_ref)):
        n = y_ref.shape[1] // parts
        f.wait(pair[0])
        turned = x_ref[...].T
        f.wait(pair[1])
        for r in range(parts):
            at = pl.multiple_of((where[0] ^ r) * n, n)
            out = mm(turned, y_ref[:, pl.ds(at, n)]).astype(BF16)
            ref = send_ref if r % 2 else keep_ref
            for s in range(span):
                for i in range(per):
                    ref[s ^ where[1], r // 2, :, col + i * n : col + (i + 1) * n] = out[
                        (s * per + i) * piece : (s * per + i + 1) * piece]
        col += per * n


def column_grads(where, grad, hidden, branch, attn, parts, span):
    rows, width = grad.shape
    piece = width // parts
    cols = (hidden.shape[1] + attn.shape[1]) // span
    shape = like((span, parts // 2, piece, cols), BF16)
    arrays = (grad, hidden, branch, attn)
    return pl.pallas_call(
        functools.partial(column_grads_kernel, parts=parts),
        in_specs=[SMEM] + [ANY] * 4,
        out_specs=[VMEM] * 2,
        out_shape=[shape, shape],
        scratch_shapes=[pltpu.VMEM(a.shape, BF16) for a in arrays]
        + [pltpu.SemaphoreType.DMA((4,))],
        compiler_params=params(),
        cost_estimate=took(9),
        name="column_grads",
    )(where, *arrays)


class Fetch:
    def __init__(self, pairs, sem):
        self.copies = [pltpu.make_async_copy(a, b, sem.at[i]) for i, (a, b) in enumerate(pairs)]
        for c in self.copies:
            c.start()

    def wait(self, *which):
        for i in which:
            self.copies[i].wait()


def unrotate(dkv, cos, sin, head_dim):
    half = head_dim // 2
    a, b = dkv[:, :half], dkv[:, half:head_dim]
    return jnp.concatenate([a * cos + b * sin, b * cos - a * sin, dkv[:, head_dim:]],
                           axis=1).astype(BF16)


def norm_back(x, gain, back, rest):
    inv = lax.rsqrt(jnp.mean(x * x, axis=-1, keepdims=True) + EPSILON)
    unit = x * inv
    scaled = back * gain
    return (rest + inv * (scaled - unit * jnp.mean(unit * scaled, axis=-1, keepdims=True)),
            jnp.sum(unit * back, axis=0, keepdims=True))


def fold_rows(out_ref, value, first, parts, piece, fold, j):
    count = value.shape[0] // parts
    for d in range(parts):
        at = d * piece + j * count
        out_ref[at : at + count, first : first + fold] = value[d * count : (d + 1) * count]


def query_side_kernel(*refs, head_dim, parts, fold, others):
    (dq_in, ww_in, w_in, normed_in, lora_in, own_in, wp_in, x_in, mg_in, gains_ref, cos_ref,
     sin_ref, keep_ref, got_ref) = refs[:14]
    others_in = refs[14 : 14 + others]
    (queries_ref, back_ref, pair_ref, in_grad_ref, one_ref, near_ref, far_ref,
     dq, ww, w, normed, lora, own, wp, x, mg, there, hold, sem) = refs[14 + others :]
    rows = x.shape[0]
    f = Fetch([(dq_in, dq), (ww_in, ww), (w_in, w), (normed_in, normed), (lora_in, lora),
               (own_in, own), (wp_in, wp), (x_in.at[pl.ds(0, rows)], x),
               (mg_in.at[pl.ds(0, rows)], mg)]
              + [(r, there.at[i]) for i, r in enumerate(others_in)], sem)
    near_ref[...] = (keep_ref[0].astype(F32) + got_ref[0].astype(F32)).astype(BF16)
    far_ref[...] = (keep_ref[1].astype(F32) + got_ref[1].astype(F32)).astype(BF16)
    q_cols, mid = dq.shape[1], lora.shape[1]
    f.wait(0, 1, 2)
    lora_grad = mm_nt(dq[...], ww[...]).astype(BF16)
    for m in range(dq.shape[0] // rows):
        at = slice(m * rows, (m + 1) * rows)
        back = mm_nt(dq[at, :], w[:, :q_cols]) + mm_nt(lora_grad[at], w[:, q_cols : q_cols + mid])
        if m == 0:
            hold[...] = back
        else:
            back_ref[(m - 1) * rows : m * rows] = back
    f.wait(3, 4)
    step = math.gcd(q_cols, 512)
    turned = normed[...].T
    for c in range(0, q_cols, step):
        queries_ref[:, c : c + step] = mm(turned, dq[:, c : c + step]).astype(BF16)
    queries_ref[:, q_cols : q_cols + mid] = mm(turned, lora_grad).astype(BF16)
    piece, count = normed.shape[1] // parts, mid // parts
    turned = lora[...].T
    for j in range(q_cols // fold):
        out = mm(turned, dq[:, j * fold : (j + 1) * fold]).astype(BF16)
        fold_rows(queries_ref, out, q_cols + mid, parts, piece, fold, j)
    rest = (q_cols // fold) * count
    for d in range(parts):
        queries_ref[d * piece + rest : (d + 1) * piece, q_cols + mid :] = jnp.zeros(
            (piece - rest, fold), BF16)
    f.wait(*range(5, 9 + others))
    dkv = own[...]
    for i in range(others):
        dkv = dkv + there[i].astype(F32)
    pair = unrotate(dkv, cos_ref[...], sin_ref[...], head_dim)
    pair_ref[...] = pair
    back = hold[...] + mm_nt(pair, wp[:, : 2 * head_dim])
    in_grad_ref[...], one_ref[...] = norm_back(x[...].astype(F32), gains_ref[0:1, :], back, mg[...])


def query_side(dq, ww, w, normed, lora_mid, own, others, w_pair, x, mid_grad, gains, cos, sin,
               keep, got, head_dim, parts, fold, batches, later):
    total, q_cols = dq.shape
    rows = total // batches
    width, mid = normed.shape[1], lora_mid.shape[1]
    half, cols = head_dim // 2, 2 * head_dim
    angle = pl.BlockSpec((rows, half), lambda i: (0, 0))
    n = len(others)
    return pl.pallas_call(
        skipping(functools.partial(query_side_kernel, head_dim=head_dim, parts=parts, fold=fold,
                                   others=n), 14 + n, len(later)),
        grid=(1,),
        in_specs=[ANY] * 9 + [VMEM, angle, angle, VMEM, VMEM] + [ANY] * (n + len(later)),
        out_specs=[VMEM] * 3 + [pl.BlockSpec((rows, width), lambda i: (0, 0))] + [VMEM] * 3,
        out_shape=[like((width, q_cols + mid + fold), BF16), like((total - rows, width), F32),
                   like((rows, cols), BF16), like((total, width), F32), like((1, width), F32)]
        + [like(keep.shape[1:], BF16)] * 2,
        scratch_shapes=[pltpu.VMEM(dq.shape, BF16), pltpu.VMEM(ww.shape, BF16),
                        pltpu.VMEM(w.shape, BF16), pltpu.VMEM(normed.shape, BF16),
                        pltpu.VMEM(lora_mid.shape, BF16), pltpu.VMEM((rows, cols), F32),
                        pltpu.VMEM(w_pair.shape, BF16), pltpu.VMEM((rows, width), BF16),
                        pltpu.VMEM((rows, width), F32), pltpu.VMEM((n, rows, cols), BF16),
                        pltpu.VMEM((rows, width), F32), pltpu.SemaphoreType.DMA((9 + n,))],
        compiler_params=params(),
        cost_estimate=cost(LONG, 20e6),
        name="query_side",
    )(dq, ww, w, normed, lora_mid, own, w_pair, x, mid_grad, gains, cos, sin, keep, got, *others,
      *later)


def pair_side_kernel(*refs, head_dim, parts, others):
    (where, own_in, wp_in, back_in, x_in, mg_in, normed_in, first_in, gains_ref, cos_ref, sin_ref,
     one_ref, two_ref) = refs[:13]
    others_in = refs[13 : 13 + others]
    outs = refs[14 + others :]
    in_grad_ref, send_ref = outs[:2]
    keeps = outs[2 : 2 + parts // 2]
    (own, wp, back, x, mg, normed, pair_ref, there, flat_ref, xt_ref, gain_ref,
     sem) = outs[2 + parts // 2 :]
    rows = x.shape[0]
    f = Fetch([(normed_in, normed), (own_in, own)]
              + [(r, there.at[i]) for i, r in enumerate(others_in)]
              + [(first_in, pair_ref.at[pl.ds(0, rows)]), (wp_in, wp), (back_in, back),
                 (x_in.at[pl.ds(rows, rows)], x), (mg_in.at[pl.ds(rows, rows)], mg)], sem)
    f.wait(0)
    turn(normed, flat_ref, xt_ref, where[0], parts)
    f.wait(*range(1, 2 + others))
    dkv = own[...]
    for i in range(others):
        dkv = dkv + there[i].astype(F32)
    pair = unrotate(dkv, cos_ref[...], sin_ref[...], head_dim)
    pair_ref[rows:, :] = pair
    f.wait(*range(2 + others, 7 + others))
    grads = back[...] + mm_nt(pair, wp[:, : 2 * head_dim])
    in_grad_ref[...], one = norm_back(x[...].astype(F32), gains_ref[0:1, :], grads, mg[...])
    width = flat_ref.shape[0]
    piece, half, cols = width // parts, parts // 2, 2 * head_dim
    out = mm(xt_ref[...], pair_ref[...]).astype(BF16)
    pad = jnp.zeros((126, width), F32)
    gain_ref[...] = jnp.concatenate([one + one_ref[...], two_ref[...], pad], axis=0).T.astype(BF16)
    for k in range(half):
        keeps[k][:, :cols] = out[k * piece : (k + 1) * piece]
        send_ref[k, :, :cols] = out[(half + k) * piece : (half + k + 1) * piece]
        at = pl.multiple_of((where[0] ^ (2 * k)) * piece, piece)
        keeps[k][:, cols:] = gain_ref[pl.ds(at, piece), :]
        at = pl.multiple_of((where[0] ^ (2 * k + 1)) * piece, piece)
        send_ref[k, :, cols:] = gain_ref[pl.ds(at, piece), :]


def pair_side(where, own, others, w_pair, back, x, mid_grad, normed, first, gains, cos, sin, one,
              two, in_grad, head_dim, parts):
    total, width = normed.shape
    rows = total // 2
    half, cols = head_dim // 2, 2 * head_dim
    piece = width // parts
    angle = pl.BlockSpec((rows, half), lambda i: (1, 0))
    n = len(others)
    return pl.pallas_call(
        functools.partial(pair_side_kernel, head_dim=head_dim, parts=parts, others=n),
        grid=(1,),
        in_specs=[SMEM] + [ANY] * 7 + [VMEM, angle, angle, VMEM, VMEM] + [ANY] * (n + 1),
        out_specs=[pl.BlockSpec((rows, width), lambda i: (1, 0))] + [VMEM] * (1 + parts // 2),
        out_shape=[like((total, width), F32), like((parts // 2, piece, cols + 128), BF16)]
        + [like((piece, cols + 128), BF16)] * (parts // 2),
        scratch_shapes=[pltpu.VMEM((rows, cols), F32), pltpu.VMEM(w_pair.shape, BF16),
                        pltpu.VMEM((rows, width), F32), pltpu.VMEM((rows, width), BF16),
                        pltpu.VMEM((rows, width), F32), pltpu.VMEM(normed.shape, BF16),
                        pltpu.VMEM((total, cols), BF16), pltpu.VMEM((n, rows, cols), BF16),
                        pltpu.VMEM((width, total), BF16), pltpu.VMEM((width, total), BF16),
                        pltpu.VMEM((width, 128), BF16), pltpu.SemaphoreType.DMA((7 + n,))],
        input_output_aliases={13 + n: 0},
        compiler_params=params(),
        cost_estimate=cost(LONG, 12e6),
        name="pair_side",
    )(where, own, w_pair, back, x, mid_grad, normed, first, gains, cos, sin, one, two, *others,
      in_grad)


def join_kernel(left_ref, *refs):
    out_ref = refs[-1]
    n = left_ref.shape[1]
    out_ref[:, :n] = left_ref[...]
    out_ref[:, n:] = tree([r[...].astype(F32) for r in refs[:-1]]).astype(BF16)


def join(left, parts, later=()):
    rows, n = left.shape
    count = 1 + len(parts)
    return pl.pallas_call(
        skipping(join_kernel, count, len(later)),
        in_specs=[VMEM] * count + [ANY] * len(later),
        out_specs=VMEM,
        out_shape=like((rows, n + parts[0].shape[1]), BF16),
        compiler_params=params(),
        cost_estimate=took(2),
        name="join",
    )(left, *parts, *later)


def finish_kernel(*refs, mid, q_cols, cols, fold):
    parts, outs = refs[:-6], refs[-6:]
    query_ref, narrow_ref, widen_ref, kv_ref, one_ref, two_ref = outs
    total = tree([p[...].astype(F32) for p in parts])
    query_ref[...] = total[:, :q_cols]
    narrow_ref[...] = total[:, q_cols : q_cols + mid]
    first = q_cols + mid
    count = widen_ref.shape[0]
    for j in range(q_cols // fold):
        widen_ref[:, j * fold : (j + 1) * fold] = total[j * count : (j + 1) * count,
                                                        first : first + fold]
    first += fold
    kv_ref[...] = total[:, first : first + cols]
    gains = total[:, first + cols :].T
    one_ref[...] = gains[0:1]
    two_ref[...] = gains[1:2]


def finish(parts, q_cols, mid, count, cols, fold):
    piece = parts[0].shape[0]
    return pl.pallas_call(
        functools.partial(finish_kernel, q_cols=q_cols, mid=mid, cols=cols, fold=fold),
        in_specs=[VMEM] * len(parts),
        out_specs=[VMEM] * 6,
        out_shape=[like((piece, q_cols), F32), like((piece, mid), F32), like((count, q_cols), F32),
                   like((piece, cols), F32), like((1, piece), F32), like((1, piece), F32)],
        compiler_params=params(),
        cost_estimate=took(2.5),
        name="finish",
    )(*parts)


def swap_cores(keeps, send, later=()):
    got, count = swap(send, "fsdp", 1), len(keeps)
    return add([*keeps, got], [[(k, None), (count, k)] for k in range(count)], later)


def pairs_kernel(*refs):
    parts, (keep_ref, send_ref) = refs[:-2], refs[-2:]
    for i in range(2):
        for k, ref in ((2 * i, keep_ref), (2 * i + 1, send_ref)):
            ref[i] = tree([p[k].astype(F32) for p in parts]).astype(BF16)


def sum_pairs(parts, later=()):
    count, shape = len(parts), like((2,) + parts[0].shape[1:], BF16)
    return pl.pallas_call(
        skipping(pairs_kernel, count, len(later)),
        in_specs=[VMEM] * count + [ANY] * len(later),
        out_specs=[VMEM] * 2,
        out_shape=[shape] * 2,
        compiler_params=params(),
        cost_estimate=took(2.4),
        name="sum_pairs",
    )(*parts, *later)


def cut_kernel(where, x_ref, *outs):
    part = outs[0].shape[1]
    for s, out in enumerate(outs):
        at = pl.multiple_of((where[1] ^ s) * part, part)
        out[...] = x_ref[:, pl.ds(at, part)]


def cut_parts(where, x, later=()):
    span = lax.axis_size("seq")
    rows, part = x.shape[0], x.shape[1] // span
    cut = pl.pallas_call(
        skipping(cut_kernel, 2, len(later)),
        in_specs=[SMEM, VMEM] + [ANY] * len(later),
        out_specs=[VMEM] * span,
        out_shape=[like((rows, part), x.dtype)] * span,
        compiler_params=params(),
        cost_estimate=took(2),
        name="cut",
    )(where, x, *later)
    return cut


def halves_kernel(*refs):
    out_ref = refs[-1]
    n = refs[0].shape[1]
    out_ref[:, :n] = tree([r[...].astype(F32) for r in refs[:-3]]).astype(BF16)
    out_ref[:, n:] = tree([r[...].astype(F32) for r in refs[-3:-1]]).astype(BF16)


def halves(left, right, later=()):
    count = len(left) + 2
    shape = (left[0].shape[0], left[0].shape[1] + right[0].shape[1])
    return pl.pallas_call(
        skipping(halves_kernel, count, len(later)),
        in_specs=[VMEM] * count + [ANY] * len(later),
        out_specs=VMEM,
        out_shape=like(shape, BF16),
        compiler_params=params(),
        cost_estimate=cost(LONG, 2e6),
        name="halves",
    )(*left, *right, *later)


def lay_kernel(where, *refs, n, k):
    parts = refs[:-6]
    span = len(parts)
    gate_ref, up_ref, down_ref, out_ref, tall_ref, tall2_ref = refs[-6:]
    piece = parts[0].shape[0]
    half = span // 2
    wide = gate_ref.shape[1] // half
    per = (parts[0].shape[1] - wide) // (n + k)
    for s, ref in enumerate(parts):
        q = where[1] ^ s
        for i, out in enumerate((gate_ref, up_ref)):
            @pl.when(q // half == i)
            def _():
                at = pl.multiple_of((q % half) * wide, wide)
                out[:, pl.ds(at, wide)] = ref[:, :wide].astype(F32)
        for i in range(per):
            at = pl.ds(pl.multiple_of((q * per + i) * piece, piece), piece)
            first = wide + i * n
            tall_ref[at, :] = ref[:, first : first + n].astype(F32)
            first = wide + per * n + i * k
            tall2_ref[at, :] = ref[:, first : first + k].astype(F32)
    down_ref[...] = tall_ref[...].T
    out_ref[...] = tall2_ref[...].T


def lay(where, parts, hidden, n, k, later=()):
    piece = parts[0].shape[0]
    width = piece * lax.axis_size("fsdp")
    return pl.pallas_call(
        skipping(functools.partial(lay_kernel, n=n, k=k), 1 + len(parts), len(later)),
        in_specs=[SMEM] + [VMEM] * len(parts) + [ANY] * len(later),
        out_specs=[VMEM] * 4,
        out_shape=[like((piece, hidden), F32)] * 2 + [like((n, width), F32), like((k, width), F32)],
        scratch_shapes=[pltpu.VMEM((width, n), F32), pltpu.VMEM((width, k), F32)],
        compiler_params=params(),
        cost_estimate=took(3),
        name="lay",
    )(where, *parts, *later)


def begin_of(index, lengths):
    ends = [lengths[0]]
    for n in lengths[1:]:
        ends.append(ends[-1] + n)
    begin = index
    for d in reversed(range(len(lengths))):
        begin = jnp.where(index < ends[d], ends[d] - lengths[d], begin)
    return begin


def local(tokens, document_lengths, cotangent, attention_gain, query_projection, narrowing_factor,
          widening_factor, key_value_projection, output_projection, feedforward_gain,
          gate_projection, up_projection, down_projection):
    batches, _, rows, width = tokens.shape
    head_dim = key_value_projection.shape[1] // 2
    q_cols = query_projection.shape[1]
    mid = narrowing_factor.shape[1]
    hidden = gate_projection.shape[1]
    kv_cols = 2 * head_dim
    scale = head_dim ** (-0.5)
    parts, span = lax.axis_size("fsdp"), lax.axis_size("seq")
    place = lax.axis_index("seq")
    tile = block = math.gcd(rows, 512)
    where = jnp.stack([lax.axis_index("fsdp"), place]).astype(jnp.int32)
    piece = width // parts
    direct = piece % 16 == 0
    fold = 512
    folds = q_cols // fold

    lengths = document_lengths[:, 0]
    half = head_dim // 2
    index = place * rows + lax.broadcasted_iota(jnp.int32, (batches, rows, half), 1)
    begin = begin_of(index, [lengths[:, d][:, None, None] for d in range(lengths.shape[1])])
    freqs = THETA ** (-(lax.broadcasted_iota(jnp.int32, (1, half), 1).astype(F32) * 2.0 / head_dim))
    angles = ((index - begin).astype(F32) * freqs).reshape(batches * rows, half)
    cos, sin = jnp.cos(angles), jnp.sin(angles)

    if direct:
        first = Shards(pack_pair(key_value_projection, attention_gain, feedforward_gain))
        third = pack(where, gate_projection, up_projection, down_projection, output_projection,
                     span, [cos, sin] + first.arrays[2::2])
        held = Tiled(third, 2 * hidden, down_projection, output_projection)
        weights = None
    else:
        def gather(x):
            return lax.all_gather(x, "fsdp", axis=0, tiled=True)

        first = jnp.concatenate(
            [key_value_projection,
             jnp.pad(jnp.stack([attention_gain, feedforward_gain], axis=1), ((0, 0), (0, 126)))],
            axis=1)
        turned = jnp.concatenate(
            [widening_factor[:, j * fold : (j + 1) * fold] for j in range(folds)])
        turned = jnp.pad(turned, ((0, piece - turned.shape[0]), (0, 0)))
        second = jnp.concatenate([query_projection, narrowing_factor, turned], axis=1)
        first, second = Whole(gather(first)), Whole(gather(second))
        second.rows = piece
        held = None
        weights = [gather(jnp.concatenate([gate_projection, up_projection], axis=1)),
                   gather(down_projection), gather(output_projection)]

    x = tokens.reshape(batches * rows, width)
    grad = cotangent.reshape(batches * rows, width)
    normed, kv, w_pair, gains = project_kv(where, x, cos, sin, first, head_dim)
    kvs = [kv] + [swap(kv, "seq", s) for s in range(1, span)]
    if direct:
        second = Shards(pack_query(query_projection, narrowing_factor, widening_factor, fold,
                                   [kv]), True)
    lora_mid, q, w_query, ww = project_q(where, normed, cos, sin, second, head_dim, q_cols, mid,
                                         scale, kvs[1:])
    attended, lse = attend(where, lengths, q, kvs, head_dim, tile, block)
    (output, mid_grad, branch, attn_grad, delta, ffn_low, hidden_low, lift_grads,
     gain_two_grad) = middle_part(x, attended, grad, gains, held, weights, head_dim)

    if direct:
        keep, send = column_grads(where, grad, hidden_low, branch, attended, parts, span)
        got = swap(send, "fsdp", 1)
        lifts = weight_grad(ffn_low, lift_grads, 1024, [keep])
        lifts_sum = lax.psum_scatter(lifts, "fsdp", scatter_dimension=0, tiled=True)
        columns = add([keep, got], [[(0, s), (1, s)] for s in range(span)], [lifts])
        there = [columns[0]] + [swap(a, "seq", s) for s, a in enumerate(columns) if s > 0]
    dq, owns, others = None, [], []
    for m in range(batches):
        later = []
        if direct and m == 0:
            later = columns
        if direct and m == 1:
            keep, send = sum_pairs(there, [dq])
            got = swap(send, "fsdp", 2)
            later = [keep]
        dq, own, *sends = attend_back(where, lengths, lse, delta, q, attn_grad, kvs, cos, sin,
                                      head_dim, tile, block, scale, m, dq, later)
        owns.append(own)
        others.append([swap(a, "seq", s) for s, a in enumerate(sends, 1)])
    if direct:
        queries, back, pair, in_grad, one, near, far = query_side(
            dq, ww, w_query, normed, lora_mid, owns[0], others[0], w_pair, x, mid_grad, gains, cos,
            sin, keep, got, head_dim, parts, fold, batches, [lifts_sum])
        queries_sum = lax.psum_scatter(queries, "fsdp", scatter_dimension=0, tiled=True)
        in_grad, send, *keeps = pair_side(where, owns[1], others[1], w_pair, back, x, mid_grad,
                                          normed, pair, gains, cos, sin, one, gain_two_grad,
                                          in_grad, head_dim, parts)

        def share(x):
            return [x] + [swap(x, "seq", s) for s in range(1, span)]

        lifts_cut = cut_parts(where, lifts_sum, others[1])
        lifts_parts = [lifts_cut[0]] + [swap(lifts_cut[s], "seq", s) for s in range(1, span)]
        mine = halves(lifts_parts, [near, swap(far, "fsdp", 4)], [send])
        laid = share(mine)
        shards = swap_cores(keeps, send, [mine])
        mine = join(queries_sum, [shards[0]] + [
            swap(a, "fsdp", 2 * k) for k, a in enumerate(shards) if k > 0])
        last = share(mine)
        gate_grad, up_grad, down_grad, out_grad = lay(
            where, laid, hidden, hidden // parts, q_cols // parts, [mine])
        query_grad, narrow_grad, widen_grad, key_value_grad, one, two = finish(
            last, q_cols, mid, mid // parts, kv_cols, fold)
        gain_one_grad, gain_two_grad = one.reshape(piece), two.reshape(piece)
    else:
        lora_grad, back = query_back(dq, w_query, ww)
        in_grad, pairs, ones = None, [], []
        for m in range(batches):
            pair, in_grad, one = pair_back(x, gains, cos, sin, w_pair, owns[m], others[m], back,
                                           mid_grad, head_dim, m, batches, in_grad)
            pairs.append(pair)
            ones.append(one)

        def scatter(x):
            part = lax.psum_scatter(x.astype(BF16), "fsdp", scatter_dimension=0, tiled=True)
            return lax.psum(part, "seq").astype(F32)

        pair_grad = jnp.concatenate(pairs)
        gain_one_grad = sum(ones)
        down_grad = scatter(weight_grad(grad, hidden_low).T)
        out_grad = scatter(weight_grad(branch, attended).T)
        lift_w = scatter(weight_grad(ffn_low, lift_grads))
        gate_grad, up_grad = lift_w[:, :hidden], lift_w[:, hidden:]
        query_grad = scatter(weight_grad(normed, dq))
        narrow_grad = scatter(weight_grad(normed, lora_grad))
        widen_grad = scatter(weight_grad(lora_mid, dq))
        key_value_grad = scatter(weight_grad(normed, pair_grad))
        gains_grad = scatter(jnp.concatenate([gain_one_grad, gain_two_grad]).T)
        gain_one_grad, gain_two_grad = gains_grad[:, 0], gains_grad[:, 1]
    return (output.reshape(batches, 1, rows, width), in_grad.reshape(batches, 1, rows, width),
            gain_one_grad, query_grad, narrow_grad, widen_grad, key_value_grad, out_grad,
            gain_two_grad, gate_grad, up_grad, down_grad)


def solution(mesh):
    rows = P(None, "fsdp", "seq", None)
    vector, matrix = P("fsdp"), P("fsdp", None)
    in_specs = (rows, P(None, "fsdp", None), rows, vector) + (matrix,) * 5 + (vector,) + (matrix,) * 3
    out_specs = (rows, rows, vector) + (matrix,) * 5 + (vector,) + (matrix,) * 3
    return jax.shard_map(local, mesh=mesh, in_specs=in_specs, out_specs=out_specs, check_vma=False)
```

time: 420 us -> 352 us (0.84)
  starting transfers between devices: 79.3 us -> 62.4 us
  local copies, waits for them, and re-layouts: 25.2 us -> 8.6 us
  Pallas kernels: 161 us -> 145 us
  between operations: 25.4 us -> 14.3 us
  other arithmetic: 11.4 us -> 3.89 us
    ppermute x49 -> x42, waiting for transfers between devices: 107 us -> 84.7 us  [swap(): lax.ppermute(x, axis, [(i, i ^ by) for i in range(lax.axis_size(axis))])]
    all_gather x1, waiting for transfers between devices: 4.12 us -> 25.8 us  [__init__(): self.array = lax.all_gather(packed, ('seq', 'fsdp'), axis=0, tiled=True)]
    ppermute x49 -> x42, starting transfers between devices: 79.2 us -> 62.2 us  [swap(): lax.ppermute(x, axis, [(i, i ^ by) for i in range(lax.axis_size(axis))])]
    slice x11 -> x1, local copies, waits for them, and re-layouts: 10.8 us -> 0.18 us  [local(): lengths[:, d][:, None, None]]
    pallas_call x7 -> x2, Pallas kernels: 15.7 us -> 5.57 us  [add(): pl.pallas_call(skipping(functools.partial(add_kernel, count=count, groups...]
    pallas_call x2 -> x1, Pallas kernels: 15.6 us -> 10 us  [attend(): pl.pallas_call(functools.partial(attend_kernel, head_dim=head_dim, tile=t...]
    pallas_call x9 -> x13, Pallas kernels: 53.7 us -> 58.4 us  [the longest x1 12.4 us: query_side(): pl.pallas_call(skipping(functools.partial(query_side_kernel, head_dim=hea...]
    unnamed x135 -> x82, local copies, waits for them, and re-layouts: 11.8 us -> 8.42 us
  transfers between devices with their start and end apart: 52 -> 45, of which waited for: 20 -> 23; matrix products, arithmetic and copies ran while one was open for 3% -> 1% of each run, Pallas kernels for 23% -> 23%
where the time goes in v3:
time: 352 us; the launch traced here: 346 us
  Pallas kernels  145 us (41%)
  waiting for transfers between devices  112 us (32%)
  starting transfers between devices  62.4 us (18%)
  between operations  14.3 us (4%)
  local copies, waits for them, and re-layouts  8.6 us (2%)
  other arithmetic  3.89 us (1%)
    ppermute x42, waiting for transfers between devices, swap(): lax.ppermute(x, axis, [(i, i ^ by) for i in range(lax.axis_size(axis))])  84.7 us
    ppermute x42, starting transfers between devices, swap(): lax.ppermute(x, axis, [(i, i ^ by) for i in range(lax.axis_size(axis))])  62.2 us
    pallas_call x1, Pallas kernels, middle_part(): pl.pallas_call(functools.partial(middle_kernel, held=held, head_dim=head_...  37.8 us
    all_gather x1, waiting for transfers between devices, __init__(): self.array = lax.all_gather(packed, ('seq', 'fsdp'), axis=0, tiled=True)  25.8 us
    pallas_call x2, Pallas kernels, attend_back(): pl.pallas_call(functools.partial(attend_back_kernel, head_dim=head_dim, t...  17.8 us
    pallas_call x1, Pallas kernels, query_side(): pl.pallas_call(skipping(functools.partial(query_side_kernel, head_dim=hea...  12.4 us
    pallas_call x1, Pallas kernels, column_grads(): pl.pallas_call(functools.partial(column_grads_kernel, parts=parts), in_sp...  11.4 us
    pallas_call x1, Pallas kernels, weight_grad(): pl.pallas_call(skipping(weight_grad_kernel, 2, len(later)), grid=(cols //...  10.3 us
  transfers between devices with their start and end apart: 45, of which 23 were waited for; matrix products, arithmetic and copies ran while one was open for 1% of the time, Pallas kernels for 23%

profile of v3, /device:TPU:0, one launch (start us, length us, event | category | flops | bytes accessed | tf_op | source)
XLA Modules:
  0.0 345.9 jit_solution(14932140571986658094)
XLA Ops:
  8.9 5.0 %collective-permute-start.5 = (bf16[80,640]{1,0:T(8,128)(2,1)}, bf16[80,640]{1,0:T(8,128)(2,1)S(1)}, u32[]{:S(2)}, u32[]{:S(2)}) collective-permute-start(bf16[80,640]{1,0:T(8,128)(2,1)} %pack_pair.1.refs_4_), channel_id=1, source_target_pairs={{0,6},{1,7},{2,4},{3,5},{4,2},{5,3},{6,0},{7,1},{8,14},{9,15},{10,... | collective-permute-start | bytes 307208 | tf_op jit(solution)/shard_map/ppermute | solution.py:62
  18.8 4.0 %collective-permute-done.3.refs_8_ = bf16[80,640]{1,0:T(8,128)(2,1)S(1)} collective-permute-done((bf16[80,640]{1,0:T(8,128)(2,1)}, bf16[80,640]{1,0:T(8,128)(2,1)S(1)}, u32[]{:S(2)}, u32[]{:S(2)}) %collective-permute-start.3) | collective-permute-done | bytes 102432 | tf_op jit(solution)/shard_map/ppermute | solution.py:62
  28.4 4.8 %project_kv.1 = (bf16[1024,640]{1,0:T(8,128)(2,1)}, bf16[1024,512]{1,0:T(8,128)(2,1)}, bf16[640,640]{1,0:T(8,128)(2,1)}, f32[8,640]{1,0:T(8,128)}) custom-call(s32[2]{0:T(128)} %pad_add_fusion.refs_0_.where, bf16[1024,640]{1,0:T(8,128)(2,1)} %bitcast.35, f32[1024,128]{1,0:T(8,128)} %get-tuple-element.175.refs_2_.refs_5_.refs_6_.refs_10_.refs_9_, ...), custom_call_target="tpu_custom_call" | custom-call | flops 5500000256 | bytes 1 | tf_op jit(solution)/shard_map/project_kv/pallas_call | solution.py:292
  41.6 15.3 %collective-permute-done.10.refs_8_ = bf16[80,1792]{1,0:T(8,128)(2,1)S(1)} collective-permute-done((bf16[80,1792]{1,0:T(8,128)(2,1)}, bf16[80,1792]{1,0:T(8,128)(2,1)S(1)}, u32[]{:S(2)}, u32[]{:S(2)}) %collective-permute-start.10) | collective-permute-done | bytes 286752 | tf_op jit(solution)/shard_map/ppermute | solution.py:62
  58.8 7.4 %collective-permute-done.12.refs_10_ = bf16[80,1792]{1,0:T(8,128)(2,1)S(1)} collective-permute-done((bf16[80,1792]{1,0:T(8,128)(2,1)S(1)}, bf16[80,1792]{1,0:T(8,128)(2,1)S(1)}, u32[]{:S(2)}, u32[]{:S(2)}) %collective-permute-start.12) | collective-permute-done | bytes 286752 | tf_op jit(solution)/shard_map/ppermute | solution.py:62
  68.1 20.8 %collective-permute-done.15.refs_13_.refs_5_.refs_10_ = bf16[1024,512]{1,0:T(8,128)(2,1)S(1)} collective-permute-done((bf16[1024,512]{1,0:T(8,128)(2,1)S(1)}, bf16[1024,512]{1,0:T(8,128)(2,1)S(1)}, u32[]{:S(2)}, u32[]{:S(2)}) %collective-permute-start.15) | collective-permute-done | bytes 1048608 | tf_op jit(solution)/shard_map/ppermute | solution.py:62
  92.4 8.4 %project_q.1 = (bf16[1024,256]{1,0:T(8,128)(2,1)}, bf16[1024,1024]{1,0:T(8,128)(2,1)}, bf16[640,1792]{1,0:T(8,128)(2,1)}, bf16[256,1024]{1,0:T(8,128)(2,1)}) custom-call(s32[2]{0:T(128)} %pad_add_fusion.refs_0_.where, bf16[1024,640]{1,0:T(8,128)(2,1)} %get-tuple-element.80.refs_1_.refs_3_.refs_6_, ...), custom_call_target="tpu_custom_call" | custom-call | flops 9349999616 | bytes 1 | tf_op jit(solution)/shard_map/project_q/pallas_call | solution.py:343
  100.7 10.0 %attend.1 = (bf16[1024,1024]{1,0:T(8,128)(2,1)}, f32[2,4,512]{2,1,0:T(4,128)}) custom-call(s32[2]{0:T(128)} %pad_add_fusion.refs_0_.where, s32[2,2]{1,0:T(2,128)} %bitcast.29, bf16[1024,1024]{1,0:T(8,128)(2,1)} %get-tuple-element.82.refs_2_.refs_4_, bf16[1024,512]{1,0:T(8,128)(2,1)} %get-tuple-element.81.refs_3_.refs_8_, bf16[1024,512]{1,0:T(8,128)(2,1)} %copy-done.5, ...), custom_call_target="tpu_custom_call" | custom-call | flops 19800000512 | bytes 1 | tf_op jit(solution)/shard_map/attend/pallas_call | solution.py:438
  110.8 25.8 %all-gather.2.cloned.1.call-done.refs_4_ = bf16[2560,1792]{1,0:T(8,128)(2,1)} async-done(((bf16[80,1792]{1,0:T(8,128)(2,1)}), bf16[2560,1792]{1,0:T(8,128)(2,1)}) %all-gather.2.cloned.1.call-update) | async-done | bytes 9175056 | tf_op jit(solution)/shard_map/all_gather | solution.py:217
  136.5 37.8 %middle.1 = (bf16[1024,640]{1,0:T(8,128)(2,1)}, f32[1024,640]{1,0:T(8,128)}, bf16[1024,640]{1,0:T(8,128)(2,1)}, bf16[1024,1024]{1,0:T(8,128)(2,1)}, f32[4,1024]{...) custom-call(bf16[1024,640]{1,0:T(8,128)(2,1)} %bitcast.36, ...), custom_call_target="tpu_custom_call" | custom-call | flops 42900000768 | bytes 1 | tf_op jit(solution)/shard_map/middle/pallas_call | solution.py:533
  174.3 11.4 %column_grads.1 = (bf16[4,4,80,768]{3,2,1,0:T(8,128)(2,1)}, bf16[4,4,80,768]{3,2,1,0:T(8,128)(2,1)}) custom-call(s32[2]{0:T(128)} %pad_add_fusion.refs_0_.where, bf16[1024,640]{1,0:T(8,128)(2,1)} %bitcast.34, bf16[1024,2048]{1,0:T(8,128)(2,1)} %get-tuple-element.89.hidden_in, bf16[1024,640]{1,0:T(8,128)(2,1)} %get-tuple-element.90.b_in, ...), custom_call_target="tpu_custom_call" | custom-call | flops 9900000256 | bytes 1 | tf_op jit(solution)/shard_map/column_grads/pallas_call | solution.py:799
  185.8 10.3 %weight_grad.1.refs_2_ = bf16[640,4096]{1,0:T(8,128)(2,1)} custom-call(bf16[1024,640]{1,0:T(8,128)(2,1)} %get-tuple-element.93.refs_0_, bf16[1024,4096]{1,0:T(8,128)(2,1)} %get-tuple-element.94.refs_1_, bf16[4,4,80,768]{3,2,1,0:T(8,128)(2,1)} %get-tuple-element.91.refs_2_.refs_0_), custom_call_target="tpu_custom_call" | custom-call | flops 11329999872 | bytes 1 | tf_op jit(solution)/shard_map/weight_grad/pallas_call | solution.py:749
  197.9 3.8 %collective-permute-done.17.refs_1_ = bf16[4,4,80,768]{3,2,1,0:T(8,128)(2,1)} collective-permute-done((bf16[4,4,80,768]{3,2,1,0:T(8,128)(2,1)S(1)}, bf16[4,4,80,768]{3,2,1,0:T(8,128)(2,1)}, u32[]{:S(2)}, u32[]{:S(2)}) %collective-permute-start.17) | collective-permute-done | bytes 1966112 | tf_op jit(solution)/shard_map/ppermute | solution.py:62
  208.8 8.8 %attend_back.2 = (bf16[1024,1024]{1,0:T(8,128)(2,1)}, f32[512,512]{1,0:T(8,128)}, bf16[512,512]{1,0:T(8,128)(2,1)}, bf16[512,512]{1,0:T(8,128)(2,1)}, bf16[512,512]{1,0:T(8,128)(2,1)}) custom-call(s32[2]{0:T(128)} %pad_add_fusion.refs_0_.where, s32[2,2]{1,0:T(2,128)} %bitcast.30, f32[2,4,512]{2,1,0:T(4,128)} %get-tuple-element.86.refs_2_, ...), custom_call_target="tpu_custom_call" | custom-call | flops 22000001024 | bytes 1 | tf_op jit(solution)/shard_map/attend_back/pallas_call | solution.py:636
  217.6 5.0 %collective-permute-start.22 = (bf16[512,512]{1,0:T(8,128)(2,1)}, bf16[512,512]{1,0:T(8,128)(2,1)S(1)}, u32[]{:S(2)}, u32[]{:S(2)}) collective-permute-start(bf16[512,512]{1,0:T(8,128)(2,1)} %get-tuple-element.110), channel_id=1, source_target_pairs={{0,8},{8,0},{16,24},{24,16},{1,9},{9,1},{17,25},{25,17},{2,10},{10... | collective-permute-start | bytes 1572872 | tf_op jit(solution)/shard_map/ppermute | solution.py:62
  222.6 7.9 %collective-permute-start.23 = (bf16[512,512]{1,0:T(8,128)(2,1)}, bf16[512,512]{1,0:T(8,128)(2,1)S(1)}, u32[]{:S(2)}, u32[]{:S(2)}) collective-permute-start(bf16[512,512]{1,0:T(8,128)(2,1)} %get-tuple-element.111), channel_id=1, source_target_pairs={{0,16},{8,24},{16,0},{24,8},{1,17},{9,25},{17,1},{25,9},{2,18},{10... | collective-permute-start | bytes 1572872 | tf_op jit(solution)/shard_map/ppermute | solution.py:62
  235.5 9.0 %attend_back.3 = (bf16[1024,1024]{1,0:T(8,128)(2,1)}, f32[512,512]{1,0:T(8,128)}, bf16[512,512]{1,0:T(8,128)(2,1)}, bf16[512,512]{1,0:T(8,128)(2,1)}, bf16[512,512]{1,0:T(8,128)(2,1)}) custom-call(s32[2]{0:T(128)} %pad_add_fusion.refs_0_.where, s32[2,2]{1,0:T(2,128)} %bitcast.31, ...), custom_call_target="tpu_custom_call", output_to_operand_aliasing={{0}: (12, {})} | custom-call | flops 22000001024 | bytes 1 | tf_op jit(solution)/shard_map/attend_back/pallas_call | solution.py:636
  244.5 4.9 %collective-permute-start.25 = (bf16[512,512]{1,0:T(8,128)(2,1)}, bf16[512,512]{1,0:T(8,128)(2,1)}, u32[]{:S(2)}, u32[]{:S(2)}) collective-permute-start(bf16[512,512]{1,0:T(8,128)(2,1)} %get-tuple-element.117), channel_id=1, source_target_pairs={{0,8},{8,0},{16,24},{24,16},{1,9},{9,1},{17,25},{25,17},{2,10},{10... | collective-permute-start | bytes 1572872 | tf_op jit(solution)/shard_map/ppermute | solution.py:62
  249.4 9.0 %collective-permute-start.26 = (bf16[512,512]{1,0:T(8,128)(2,1)}, bf16[512,512]{1,0:T(8,128)(2,1)}, u32[]{:S(2)}, u32[]{:S(2)}) collective-permute-start(bf16[512,512]{1,0:T(8,128)(2,1)} %get-tuple-element.118), channel_id=1, source_target_pairs={{0,16},{8,24},{16,0},{24,8},{1,17},{9,25},{17,1},{25,9},{2,18},{10... | collective-permute-start | bytes 1572872 | tf_op jit(solution)/shard_map/ppermute | solution.py:62
  260.1 12.4 %query_side.1 = (bf16[640,1792]{1,0:T(8,128)(2,1)}, f32[512,640]{1,0:T(8,128)}, bf16[512,512]{1,0:T(8,128)(2,1)}, f32[1024,640]{1,0:T(8,128)}, f32[1,640]{1,0:T(...) custom-call(bf16[1024,1024]{1,0:T(8,128)(2,1)} %get-tuple-element.103.refs_0_, ...), custom_call_target="tpu_custom_call" | custom-call | flops 999999995904 | bytes 20000000 | tf_op jit(solution)/shard_map/query_side/pallas_call | solution.py:901
  273.2 7.0 %collective-permute-done.26.refs_14_.refs_3_ = bf16[512,512]{1,0:T(8,128)(2,1)} collective-permute-done((bf16[512,512]{1,0:T(8,128)(2,1)}, bf16[512,512]{1,0:T(8,128)(2,1)}, u32[]{:S(2)}, u32[]{:S(2)}) %collective-permute-start.26) | collective-permute-done | bytes 524320 | tf_op jit(solution)/shard_map/ppermute | solution.py:62
  285.6 7.1 %pair_side.1 = (f32[1024,640]{1,0:T(8,128)}, bf16[4,80,640]{2,1,0:T(8,128)(2,1)}, bf16[80,640]{1,0:T(8,128)(2,1)}, bf16[80,640]{1,0:T(8,128)(2,1)}, bf16[80,640]{1,0:T(8,128)(2,1)}, /*index=5*/bf16[80,640]{1,0:T(8,128)(2,1)}) custom-call(s32[2]{0:T(128)} %pad_add_fusion.refs_0_.where, ...), custom_call_target="tpu_custom_call", output_to_operand_aliasing={{0}: (16, {})} | custom-call | flops 999999995904 | bytes 12000000 | tf_op jit(solution)/shard_map/pair_side/pallas_call | solution.py:970
  322.8 5.3 %collective-permute-done.38.refs_3_ = bf16[80,2432]{1,0:T(8,128)(2,1)S(1)} collective-permute-done((bf16[80,2432]{1,0:T(8,128)(2,1)}, bf16[80,2432]{1,0:T(8,128)(2,1)S(1)}, u32[]{:S(2)}, u32[]{:S(2)}) %collective-permute-start.38) | collective-permute-done | bytes 389152 | tf_op jit(solution)/shard_map/ppermute | solution.py:62
  328.1 7.2 %collective-permute-done.37.refs_2_ = bf16[80,2432]{1,0:T(8,128)(2,1)S(1)} collective-permute-done((bf16[80,2432]{1,0:T(8,128)(2,1)}, bf16[80,2432]{1,0:T(8,128)(2,1)S(1)}, u32[]{:S(2)}, u32[]{:S(2)}) %collective-permute-start.37) | collective-permute-done | bytes 389152 | tf_op jit(solution)/shard_map/ppermute | solution.py:62
  (179 shorter events, 83.3 us)
Async XLA Ops:
  7.2 129.4 %all-gather.2.cloned.1.call-start = ((), (), s32[]{:S(2)}) async-start(), calls=%async_computation.2 | async-start | bytes 9461760 | tf_op jit(solution)/shard_map/all_gather | solution.py:217
  25.5 234.6 %reduce-scatter.3.cloned.1.call-start = ((), (), s32[]{:S(2)}) async-start(), calls=%async_computation.3 | async-start | bytes 5898240 | tf_op jit(solution)/shard_map/reduce_scatter | solution.py:1230
  35.1 21.8 %collective-permute-start.10 = (bf16[80,1792]{1,0:T(8,128)(2,1)}, bf16[80,1792]{1,0:T(8,128)(2,1)S(1)}, u32[]{:S(2)}, u32[]{:S(2)}) collective-permute-start(bf16[80,1792]{1,0:T(8,128)(2,1)} %pack_query.1.refs_4_), channel_id=1, source_target_pairs={{0,4},{1,5},{2,6},{3,7},{4,0},{5,1},{6,2},{7,3},{8,12},{9,13},{10,... | collective-permute-start | bytes 860168 | tf_op jit(solution)/shard_map/ppermute | solution.py:62
  35.6 32.6 %collective-permute-start.16 = (bf16[1024,512]{1,0:T(8,128)(2,1)S(1)}, bf16[1024,512]{1,0:T(8,128)(2,1)S(1)}, u32[]{:S(2)}, u32[]{:S(2)}) collective-permute-start(bf16[1024,512]{1,0:T(8,128)(2,1)S(1)} %copy-done.2), channel_id=1, source_target_pairs={{0,24},{8,16},{16,8},{24,0},{1,25},{9,17},{17,9},{25,1},{2,26},{10... | collective-permute-start | bytes 3145736 | tf_op jit(solution)/shard_map/ppermute | solution.py:62
  38.0 50.9 %collective-permute-start.15 = (bf16[1024,512]{1,0:T(8,128)(2,1)S(1)}, bf16[1024,512]{1,0:T(8,128)(2,1)S(1)}, u32[]{:S(2)}, u32[]{:S(2)}) collective-permute-start(bf16[1024,512]{1,0:T(8,128)(2,1)S(1)} %copy-done.2), channel_id=1, source_target_pairs={{0,16},{8,24},{16,0},{24,8},{1,17},{9,25},{17,1},{25,9},{2,18},{10... | collective-permute-start | bytes 3145736 | tf_op jit(solution)/shard_map/ppermute | solution.py:62
  38.5 52.8 %collective-permute-start.14 = (bf16[1024,512]{1,0:T(8,128)(2,1)S(1)}, bf16[1024,512]{1,0:T(8,128)(2,1)S(1)}, u32[]{:S(2)}, u32[]{:S(2)}) collective-permute-start(bf16[1024,512]{1,0:T(8,128)(2,1)S(1)} %copy-done.2), channel_id=1, source_target_pairs={{0,8},{8,0},{16,24},{24,16},{1,9},{9,1},{17,25},{25,17},{2,10},{10... | collective-permute-start | bytes 3145736 | tf_op jit(solution)/shard_map/ppermute | solution.py:62
  39.0 18.8 %collective-permute-start.8 = (bf16[80,1792]{1,0:T(8,128)(2,1)}, bf16[80,1792]{1,0:T(8,128)(2,1)S(1)}, u32[]{:S(2)}, u32[]{:S(2)}) collective-permute-start(bf16[80,1792]{1,0:T(8,128)(2,1)} %pack_query.1.refs_4_), channel_id=1, source_target_pairs={{0,2},{1,3},{2,0},{3,1},{4,6},{5,7},{6,4},{7,5},{8,10},{9,11},{10,... | collective-permute-start | bytes 860168 | tf_op jit(solution)/shard_map/ppermute | solution.py:62
  196.1 116.4 %reduce-scatter.5.cloned.1.call-start = ((), (), s32[]{:S(2)}) async-start(), calls=%async_computation.4 | async-start | bytes 2580480 | tf_op jit(solution)/shard_map/reduce_scatter | solution.py:1250
  205.3 25.2 %collective-permute-start.18 = (bf16[4,80,768]{2,1,0:T(8,128)(2,1)}, bf16[4,80,768]{2,1,0:T(8,128)(2,1)S(1)}, u32[]{:S(2)}, u32[]{:S(2)}) collective-permute-start(bf16[4,80,768]{2,1,0:T(8,128)(2,1)} %get-tuple-element.96.refs_13_), channel_id=1, source_target_pairs={{0,8},{8,0},{16,24},{24,16},{1,9},{9,1},{17,25},{25,17},{2,10},{10... | collective-permute-start | bytes 1474568 | tf_op jit(solution)/shard_map/ppermute | solution.py:62
  206.7 23.8 %collective-permute-start.19 = (bf16[4,80,768]{2,1,0:T(8,128)(2,1)}, bf16[4,80,768]{2,1,0:T(8,128)(2,1)S(1)}, u32[]{:S(2)}, u32[]{:S(2)}) collective-permute-start(bf16[4,80,768]{2,1,0:T(8,128)(2,1)} %get-tuple-element.97.refs_14_), channel_id=1, source_target_pairs={{0,16},{8,24},{16,0},{24,8},{1,17},{9,25},{17,1},{25,9},{2,18},{10... | collective-permute-start | bytes 1474568 | tf_op jit(solution)/shard_map/ppermute | solution.py:62
  207.5 23.1 %collective-permute-start.20 = (bf16[4,80,768]{2,1,0:T(8,128)(2,1)}, bf16[4,80,768]{2,1,0:T(8,128)(2,1)S(1)}, u32[]{:S(2)}, u32[]{:S(2)}) collective-permute-start(bf16[4,80,768]{2,1,0:T(8,128)(2,1)} %get-tuple-element.98.refs_15_), channel_id=1, source_target_pairs={{0,24},{8,16},{16,8},{24,0},{1,25},{9,17},{17,9},{25,1},{2,26},{10... | collective-permute-start | bytes 1474568 | tf_op jit(solution)/shard_map/ppermute | solution.py:62
  217.6 31.9 %collective-permute-start.22 = (bf16[512,512]{1,0:T(8,128)(2,1)}, bf16[512,512]{1,0:T(8,128)(2,1)S(1)}, u32[]{:S(2)}, u32[]{:S(2)}) collective-permute-start(bf16[512,512]{1,0:T(8,128)(2,1)} %get-tuple-element.110), channel_id=1, source_target_pairs={{0,8},{8,0},{16,24},{24,16},{1,9},{9,1},{17,25},{25,17},{2,10},{10... | collective-permute-start | bytes 1572872 | tf_op jit(solution)/shard_map/ppermute | solution.py:62
  222.6 35.9 %collective-permute-start.23 = (bf16[512,512]{1,0:T(8,128)(2,1)}, bf16[512,512]{1,0:T(8,128)(2,1)S(1)}, u32[]{:S(2)}, u32[]{:S(2)}) collective-permute-start(bf16[512,512]{1,0:T(8,128)(2,1)} %get-tuple-element.111), channel_id=1, source_target_pairs={{0,16},{8,24},{16,0},{24,8},{1,17},{9,25},{17,1},{25,9},{2,18},{10... | collective-permute-start | bytes 1572872 | tf_op jit(solution)/shard_map/ppermute | solution.py:62
  230.5 28.0 %collective-permute-start.24 = (bf16[512,512]{1,0:T(8,128)(2,1)}, bf16[512,512]{1,0:T(8,128)(2,1)S(1)}, u32[]{:S(2)}, u32[]{:S(2)}) collective-permute-start(bf16[512,512]{1,0:T(8,128)(2,1)} %get-tuple-element.112), channel_id=1, source_target_pairs={{0,24},{8,16},{16,8},{24,0},{1,25},{9,17},{17,9},{25,1},{2,26},{10... | collective-permute-start | bytes 1572872 | tf_op jit(solution)/shard_map/ppermute | solution.py:62
  234.1 24.4 %collective-permute-start.21 = (bf16[2,80,768]{2,1,0:T(8,128)(2,1)}, bf16[2,80,768]{2,1,0:T(8,128)(2,1)S(1)}, u32[]{:S(2)}, u32[]{:S(2)}) collective-permute-start(bf16[2,80,768]{2,1,0:T(8,128)(2,1)} %get-tuple-element.109), channel_id=1, source_target_pairs={{0,2},{1,3},{2,0},{3,1},{4,6},{5,7},{6,4},{7,5},{8,10},{9,11},{10,... | collective-permute-start | bytes 737288 | tf_op jit(solution)/shard_map/ppermute | solution.py:62
  244.5 28.7 %collective-permute-start.25 = (bf16[512,512]{1,0:T(8,128)(2,1)}, bf16[512,512]{1,0:T(8,128)(2,1)}, u32[]{:S(2)}, u32[]{:S(2)}) collective-permute-start(bf16[512,512]{1,0:T(8,128)(2,1)} %get-tuple-element.117), channel_id=1, source_target_pairs={{0,8},{8,0},{16,24},{24,16},{1,9},{9,1},{17,25},{25,17},{2,10},{10... | collective-permute-start | bytes 1572872 | tf_op jit(solution)/shard_map/ppermute | solution.py:62
  249.4 30.7 %collective-permute-start.26 = (bf16[512,512]{1,0:T(8,128)(2,1)}, bf16[512,512]{1,0:T(8,128)(2,1)}, u32[]{:S(2)}, u32[]{:S(2)}) collective-permute-start(bf16[512,512]{1,0:T(8,128)(2,1)} %get-tuple-element.118), channel_id=1, source_target_pairs={{0,16},{8,24},{16,0},{24,8},{1,17},{9,25},{17,1},{25,9},{2,18},{10... | collective-permute-start | bytes 1572872 | tf_op jit(solution)/shard_map/ppermute | solution.py:62
  258.5 21.7 %collective-permute-start.27 = (bf16[512,512]{1,0:T(8,128)(2,1)}, bf16[512,512]{1,0:T(8,128)(2,1)}, u32[]{:S(2)}, u32[]{:S(2)}) collective-permute-start(bf16[512,512]{1,0:T(8,128)(2,1)} %get-tuple-element.119), channel_id=1, source_target_pairs={{0,24},{8,16},{16,8},{24,0},{1,25},{9,17},{17,9},{25,1},{2,26},{10... | collective-permute-start | bytes 1572872 | tf_op jit(solution)/shard_map/ppermute | solution.py:62
  272.6 20.3 %collective-permute-start.32 = (bf16[80,768]{1,0:T(8,128)(2,1)}, bf16[80,768]{1,0:T(8,128)(2,1)}, u32[]{:S(2)}, u32[]{:S(2)}) collective-permute-start(bf16[80,768]{1,0:T(8,128)(2,1)} %get-tuple-element.133), channel_id=1, source_target_pairs={{0,4},{1,5},{2,6},{3,7},{4,0},{5,1},{6,2},{7,3},{8,12},{9,13},{10,... | collective-permute-start | bytes 368648 | tf_op jit(solution)/shard_map/ppermute | solution.py:62
  301.4 16.5 %collective-permute-start.41 = (bf16[80,1792]{1,0:T(8,128)(2,1)S(1)}, bf16[80,1792]{1,0:T(8,128)(2,1)S(1)}, u32[]{:S(2)}, u32[]{:S(2)}) collective-permute-start(bf16[80,1792]{1,0:T(8,128)(2,1)S(1)} %copy-done.15), channel_id=1, source_target_pairs={{0,24},{8,16},{16,8},{24,0},{1,25},{9,17},{17,9},{25,1},{2,26},{10... | collective-permute-start | bytes 860168 | tf_op jit(solution)/shard_map/ppermute | solution.py:62
  302.9 15.6 %collective-permute-start.40 = (bf16[80,1792]{1,0:T(8,128)(2,1)S(1)}, bf16[80,1792]{1,0:T(8,128)(2,1)S(1)}, u32[]{:S(2)}, u32[]{:S(2)}) collective-permute-start(bf16[80,1792]{1,0:T(8,128)(2,1)S(1)} %copy-done.15), channel_id=1, source_target_pairs={{0,16},{8,24},{16,0},{24,8},{1,17},{9,25},{17,1},{25,9},{2,18},{10... | collective-permute-start | bytes 860168 | tf_op jit(solution)/shard_map/ppermute | solution.py:62
  315.1 13.1 %collective-permute-start.38 = (bf16[80,2432]{1,0:T(8,128)(2,1)}, bf16[80,2432]{1,0:T(8,128)(2,1)S(1)}, u32[]{:S(2)}, u32[]{:S(2)}) collective-permute-start(bf16[80,2432]{1,0:T(8,128)(2,1)} %join.1.refs_0_.refs_5_), channel_id=1, source_target_pairs={{0,24},{8,16},{16,8},{24,0},{1,25},{9,17},{17,9},{25,1},{2,26},{10... | collective-permute-start | bytes 1167368 | tf_op jit(solution)/shard_map/ppermute | solution.py:62
  317.3 18.0 %collective-permute-start.37 = (bf16[80,2432]{1,0:T(8,128)(2,1)}, bf16[80,2432]{1,0:T(8,128)(2,1)S(1)}, u32[]{:S(2)}, u32[]{:S(2)}) collective-permute-start(bf16[80,2432]{1,0:T(8,128)(2,1)} %join.1.refs_0_.refs_5_), channel_id=1, source_target_pairs={{0,16},{8,24},{16,0},{24,8},{1,17},{9,25},{17,1},{25,9},{2,18},{10... | collective-permute-start | bytes 1167368 | tf_op jit(solution)/shard_map/ppermute | solution.py:62
  317.9 17.5 %collective-permute-start.36 = (bf16[80,2432]{1,0:T(8,128)(2,1)}, bf16[80,2432]{1,0:T(8,128)(2,1)S(1)}, u32[]{:S(2)}, u32[]{:S(2)}) collective-permute-start(bf16[80,2432]{1,0:T(8,128)(2,1)} %join.1.refs_0_.refs_5_), channel_id=1, source_target_pairs={{0,8},{8,0},{16,24},{24,16},{1,9},{9,1},{17,25},{25,17},{2,10},{10... | collective-permute-start | bytes 1167368 | tf_op jit(solution)/shard_map/ppermute | solution.py:62
  (59 other events, 430.6 us)
Sparse Core Ops, SparseCore 0:
  25.6 110.8 all-gather.1
  196.2 63.8 reduce-scatter.2
  272.7 39.7 reduce-scatter.4
